TPU v7x, 128 devices: a whole 4x4x4 slice. The times are simulated.
128 devices in a mesh: grp: 4 (over z), sp: 32 (over y, x, core).
Axes of the slice: x: 4, y: 4, z: 4, core: 2. Of those that a mesh axis runs over, the one named last changes fastest.
Arguments:
- grad_out: bfloat16 [16384, 4096], P(('grp', 'sp')), may hold values from -3 to 3
- routes: int32 [16384, 8], P(('grp', 'sp')), may hold values from 0 to 63, as said below
- probs: bfloat16 [16384, 8], P(('grp', 'sp')), may hold values from 0.019897461 to 0.5
- hidden_act: bfloat16 [16384, 8, 768], P(('grp', 'sp')), may hold values from -1.5 to 1.5
- placement: int32 [4, 32], replicated, may hold values from 0 to 63, as said below
- down_weight: bfloat16 [64, 768, 4096], P('sp'), may hold values from -0.21875 to 0.21875
Outputs:
- grad_act: bfloat16 [16384, 8, 768], P(('grp', 'sp'))
- grad_prob: float32 [16384, 8], P(('grp', 'sp'))
- weight_grad: bfloat16 [4, 32, 768, 4096], P('grp', 'sp')
Inputs may be any that keep to these rules, and one draw needn't show every extreme that they name: `routes`: each row names 8 different experts; among the 128 rows of one device no expert is named by more than 17 rows, and some expert by exactly 17 in some device's rows. placement[g, s] is 2 s or 2 s + 1, and each of these two experts stands in at least one of the 4 entries of column s.
All inputs are finite; a program needn't handle non-finite values.
Results may differ from a plain program's by a relative error of at most 0.007.
Values may be sent and summed in bfloat16 or wider, within the bound.
No kernel may reach another device: no remote copies, remote signals or barrier semaphores. Data moves between devices by JAX's collectives and lax.ppermute only.
A program may use at most 192 MiB of HBM per device.

v0:
```python
import functools

import jax
import jax.numpy as jnp
from jax import lax
from jax.experimental import pallas as pl
from jax.experimental.pallas import tpu as pltpu
from jax.sharding import PartitionSpec as P

V = 256
MAIN = 32
TAIL = 8
SHIFT = 6
MASK = (1 << SHIFT) - 1
CHUNKS = (1, 3, 4, 4, 4)
BF16 = jnp.bfloat16
F32 = jnp.float32
VMEM = 48 * 1024 * 1024


def tie(first, second):
    return lax.optimization_barrier((first, second))


def dot(a, b, dims=((1,), (0,))):
    return lax.dot_general(a, b, (dims, ((), ())), preferred_element_type=F32)


def cost(flops, bytes_accessed):
    return pl.CostEstimate(flops=int(flops), bytes_accessed=int(bytes_accessed), transcendentals=0)


def params():
    return pltpu.CompilerParams(vmem_limit_bytes=VMEM)


def whole(shape):
    return pl.BlockSpec(shape, lambda *_: (0,) * len(shape))


def block_rows(n):
    return MAIN * n + TAIL


SEND_STEP = 8


def main_ids(first, rows):
    i = lax.broadcasted_iota(jnp.int32, (rows, 1), 0)
    return ((first + i // MAIN) << SHIFT) + i % MAIN


def tail_ids(first, part):
    i = lax.broadcasted_iota(jnp.int32, (SEND_STEP * TAIL, 1), 0)
    r = i % TAIL
    return jnp.where(r // 2 == part, ((first + i // TAIL) << SHIFT) + MAIN + r % 2, -1)


def hits(ids, codes):
    found = ids == codes[0:1, :]
    for k in range(1, codes.shape[0]):
        found = found | (ids == codes[k : k + 1, :])
    return jnp.where(found, 1.0, 0.0).astype(BF16)


def store_main(out_ref, part, values):
    out_ref[:, part * MAIN : (part + 1) * MAIN, :] = values.astype(BF16).reshape(SEND_STEP, MAIN, V)


def send_first_kernel(codes_ref, flat_ref, prob_ref, act_ref, grad_ref, out_ref):
    first = pl.program_id(0) * SEND_STEP
    codes, flat, prob = codes_ref[...], flat_ref[...], prob_ref[...]
    ids = main_ids(first, SEND_STEP * MAIN)
    pick = jnp.where(ids == flat, prob, 0.0).astype(BF16)
    act_parts = act_ref.shape[1] // V
    tail = jnp.zeros((SEND_STEP * TAIL, V), F32)
    for p in range(act_parts):
        act = act_ref[:, p * V : (p + 1) * V]
        store_main(out_ref, p, dot(pick, act))
        tail += dot(jnp.where(tail_ids(first, p) == flat, prob, 0.0).astype(BF16), act)
    grad = grad_ref[...]
    grads = hits(ids, codes)
    for p in range(grad.shape[1] // V):
        part = grad[:, p * V : (p + 1) * V]
        store_main(out_ref, act_parts + p, dot(grads, part))
        tail += dot(hits(tail_ids(first, act_parts + p), codes), part)
    out_ref[:, out_ref.shape[1] - TAIL :, :] = tail.astype(BF16).reshape(SEND_STEP, TAIL, V)


def send_kernel(chunks, codes_ref, grad_ref, *out_refs):
    first = pl.program_id(0) * SEND_STEP
    codes = codes_ref[...]
    grads = hits(main_ids(first, SEND_STEP * MAIN), codes)
    at = 0
    for n, out_ref in zip(chunks, out_refs):
        tail = jnp.zeros((SEND_STEP * TAIL, V), F32)
        for p in range(n):
            part = grad_ref[:, at : at + V]
            store_main(out_ref, p, dot(grads, part))
            tail += dot(hits(tail_ids(first, p), codes), part)
            at += V
        out_ref[:, MAIN * n :, :] = tail.astype(BF16).reshape(SEND_STEP, TAIL, V)


def send_first(codes, flat, prob, act, grad, columns, parts):
    routes, hidden = act.shape
    tok = grad.shape[0]
    rows = block_rows(hidden // V + parts)
    return pl.pallas_call(
        send_first_kernel,
        grid=(columns // SEND_STEP,),
        in_specs=[
            whole(codes.shape),
            whole(flat.shape),
            whole(prob.shape),
            whole(act.shape),
            pl.BlockSpec((tok, parts * V), lambda i: (0, 0)),
        ],
        out_specs=pl.BlockSpec((SEND_STEP, rows, V), lambda i: (i, 0, 0)),
        out_shape=jax.ShapeDtypeStruct((columns, rows, V), BF16),
        compiler_params=params(),
        cost_estimate=cost(2 * columns * MAIN * routes * hidden, 2 * columns * rows * V + 2 * routes * hidden),
        name="send_first",
    )(codes, flat, prob, act, grad)


def send_rest(codes, grad, columns, chunks):
    tok, width = grad.shape
    shapes = [(columns, block_rows(n), V) for n in chunks]
    return pl.pallas_call(
        functools.partial(send_kernel, chunks),
        grid=(columns // SEND_STEP,),
        in_specs=[whole(codes.shape), whole(grad.shape)],
        out_specs=[pl.BlockSpec((SEND_STEP, s[1], V), lambda i: (i, 0, 0)) for s in shapes],
        out_shape=[jax.ShapeDtypeStruct(s, BF16) for s in shapes],
        compiler_params=params(),
        cost_estimate=cost(2 * columns * MAIN * tok * width, 2 * columns * 34 * width + 2 * tok * width),
        name="send_rest",
    )(codes, grad)


def sorted_tail(got_ref):
    sources = got_ref.shape[0]
    tail = got_ref[:, got_ref.shape[1] - TAIL :, :].astype(F32).reshape(sources * TAIL, V).astype(BF16)
    size = sources * TAIL
    i = lax.broadcasted_iota(jnp.int32, (size, size), 0)
    j = lax.broadcasted_iota(jnp.int32, (size, size), 1)
    order = (i % sources == j // TAIL) & (i // sources == j % TAIL)
    return dot(jnp.where(order, 1.0, 0.0).astype(BF16), tail).astype(BF16)


def main_rows(got_ref, part, expert):
    half = MAIN // 2
    rows = got_ref[:, pl.ds(part * MAIN + expert * half, half), :]
    return rows.reshape(got_ref.shape[0] * half, V)


def tail_rows(tail, sources, part, expert):
    at = (2 * part + expert) * sources
    return tail[at : at + sources, :]


def weight_step(acts, rows, more, out_ref, expert):
    depth = rows.shape[0]
    total = dot(acts[:, :depth], rows) + dot(acts[:, depth:], more)
    quarters, _, size, _ = out_ref.shape
    for q in range(quarters):
        out_ref[q, expert] = total[q * size : (q + 1) * size].astype(BF16)


def weight_first_kernel(act_parts, got_ref, acts_ref, out_ref):
    sources = got_ref.shape[0]
    tail = sorted_tail(got_ref)
    for e in range(2):
        for p in range(act_parts):
            block = main_rows(got_ref, p, e)
            more = tail_rows(tail, sources, p, e)
            acts_ref[e, p * V : (p + 1) * V, : block.shape[0]] = block.astype(F32).T.astype(BF16)
            acts_ref[e, p * V : (p + 1) * V, block.shape[0] :] = more.astype(F32).T.astype(BF16)
        weight_step(
            acts_ref[e], main_rows(got_ref, act_parts, e), tail_rows(tail, sources, act_parts, e), out_ref, e
        )


def weight_kernel(parts, acts_ref, got_ref, out_ref, tail_ref):
    sources = got_ref.shape[0]
    part = pl.program_id(0)

    @pl.when(part == 0)
    def _():
        tail_ref[...] = sorted_tail(got_ref)

    for e in range(2):
        more = tail_ref[pl.ds(pl.multiple_of((2 * part + e) * sources, sources), sources), :]
        weight_step(acts_ref[e], main_rows(got_ref, part, e), more, out_ref, e)


def weight_first(got, hidden, groups):
    sources = got.shape[0]
    depth = sources * (MAIN // 2 + 1)
    return pl.pallas_call(
        functools.partial(weight_first_kernel, hidden // V),
        grid=(1,),
        in_specs=[whole(got.shape)],
        out_specs=[whole((2, hidden, depth)), whole((groups, 2, hidden // groups, V))],
        out_shape=[
            jax.ShapeDtypeStruct((2, hidden, depth), BF16),
            jax.ShapeDtypeStruct((groups, 2, hidden // groups, V), BF16),
        ],
        compiler_params=params(),
        cost_estimate=cost(4 * depth * hidden * V, 2 * (got.size + 4 * depth * hidden)),
        name="weight_first",
    )(got)


def weight_rest(acts, got, parts, groups):
    hidden, depth = acts.shape[1:]
    return pl.pallas_call(
        functools.partial(weight_kernel, parts),
        grid=(parts,),
        in_specs=[whole(acts.shape), whole(got.shape)],
        out_specs=pl.BlockSpec((groups, 2, hidden // groups, V), lambda p: (0, 0, 0, p)),
        out_shape=jax.ShapeDtypeStruct((groups, 2, hidden // groups, parts * V), BF16),
        scratch_shapes=[pltpu.VMEM((got.shape[0] * TAIL, V), BF16)],
        compiler_params=params(),
        cost_estimate=cost(4 * depth * hidden * V * parts, 2 * (got.size + acts.size + 2 * hidden * V * parts)),
        name="weight_rest",
    )(acts, got)


def project_kernel(skip, parts, chained, final, *refs):
    refs = list(refs)
    got_ref, weight_ref = refs[:2]
    refs = refs[2:]
    if chained:
        main_in, tail_in = refs[:2]
        refs = refs[2:]
    if final:
        out_ref, main_acc, tail_acc, tail_ref = refs
    else:
        main_acc, tail_acc, tail_ref = refs
    sources = got_ref.shape[0]
    half = MAIN // 2
    part = pl.program_id(0)

    @pl.when(part == 0)
    def _():
        tail_ref[...] = sorted_tail(got_ref)
        if chained:
            main_acc[...] = main_in[...]
            tail_acc[...] = tail_in[...]
        else:
            main_acc[...] = jnp.zeros_like(main_acc)
            tail_acc[...] = jnp.zeros_like(tail_acc)

    for e in range(2):
        weight = weight_ref[e]
        rows = main_rows(got_ref, part + skip, e)
        main_acc[e] += dot(rows, weight, ((1,), (1,)))
        more = tail_ref[pl.ds(pl.multiple_of((2 * (part + skip) + e) * sources, sources), sources), :]
        tail_acc[e] += dot(more, weight, ((1,), (1,)))

    if final:

        @pl.when(part == parts - 1)
        def _():
            hidden = weight_ref.shape[1]
            n = hidden // V
            size = sources * TAIL
            i = lax.broadcasted_iota(jnp.int32, (size, sources), 0)
            j = lax.broadcasted_iota(jnp.int32, (size, sources), 1)
            tail = jnp.zeros((size, V), F32)
            for e in range(2):
                for p in range(n):
                    block = main_acc[e, :, p * V : (p + 1) * V].astype(BF16)
                    at = p * MAIN + e * half
                    out_ref[:, at : at + half, :] = block.reshape(sources, half, V)
                    order = (i // TAIL == j) & (i % TAIL == 2 * p + e)
                    more = tail_acc[e, :, p * V : (p + 1) * V].astype(BF16)
                    tail += dot(jnp.where(order, 1.0, 0.0).astype(BF16), more)
            out_ref[:, n * MAIN :, :] = tail.reshape(sources, TAIL, V).astype(BF16)


def project(got, weight, at, skip, parts, state, final):
    sources = got.shape[0]
    hidden = weight.shape[1]
    half = MAIN // 2
    main_shape, tail_shape = (2, sources * half, hidden), (2, sources, hidden)
    in_specs = [whole(got.shape), pl.BlockSpec((2, hidden, V), lambda p: (0, 0, at + p))]
    args = [got, weight]
    if state is not None:
        in_specs += [whole(main_shape), whole(tail_shape)]
        args += list(state)
    scratch = [pltpu.VMEM((sources * TAIL, V), BF16)]
    if final:
        shape = (sources, block_rows(hidden // V), V)
        out_specs, out_shape = whole(shape), jax.ShapeDtypeStruct(shape, BF16)
        scratch = [pltpu.VMEM(main_shape, F32), pltpu.VMEM(tail_shape, F32)] + scratch
    else:
        out_specs = [whole(main_shape), whole(tail_shape)]
        out_shape = [jax.ShapeDtypeStruct(main_shape, F32), jax.ShapeDtypeStruct(tail_shape, F32)]
    return pl.pallas_call(
        functools.partial(project_kernel, skip, parts, state is not None, final),
        grid=(parts,),
        in_specs=in_specs,
        out_specs=out_specs,
        out_shape=out_shape,
        scratch_shapes=scratch,
        compiler_params=params(),
        cost_estimate=cost(4 * sources * 17 * hidden * V * parts, 2 * got.size + 4 * hidden * V * parts + 16 * sources * 17 * hidden),
        name="project",
    )(*args)


FINISH_STEP = 256


def finish_kernel(code_ref, prob_ref, act_ref, back_ref, grad_act_ref, grad_prob_ref):
    code = code_ref[...]
    column, row = code >> SHIFT, code & MASK
    sources = back_ref.shape[0]
    hidden = act_ref.shape[1]
    n = hidden // V
    steps = code.shape[0]
    main_id = jnp.where(row < MAIN, column * MAIN + row, -1)
    lanes = lax.broadcasted_iota(jnp.int32, (steps, sources * MAIN), 1)
    pick = jnp.where(lanes == main_id, 1.0, 0.0).astype(BF16)
    tail = back_ref[:, n * MAIN :, :].astype(F32).reshape(sources * TAIL, V).astype(BF16)
    lanes = lax.broadcasted_iota(jnp.int32, (steps, sources * TAIL), 1)
    prob = prob_ref[...]
    total = jnp.zeros((steps, 1), F32)
    for p in range(n):
        main = back_ref[:, p * MAIN : (p + 1) * MAIN, :].reshape(sources * MAIN, V)
        tail_id = jnp.where(row >= MAIN, column * TAIL + 2 * p + (row - MAIN), -1)
        proj = dot(pick, main) + dot(jnp.where(lanes == tail_id, 1.0, 0.0).astype(BF16), tail)
        act = act_ref[:, p * V : (p + 1) * V].astype(F32)
        total += jnp.sum(act * proj, axis=1, keepdims=True)
        grad_act_ref[:, p * V : (p + 1) * V] = (prob * proj).astype(BF16)
    grad_prob_ref[...] = total


def finish(code, prob, act, back):
    routes, hidden = act.shape
    one = pl.BlockSpec((FINISH_STEP, 1), lambda i: (i, 0))
    rows = pl.BlockSpec((FINISH_STEP, hidden), lambda i: (i, 0))
    return pl.pallas_call(
        finish_kernel,
        grid=(routes // FINISH_STEP,),
        in_specs=[one, one, rows, whole(back.shape)],
        out_specs=[rows, one],
        out_shape=[jax.ShapeDtypeStruct((routes, hidden), BF16), jax.ShapeDtypeStruct((routes, 1), F32)],
        compiler_params=params(),
        cost_estimate=cost(2 * routes * routes * hidden, 2 * (back.size + 2 * routes * hidden)),
        name="finish",
    )(code, prob, act, back)


def route_codes(routes, columns):
    tok, top = routes.shape
    experts = 2 * columns
    base = MAIN // 2
    hit = routes[:, :, None] == jnp.arange(experts)[None, None, :]
    member = jnp.any(hit, axis=1).astype(BF16)
    lower = (jnp.arange(tok)[:, None] > jnp.arange(tok)[None, :]).astype(BF16)
    rank = dot(lower, member)
    rank = jnp.sum(jnp.where(hit, rank[:, None, :], 0.0), axis=2).astype(jnp.int32)
    low = routes % 2
    row = jnp.where(rank < base, low * base + rank, MAIN + low)
    return ((routes // 2) << SHIFT) + row


def shards(grad_out, routes, probs, hidden_act, placement, down_weight):
    groups = lax.axis_size("grp")
    columns = lax.axis_size("sp")
    my_group = lax.axis_index("grp")
    my_column = lax.axis_index("sp")
    tok, width = grad_out.shape
    top = routes.shape[1]
    hidden = hidden_act.shape[2]
    quarter = hidden // groups
    act_parts = hidden // V
    last = len(CHUNKS) - 1

    codes = route_codes(routes, columns)
    flat = codes.reshape(1, tok * top)
    prob = probs.astype(F32)
    act = hidden_act.reshape(tok * top, hidden)

    def exchange(v):
        return lax.all_to_all(v, "sp", 0, 0, tiled=True)

    held = lax.dynamic_index_in_dim(placement, my_column, 1, keepdims=False) - 2 * my_column
    hops = [[(i, (i + d) % groups) for i in range(groups)] for d in range(groups)]

    def reduced(part):
        size = part.shape[-1]
        flat_part = part.reshape(groups * 2 * quarter, size)
        return lax.psum_scatter(flat_part, "grp", scatter_dimension=0, tiled=True).reshape(2, quarter, size)

    def wanted(mine):
        out = []
        for d in range(groups):
            which = lax.dynamic_index_in_dim(held, (my_group + d) % groups, 0, keepdims=False)
            out.append(jnp.where(which == 0, mine[0], mine[1]))
        return out

    own = jnp.zeros((hidden, width), BF16)

    def moved(sends):
        return [lax.ppermute(sends[d], "grp", hops[d]) if d else sends[d] for d in range(groups)]

    def place(own, blocks, at):
        for d in range(groups):
            source = (my_group + groups - d) % groups
            own = lax.dynamic_update_slice(own, blocks[d], (source * quarter, at))
        return own

    codes_t = codes.T
    first = send_first(codes_t, flat, prob.reshape(1, tok * top), act, grad_out, columns, CHUNKS[0])
    got = {0: exchange(first)}
    outs = send_rest(codes_t, grad_out[:, CHUNKS[0] * V :], columns, CHUNKS[1:])
    outs = dict(enumerate(outs, 1))

    starts = [sum(CHUNKS[:c]) for c in range(last + 1)]
    mine, sends, blocks = {}, {}, {}
    state = None
    acts, part = weight_first(got[0], hidden, groups)
    for c in range(last + 1):
        if c:
            if c == last:
                got[c], state = tie(got[c], state)
            if c >= 2:
                got[c], blocks[c - 2] = tie(got[c], moved(sends[c - 2]))
            part = weight_rest(acts, got[c], CHUNKS[c], groups)
        mine[c] = reduced(part)
        if c < last:
            if c >= 1:
                outs[c + 1], sends[c - 1] = tie(outs[c + 1], wanted(mine[c - 1]))
            got[c + 1] = exchange(outs[c + 1])
            skip = act_parts if c == 0 else 0
            state = project(got[c], down_weight, starts[c], skip, CHUNKS[c], state, False)
    proj = project(got[last], down_weight, starts[last], 0, CHUNKS[last], state, True)
    proj, sends[last - 1] = tie(proj, wanted(mine[last - 1]))
    back = exchange(proj)
    sends[last] = wanted(mine[last])
    for c in range(last + 1):
        own = place(own, blocks[c] if c in blocks else moved(sends[c]), starts[c] * V)

    grad_act, grad_prob = finish(codes.reshape(tok * top, 1), prob.reshape(tok * top, 1), act, back)
    return (
        grad_act.reshape(tok, top, hidden),
        grad_prob.reshape(tok, top),
        own.reshape(1, 1, hidden, width),
    )


def solution(mesh):
    placed = (
        P(("grp", "sp"), None),
        P(("grp", "sp"), None),
        P(("grp", "sp"), None),
        P(("grp", "sp"), None, None),
        P(),
        P("sp", None, None),
    )
    return jax.shard_map(
        shards,
        mesh=mesh,
        in_specs=placed,
        out_specs=(
            P(("grp", "sp"), None, None),
            P(("grp", "sp"), None),
            P("grp", "sp", None, None),
        ),
        check_vma=False,
    )
```

profile of v0, /device:TPU:0, one launch (start us, length us, event | category | flops | bytes accessed | tf_op | source)
XLA Modules:
  0.0 342.9 jit_solution(13629643033022439720)
XLA Ops:
  10.6 1.2 copy-done.11
  11.8 1.4 copy-done.13
  13.2 3.8 %send_first.1 = bf16[32,136,256]{2,1,0:T(8,128)(2,1)S(1)} custom-call(s32[8,128]{1,0:T(8,128)S(1)} %bitcast.54, s32[1,1024]{1,0:T(1,128)S(1)} %reshape.181.flat_ref, f32[1,1024]{1,0:T(1,128)S(1)} %reshape.182.prob_ref, bf16[1024,768]{1,0:T(8,128)(2,1)S(1)} %bitcast.56, bf16[128,4096]{1,0:T(8,128)(2,1)S(1)} %copy-done.11), custom_call_target="tpu_custom_call" | custom-call | flops 1610612736 | bytes 3801088 | tf_op jit(solution)/shard_map/send_first/pallas_call | solution.py:109
  17.0 1.4 copy-done.9
  18.4 7.4 %all-to-all-start = ((bf16[32,136,256]{2,1,0:T(8,128)(2,1)}), bf16[32,136,256]{2,1,0:T(8,128)(2,1)S(1)}, u32[]{:S(2)}, u32[]{:S(2)}) async-start(bf16[32,136,256]{2,1,0:T(8,128)(2,1)} %copy-done.9), calls=%async_computation | async-start | bytes 4456448 | tf_op jit(solution)/shard_map/all_to_all | solution.py:390
  25.9 4.4 %send_rest.1 = (bf16[32,104,256]{2,1,0:T(8,128)(2,1)S(1)}, bf16[32,136,256]{2,1,0:T(8,128)(2,1)S(1)}, bf16[32,136,256]{2,1,0:T(8,128)(2,1)}, bf16[32,136,256]{2,1,0:T(8,128)(2,1)}) custom-call(s32[8,128]{1,0:T(8,128)S(1)} %bitcast.55, bf16[128,3840]{1,0:T(8,128)(2,1)S(1)} %slice.32.grad_ref), custom_call_target="tpu_custom_call" | custom-call | flops 1006632960 | bytes 9338880 | tf_op jit(solution)/shard_map/send_rest/pallas_call | solution.py:130
  30.3 1.4 copy-done.8
  32.9 24.5 %all-to-all-done.got_ref.refs_0_ = bf16[32,136,256]{2,1,0:T(8,128)(2,1)S(1)} async-done(((bf16[32,136,256]{2,1,0:T(8,128)(2,1)}), bf16[32,136,256]{2,1,0:T(8,128)(2,1)S(1)}, u32[]{:S(2)}, u32[]{:S(2)}) %all-to-all-start) | async-done | bytes 2228256 | tf_op jit(solution)/shard_map/all_to_all | solution.py:390
  57.4 4.7 %all-to-all-start.3 = ((bf16[32,104,256]{2,1,0:T(8,128)(2,1)}), bf16[32,104,256]{2,1,0:T(8,128)(2,1)}, u32[]{:S(2)}, u32[]{:S(2)}) async-start(bf16[32,104,256]{2,1,0:T(8,128)(2,1)} %copy-done.10), calls=%async_computation.5 | async-start | bytes 3407872 | tf_op jit(solution)/shard_map/all_to_all | solution.py:390
  62.2 1.6 copy-done.1
  63.8 1.9 weight_first.1
  65.8 21.7 %all-to-all-done.3.got_ref.refs_0_ = bf16[32,104,256]{2,1,0:T(8,128)(2,1)} async-done(((bf16[32,104,256]{2,1,0:T(8,128)(2,1)}), bf16[32,104,256]{2,1,0:T(8,128)(2,1)}, u32[]{:S(2)}, u32[]{:S(2)}) %all-to-all-start.3) | async-done | bytes 1703968 | tf_op jit(solution)/shard_map/all_to_all | solution.py:390
  87.5 4.0 %weight_rest.5 = bf16[4,2,192,768]{3,2,1,0:T(8,128)(2,1)S(1)} custom-call(bf16[2,768,544]{2,1,0:T(8,128)(2,1)S(1)} %get-tuple-element.58.acts_ref, bf16[32,104,256]{2,1,0:T(8,128)(2,1)} %all-to-all-done.3.got_ref.refs_0_), custom_call_target="tpu_custom_call" | custom-call | flops 1283457024 | bytes 5734400 | tf_op jit(solution)/shard_map/weight_rest/pallas_call | solution.py:218
  91.5 1.4 copy-done.3
  96.4 1.6 broadcast_select_fusion.15
  98.0 4.8 %all-to-all-start.1 = ((bf16[32,136,256]{2,1,0:T(8,128)(2,1)}), bf16[32,136,256]{2,1,0:T(8,128)(2,1)}, u32[]{:S(2)}, u32[]{:S(2)}) async-start(bf16[32,136,256]{2,1,0:T(8,128)(2,1)} %copy-done.8), calls=%async_computation.2 | async-start | bytes 4456448 | tf_op jit(solution)/shard_map/all_to_all | solution.py:390
  102.9 2.0 collective-permute-start
  104.9 3.6 %collective-permute-start.1 = (bf16[192,256]{1,0:T(8,128)(2,1)S(1)}, bf16[192,256]{1,0:T(8,128)(2,1)S(1)}, u32[]{:S(2)}, u32[]{:S(2)}) collective-permute-start(bf16[192,256]{1,0:T(8,128)(2,1)S(1)} %get-tuple-element.64), channel_id=1, source_target_pairs={{0,64},{32,96},{64,0},{96,32},{1,65},{33,97},{65,1},{97,33},{2,66}... | collective-permute-start | bytes 294920 | tf_op jit(solution)/shard_map/ppermute | solution.py:410
  109.4 3.1 collective-permute-done
  112.5 5.6 %collective-permute-done.1 = bf16[192,256]{1,0:T(8,128)(2,1)S(1)} collective-permute-done((bf16[192,256]{1,0:T(8,128)(2,1)S(1)}, bf16[192,256]{1,0:T(8,128)(2,1)S(1)}, u32[]{:S(2)}, u32[]{:S(2)}) %collective-permute-start.1) | collective-permute-done | bytes 98336 | tf_op jit(solution)/shard_map/ppermute | solution.py:410
  118.1 16.3 %all-to-all-done.1.got_ref.refs_0_ = bf16[32,136,256]{2,1,0:T(8,128)(2,1)} async-done(((bf16[32,136,256]{2,1,0:T(8,128)(2,1)}), bf16[32,136,256]{2,1,0:T(8,128)(2,1)}, u32[]{:S(2)}, u32[]{:S(2)}) %all-to-all-start.1) | async-done | bytes 2228256 | tf_op jit(solution)/shard_map/all_to_all | solution.py:390
  134.4 5.8 %weight_rest.4 = bf16[4,2,192,1024]{3,2,1,0:T(8,128)(2,1)} custom-call(bf16[2,768,544]{2,1,0:T(8,128)(2,1)S(1)} %get-tuple-element.58.acts_ref, bf16[32,136,256]{2,1,0:T(8,128)(2,1)} %all-to-all-done.1.got_ref.refs_0_), custom_call_target="tpu_custom_call" | custom-call | flops 1711276032 | bytes 7045120 | tf_op jit(solution)/shard_map/weight_rest/pallas_call | solution.py:218
  140.3 2.0 broadcast_select_fusion.11
  142.3 4.8 %all-to-all-start.4 = ((bf16[32,136,256]{2,1,0:T(8,128)(2,1)}), bf16[32,136,256]{2,1,0:T(8,128)(2,1)}, u32[]{:S(2)}, u32[]{:S(2)}) async-start(bf16[32,136,256]{2,1,0:T(8,128)(2,1)} %get-tuple-element.70), calls=%async_computation.7 | async-start | bytes 4456448 | tf_op jit(solution)/shard_map/all_to_all | solution.py:390
  147.2 2.0 collective-permute-start.3
  149.2 3.6 %collective-permute-start.4 = (bf16[192,768]{1,0:T(8,128)(2,1)}, bf16[192,768]{1,0:T(8,128)(2,1)S(1)}, u32[]{:S(2)}, u32[]{:S(2)}) collective-permute-start(bf16[192,768]{1,0:T(8,128)(2,1)} %get-tuple-element.73), channel_id=1, source_target_pairs={{0,64},{32,96},{64,0},{96,32},{1,65},{33,97},{65,1},{97,33},{2,66}... | collective-permute-start | bytes 884744 | tf_op jit(solution)/shard_map/ppermute | solution.py:410
  153.8 11.7 %collective-permute-done.3 = bf16[192,768]{1,0:T(8,128)(2,1)S(1)} collective-permute-done((bf16[192,768]{1,0:T(8,128)(2,1)}, bf16[192,768]{1,0:T(8,128)(2,1)S(1)}, u32[]{:S(2)}, u32[]{:S(2)}) %collective-permute-start.3) | collective-permute-done | bytes 294944 | tf_op jit(solution)/shard_map/ppermute | solution.py:410
  165.5 14.0 %collective-permute-done.4 = bf16[192,768]{1,0:T(8,128)(2,1)S(1)} collective-permute-done((bf16[192,768]{1,0:T(8,128)(2,1)}, bf16[192,768]{1,0:T(8,128)(2,1)S(1)}, u32[]{:S(2)}, u32[]{:S(2)}) %collective-permute-start.4) | collective-permute-done | bytes 294944 | tf_op jit(solution)/shard_map/ppermute | solution.py:410
  179.5 6.2 %weight_rest.6 = bf16[4,2,192,1024]{3,2,1,0:T(8,128)(2,1)} custom-call(bf16[2,768,544]{2,1,0:T(8,128)(2,1)S(1)} %get-tuple-element.58.acts_ref, bf16[32,136,256]{2,1,0:T(8,128)(2,1)} %all-to-all-done.4.refs_0_.got_ref), custom_call_target="tpu_custom_call" | custom-call | flops 1711276032 | bytes 7045120 | tf_op jit(solution)/shard_map/weight_rest/pallas_call | solution.py:218
  185.7 3.7 %reduce-scatter.8.cloned.1.call-done = bf16[384,1024]{1,0:T(8,128)(2,1)} async-done(((bf16[1536,1024]{1,0:T(8,128)(2,1)}), bf16[384,1024]{1,0:T(8,128)(2,1)}) %reduce-scatter.8.cloned.1.call-update) | async-done | bytes 786448 | tf_op jit(solution)/shard_map/reduce_scatter | solution.py:398
  189.4 2.3 broadcast_select_fusion.2
  191.7 7.2 %all-to-all-start.2 = ((bf16[32,136,256]{2,1,0:T(8,128)(2,1)}), bf16[32,136,256]{2,1,0:T(8,128)(2,1)}, u32[]{:S(2)}, u32[]{:S(2)}) async-start(bf16[32,136,256]{2,1,0:T(8,128)(2,1)} %get-tuple-element.67), calls=%async_computation.4 | async-start | bytes 4456448 | tf_op jit(solution)/shard_map/all_to_all | solution.py:390
  199.0 2.1 copy-done.2
  201.1 1.9 project.5
  203.1 1.7 copy-done.5
  204.7 1.7 collective-permute-start.7
  206.4 1.9 collective-permute-start.8
  208.4 5.7 %project.6 = (f32[2,512,768]{2,1,0:T(8,128)S(1)}, f32[2,32,768]{2,1,0:T(8,128)S(1)}) custom-call(bf16[32,104,256]{2,1,0:T(8,128)(2,1)} %all-to-all-done.3.got_ref.refs_0_, bf16[2,768,4096]{2,1,0:T(8,128)(2,1)} %refs_1_.9, f32[2,512,768]{2,1,0:T(8,128)} %copy-done.5, f32[2,32,768]{2,1,0:T(8,128)S(1)} %get-tuple-element.77.refs_3_), custom_call_target="tpu_custom_call" | custom-call | flops 1283457024 | bytes 10747904 | tf_op jit(solution)/shard_map/project/pallas_call | solution.py:302
  214.1 1.7 copy-done.6
  215.8 6.7 %project.7 = (f32[2,512,768]{2,1,0:T(8,128)S(1)}, f32[2,32,768]{2,1,0:T(8,128)S(1)}) custom-call(bf16[32,136,256]{2,1,0:T(8,128)(2,1)} %all-to-all-done.1.got_ref.refs_0_, bf16[2,768,4096]{2,1,0:T(8,128)(2,1)} %refs_1_.9, f32[2,512,768]{2,1,0:T(8,128)} %copy-done.6, f32[2,32,768]{2,1,0:T(8,128)S(1)} %get-tuple-element.79.refs_3_), custom_call_target="tpu_custom_call" | custom-call | flops 1711276032 | bytes 12058624 | tf_op jit(solution)/shard_map/project/pallas_call | solution.py:302
  222.5 1.7 copy-done.7
  224.2 6.7 %project.8 = (f32[2,512,768]{2,1,0:T(8,128)S(1)}, f32[2,32,768]{2,1,0:T(8,128)S(1)}) custom-call(bf16[32,136,256]{2,1,0:T(8,128)(2,1)} %all-to-all-done.4.refs_0_.got_ref, bf16[2,768,4096]{2,1,0:T(8,128)(2,1)} %refs_1_.9, f32[2,512,768]{2,1,0:T(8,128)} %copy-done.7, f32[2,32,768]{2,1,0:T(8,128)S(1)} %get-tuple-element.81.refs_3_), custom_call_target="tpu_custom_call" | custom-call | flops 1711276032 | bytes 12058624 | tf_op jit(solution)/shard_map/project/pallas_call | solution.py:302
  230.9 1.6 copy-done.4
  232.5 9.2 %collective-permute-done.7 = bf16[192,1024]{1,0:T(8,128)(2,1)} collective-permute-done((bf16[192,1024]{1,0:T(8,128)(2,1)}, bf16[192,1024]{1,0:T(8,128)(2,1)}, u32[]{:S(2)}, u32[]{:S(2)}) %collective-permute-start.7) | collective-permute-done | bytes 393248 | tf_op jit(solution)/shard_map/ppermute | solution.py:410
  241.7 2.1 collective-permute-done.8
  243.8 6.2 %weight_rest.7 = bf16[4,2,192,1024]{3,2,1,0:T(8,128)(2,1)} custom-call(bf16[2,768,544]{2,1,0:T(8,128)(2,1)S(1)} %get-tuple-element.58.acts_ref, bf16[32,136,256]{2,1,0:T(8,128)(2,1)} %all-to-all-done.2.refs_0_.got_ref), custom_call_target="tpu_custom_call" | custom-call | flops 1711276032 | bytes 7045120 | tf_op jit(solution)/shard_map/weight_rest/pallas_call | solution.py:218
  250.5 3.5 %reshape.189 = bf16[1,1,768,4096]{3,2,1,0:T(8,128)(2,1)} broadcast(bf16[]{:T(256)} %constant.244.clone.1), dimensions={} | broadcast | bytes 6291458 | tf_op jit(solution)/shard_map/reshape | solution.py:453
  259.5 8.3 %project.9 = bf16[32,104,256]{2,1,0:T(8,128)(2,1)} custom-call(bf16[32,136,256]{2,1,0:T(8,128)(2,1)} %all-to-all-done.2.refs_0_.got_ref, bf16[2,768,4096]{2,1,0:T(8,128)(2,1)} %refs_1_.9, f32[2,512,768]{2,1,0:T(8,128)} %copy-done.4, f32[2,32,768]{2,1,0:T(8,128)S(1)} %get-tuple-element.91.refs_3_), custom_call_target="tpu_custom_call" | custom-call | flops 1711276032 | bytes 12058624 | tf_op jit(solution)/shard_map/project/pallas_call | solution.py:302
  268.6 1.8 bitcast_dynamic-update-slice_fusion.10
  270.5 2.2 broadcast_select_fusion.1
  272.7 7.2 %all-to-all-start.5 = ((bf16[32,104,256]{2,1,0:T(8,128)(2,1)}), bf16[32,104,256]{2,1,0:T(8,128)(2,1)S(1)}, u32[]{:S(2)}, u32[]{:S(2)}) async-start(bf16[32,104,256]{2,1,0:T(8,128)(2,1)} %project.9), calls=%async_computation.9 | async-start | bytes 3407872 | tf_op jit(solution)/shard_map/all_to_all | solution.py:390
  279.9 1.8 bitcast_dynamic-update-slice_fusion.9
  282.6 1.6 collective-permute-start.10
  284.3 2.6 collective-permute-start.11
  287.7 7.7 %collective-permute-done.9 = bf16[192,1024]{1,0:T(8,128)(2,1)S(1)} collective-permute-done((bf16[192,1024]{1,0:T(8,128)(2,1)}, bf16[192,1024]{1,0:T(8,128)(2,1)S(1)}, u32[]{:S(2)}, u32[]{:S(2)}) %collective-permute-start.9) | collective-permute-done | bytes 393248 | tf_op jit(solution)/shard_map/ppermute | solution.py:410
  296.1 7.9 %collective-permute-done.10 = bf16[192,1024]{1,0:T(8,128)(2,1)S(1)} collective-permute-done((bf16[192,1024]{1,0:T(8,128)(2,1)}, bf16[192,1024]{1,0:T(8,128)(2,1)S(1)}, u32[]{:S(2)}, u32[]{:S(2)}) %collective-permute-start.10) | collective-permute-done | bytes 393248 | tf_op jit(solution)/shard_map/ppermute | solution.py:410
  305.5 2.3 broadcast_select_fusion
  308.4 1.4 copy-done.14
  309.8 4.0 %finish.1 = (bf16[1024,768]{1,0:T(8,128)(2,1)}, f32[1024,1]{1,0:T(8,128)S(1)}) custom-call(s32[1024,1]{1,0:T(8,128)S(1)} %reshape.211.code_ref, f32[1024,1]{1,0:T(8,128)S(1)} %reshape.212.prob_ref, bf16[1024,768]{1,0:T(8,128)(2,1)S(1)} %bitcast.57, bf16[32,104,256]{2,1,0:T(8,128)(2,1)S(1)} %all-to-all-done.5.back_ref), custom_call_target="tpu_custom_call" | custom-call | flops 1610612736 | bytes 4849664 | tf_op jit(solution)/shard_map/finish/pallas_call | solution.py:346
  314.7 2.9 collective-permute-start.13
  318.0 2.0 bitcast_dynamic-update-slice_fusion.3
  321.0 1.8 bitcast_dynamic-update-slice_fusion.2
  322.8 6.2 %collective-permute-done.13 = bf16[192,1024]{1,0:T(8,128)(2,1)S(1)} collective-permute-done((bf16[192,1024]{1,0:T(8,128)(2,1)}, bf16[192,1024]{1,0:T(8,128)(2,1)S(1)}, u32[]{:S(2)}, u32[]{:S(2)}) %collective-permute-start.13) | collective-permute-done | bytes 393248 | tf_op jit(solution)/shard_map/ppermute | solution.py:410
  329.8 5.9 %collective-permute-done.14 = bf16[192,1024]{1,0:T(8,128)(2,1)S(1)} collective-permute-done((bf16[192,1024]{1,0:T(8,128)(2,1)}, bf16[192,1024]{1,0:T(8,128)(2,1)S(1)}, u32[]{:S(2)}, u32[]{:S(2)}) %collective-permute-start.14) | collective-permute-done | bytes 393248 | tf_op jit(solution)/shard_map/ppermute | solution.py:410
  (112 shorter events, 22.9 us)
Async XLA Ops:
  10.6 1.2 copy-start.11
  11.8 1.4 copy-start.13
  13.2 12.6 %copy-start.12 = (bf16[128,4096]{1,0:T(8,128)(2,1)S(1)}, bf16[128,4096]{1,0:T(8,128)(2,1)}, u32[]{:S(2)}) copy-start(bf16[128,4096]{1,0:T(8,128)(2,1)} %grad_ref.1) | copy-start | bytes 3145732
  17.0 1.4 copy-start.9
  18.4 39.0 %all-to-all-start = ((bf16[32,136,256]{2,1,0:T(8,128)(2,1)}), bf16[32,136,256]{2,1,0:T(8,128)(2,1)S(1)}, u32[]{:S(2)}, u32[]{:S(2)}) async-start(bf16[32,136,256]{2,1,0:T(8,128)(2,1)} %copy-done.9), calls=%async_computation | async-start | bytes 4456448 | tf_op jit(solution)/shard_map/all_to_all | solution.py:390
  30.3 1.4 copy-start.8
  31.7 1.2 copy-start.10
  57.4 4.7 %copy-start = (bf16[32,136,256]{2,1,0:T(8,128)(2,1)}, bf16[32,136,256]{2,1,0:T(8,128)(2,1)S(1)}, u32[]{:S(2)}) copy-start(bf16[32,136,256]{2,1,0:T(8,128)(2,1)S(1)} %all-to-all-done.got_ref.refs_0_) | copy-start | bytes 6684676
  57.4 30.1 %all-to-all-start.3 = ((bf16[32,104,256]{2,1,0:T(8,128)(2,1)}), bf16[32,104,256]{2,1,0:T(8,128)(2,1)}, u32[]{:S(2)}, u32[]{:S(2)}) async-start(bf16[32,104,256]{2,1,0:T(8,128)(2,1)} %copy-done.10), calls=%async_computation.5 | async-start | bytes 3407872 | tf_op jit(solution)/shard_map/all_to_all | solution.py:390
  62.1 34.3 %reduce-scatter.6.cloned.1.call-start = ((), (), s32[]{:S(2)}) async-start(), calls=%async_computation.11 | async-start | bytes 983040 | tf_op jit(solution)/shard_map/reduce_scatter | solution.py:398
  62.1 1.6 copy-start.1
  63.8 29.2 %copy-start.31 = (s32[4,32]{1,0:T(4,128)S(1)}, s32[4,32]{1,0:T(4,128)}, u32[]{:S(2)}) copy-start(s32[4,32]{1,0:T(4,128)} %param.10) | copy-start | bytes 1540
  65.8 74.5 %reduce-scatter.10.cloned.1.call-start = ((), (), s32[]{:S(2)}) async-start(), calls=%async_computation.13 | async-start | bytes 2949120 | tf_op jit(solution)/shard_map/reduce_scatter | solution.py:398
  91.5 1.4 copy-start.3
  98.0 36.4 %all-to-all-start.1 = ((bf16[32,136,256]{2,1,0:T(8,128)(2,1)}), bf16[32,136,256]{2,1,0:T(8,128)(2,1)}, u32[]{:S(2)}, u32[]{:S(2)}) async-start(bf16[32,136,256]{2,1,0:T(8,128)(2,1)} %copy-done.8), calls=%async_computation.2 | async-start | bytes 4456448 | tf_op jit(solution)/shard_map/all_to_all | solution.py:390
  102.8 86.6 %reduce-scatter.8.cloned.1.call-start = ((), (), s32[]{:S(2)}) async-start(), calls=%async_computation.12 | async-start | bytes 3932160 | tf_op jit(solution)/shard_map/reduce_scatter | solution.py:398
  102.9 9.7 %collective-permute-start = (bf16[192,256]{1,0:T(8,128)(2,1)S(1)}, bf16[192,256]{1,0:T(8,128)(2,1)S(1)}, u32[]{:S(2)}, u32[]{:S(2)}) collective-permute-start(bf16[192,256]{1,0:T(8,128)(2,1)S(1)} %get-tuple-element.63), channel_id=1, source_target_pairs={{0,32},{32,64},{64,96},{96,0},{1,33},{33,65},{65,97},{97,1},{2,34}... | collective-permute-start | bytes 294920 | tf_op jit(solution)/shard_map/ppermute | solution.py:410
  104.9 13.2 %collective-permute-start.1 = (bf16[192,256]{1,0:T(8,128)(2,1)S(1)}, bf16[192,256]{1,0:T(8,128)(2,1)S(1)}, u32[]{:S(2)}, u32[]{:S(2)}) collective-permute-start(bf16[192,256]{1,0:T(8,128)(2,1)S(1)} %get-tuple-element.64), channel_id=1, source_target_pairs={{0,64},{32,96},{64,0},{96,32},{1,65},{33,97},{65,1},{97,33},{2,66}... | collective-permute-start | bytes 294920 | tf_op jit(solution)/shard_map/ppermute | solution.py:410
  108.4 9.6 %collective-permute-start.2 = (bf16[192,256]{1,0:T(8,128)(2,1)S(1)}, bf16[192,256]{1,0:T(8,128)(2,1)S(1)}, u32[]{:S(2)}, u32[]{:S(2)}) collective-permute-start(bf16[192,256]{1,0:T(8,128)(2,1)S(1)} %get-tuple-element.65), channel_id=1, source_target_pairs={{0,96},{32,0},{64,32},{96,64},{1,97},{33,1},{65,33},{97,65},{2,98}... | collective-permute-start | bytes 294920 | tf_op jit(solution)/shard_map/ppermute | solution.py:410
  112.5 29.8 %copy-start.25 = (bf16[192,256]{1,0:T(8,128)(2,1)}, bf16[192,256]{1,0:T(8,128)(2,1)S(1)}, u32[]{:S(2)}) copy-start(bf16[192,256]{1,0:T(8,128)(2,1)S(1)} %collective-permute-done) | copy-start | bytes 294916
  118.1 24.2 %copy-start.27 = (bf16[192,256]{1,0:T(8,128)(2,1)}, bf16[192,256]{1,0:T(8,128)(2,1)S(1)}, u32[]{:S(2)}) copy-start(bf16[192,256]{1,0:T(8,128)(2,1)S(1)} %collective-permute-done.1) | copy-start | bytes 294916
  118.1 24.2 %copy-start.29 = (bf16[192,256]{1,0:T(8,128)(2,1)}, bf16[192,256]{1,0:T(8,128)(2,1)S(1)}, u32[]{:S(2)}) copy-start(bf16[192,256]{1,0:T(8,128)(2,1)S(1)} %collective-permute-done.2) | copy-start | bytes 294916
  142.3 37.2 %all-to-all-start.4 = ((bf16[32,136,256]{2,1,0:T(8,128)(2,1)}), bf16[32,136,256]{2,1,0:T(8,128)(2,1)}, u32[]{:S(2)}, u32[]{:S(2)}) async-start(bf16[32,136,256]{2,1,0:T(8,128)(2,1)} %get-tuple-element.70), calls=%async_computation.7 | async-start | bytes 4456448 | tf_op jit(solution)/shard_map/all_to_all | solution.py:390
  147.1 123.3 %reduce-scatter.12.cloned.1.call-start = ((), (), s32[]{:S(2)}) async-start(), calls=%async_computation.14 | async-start | bytes 3932160 | tf_op jit(solution)/shard_map/reduce_scatter | solution.py:398
  147.2 18.3 %collective-permute-start.3 = (bf16[192,768]{1,0:T(8,128)(2,1)}, bf16[192,768]{1,0:T(8,128)(2,1)S(1)}, u32[]{:S(2)}, u32[]{:S(2)}) collective-permute-start(bf16[192,768]{1,0:T(8,128)(2,1)} %get-tuple-element.72), channel_id=1, source_target_pairs={{0,32},{32,64},{64,96},{96,0},{1,33},{33,65},{65,97},{97,1},{2,34}... | collective-permute-start | bytes 884744 | tf_op jit(solution)/shard_map/ppermute | solution.py:410
  149.2 30.3 %collective-permute-start.4 = (bf16[192,768]{1,0:T(8,128)(2,1)}, bf16[192,768]{1,0:T(8,128)(2,1)S(1)}, u32[]{:S(2)}, u32[]{:S(2)}) collective-permute-start(bf16[192,768]{1,0:T(8,128)(2,1)} %get-tuple-element.73), channel_id=1, source_target_pairs={{0,64},{32,96},{64,0},{96,32},{1,65},{33,97},{65,1},{97,33},{2,66}... | collective-permute-start | bytes 884744 | tf_op jit(solution)/shard_map/ppermute | solution.py:410
  152.8 26.7 %collective-permute-start.5 = (bf16[192,768]{1,0:T(8,128)(2,1)S(1)}, bf16[192,768]{1,0:T(8,128)(2,1)S(1)}, u32[]{:S(2)}, u32[]{:S(2)}) collective-permute-start(bf16[192,768]{1,0:T(8,128)(2,1)S(1)} %get-tuple-element.74), channel_id=1, source_target_pairs={{0,96},{32,0},{64,32},{96,64},{1,97},{33,1},{65,33},{97,65},{2,98}... | collective-permute-start | bytes 884744 | tf_op jit(solution)/shard_map/ppermute | solution.py:410
  165.5 26.2 %copy-start.19 = (bf16[192,768]{1,0:T(8,128)(2,1)}, bf16[192,768]{1,0:T(8,128)(2,1)S(1)}, u32[]{:S(2)}) copy-start(bf16[192,768]{1,0:T(8,128)(2,1)S(1)} %collective-permute-done.3) | copy-start | bytes 884740
  179.5 12.2 %copy-start.21 = (bf16[192,768]{1,0:T(8,128)(2,1)}, bf16[192,768]{1,0:T(8,128)(2,1)S(1)}, u32[]{:S(2)}) copy-start(bf16[192,768]{1,0:T(8,128)(2,1)S(1)} %collective-permute-done.4) | copy-start | bytes 884740
  179.5 12.2 %copy-start.23 = (bf16[192,768]{1,0:T(8,128)(2,1)}, bf16[192,768]{1,0:T(8,128)(2,1)S(1)}, u32[]{:S(2)}) copy-start(bf16[192,768]{1,0:T(8,128)(2,1)S(1)} %collective-permute-done.5) | copy-start | bytes 884740
  191.7 40.8 %all-to-all-start.2 = ((bf16[32,136,256]{2,1,0:T(8,128)(2,1)}), bf16[32,136,256]{2,1,0:T(8,128)(2,1)}, u32[]{:S(2)}, u32[]{:S(2)}) async-start(bf16[32,136,256]{2,1,0:T(8,128)(2,1)} %get-tuple-element.67), calls=%async_computation.4 | async-start | bytes 4456448 | tf_op jit(solution)/shard_map/all_to_all | solution.py:390
  199.0 106.6 %reduce-scatter.14.cloned.1.call-start = ((), (), s32[]{:S(2)}) async-start(), calls=%async_computation.15 | async-start | bytes 3932160 | tf_op jit(solution)/shard_map/reduce_scatter | solution.py:398
  199.0 2.1 copy-start.2
  203.1 1.7 copy-start.5
  204.7 27.8 %collective-permute-start.6 = (bf16[192,1024]{1,0:T(8,128)(2,1)}, bf16[192,1024]{1,0:T(8,128)(2,1)}, u32[]{:S(2)}, u32[]{:S(2)}) collective-permute-start(bf16[192,1024]{1,0:T(8,128)(2,1)} %get-tuple-element.86), channel_id=1, source_target_pairs={{0,32},{32,64},{64,96},{96,0},{1,33},{33,65},{65,97},{97,1},{2,34}... | collective-permute-start | bytes 1179656 | tf_op jit(solution)/shard_map/ppermute | solution.py:410
  204.7 37.0 %collective-permute-start.7 = (bf16[192,1024]{1,0:T(8,128)(2,1)}, bf16[192,1024]{1,0:T(8,128)(2,1)}, u32[]{:S(2)}, u32[]{:S(2)}) collective-permute-start(bf16[192,1024]{1,0:T(8,128)(2,1)} %get-tuple-element.87), channel_id=1, source_target_pairs={{0,64},{32,96},{64,0},{96,32},{1,65},{33,97},{65,1},{97,33},{2,66}... | collective-permute-start | bytes 1179656 | tf_op jit(solution)/shard_map/ppermute | solution.py:410
  206.4 37.4 %collective-permute-start.8 = (bf16[192,1024]{1,0:T(8,128)(2,1)}, bf16[192,1024]{1,0:T(8,128)(2,1)S(1)}, u32[]{:S(2)}, u32[]{:S(2)}) collective-permute-start(bf16[192,1024]{1,0:T(8,128)(2,1)} %get-tuple-element.88), channel_id=1, source_target_pairs={{0,96},{32,0},{64,32},{96,64},{1,97},{33,1},{65,33},{97,65},{2,98}... | collective-permute-start | bytes 1179656 | tf_op jit(solution)/shard_map/ppermute | solution.py:410
  214.1 1.7 copy-start.6
  222.5 1.7 copy-start.7
  230.9 1.6 copy-start.4
  243.8 6.2 %copy-start.17 = (bf16[192,1024]{1,0:T(8,128)(2,1)}, bf16[192,1024]{1,0:T(8,128)(2,1)S(1)}, u32[]{:S(2)}) copy-start(bf16[192,1024]{1,0:T(8,128)(2,1)S(1)} %collective-permute-done.8) | copy-start | bytes 1179652
  250.0 4.0 %copy-start.16 = (bf16[192,256]{1,0:T(8,128)(2,1)S(1)}, bf16[192,256]{1,0:T(8,128)(2,1)}, u32[]{:S(2)}) copy-start(bf16[192,256]{1,0:T(8,128)(2,1)} %get-tuple-element.95) | copy-start | bytes 294916
  250.0 4.6 %copy-start.26 = (bf16[192,256]{1,0:T(8,128)(2,1)S(1)}, bf16[192,256]{1,0:T(8,128)(2,1)}, u32[]{:S(2)}) copy-start(bf16[192,256]{1,0:T(8,128)(2,1)} %copy-done.25) | copy-start | bytes 294916
  250.0 5.3 %copy-start.28 = (bf16[192,256]{1,0:T(8,128)(2,1)S(1)}, bf16[192,256]{1,0:T(8,128)(2,1)}, u32[]{:S(2)}) copy-start(bf16[192,256]{1,0:T(8,128)(2,1)} %copy-done.27) | copy-start | bytes 294916
  250.0 5.9 %copy-start.30 = (bf16[192,256]{1,0:T(8,128)(2,1)S(1)}, bf16[192,256]{1,0:T(8,128)(2,1)}, u32[]{:S(2)}) copy-start(bf16[192,256]{1,0:T(8,128)(2,1)} %copy-done.29) | copy-start | bytes 294916
  250.0 6.6 %copy-start.15 = (bf16[192,768]{1,0:T(8,128)(2,1)S(1)}, bf16[192,768]{1,0:T(8,128)(2,1)}, u32[]{:S(2)}) copy-start(bf16[192,768]{1,0:T(8,128)(2,1)} %get-tuple-element.99) | copy-start | bytes 884740
  250.0 7.3 %copy-start.20 = (bf16[192,768]{1,0:T(8,128)(2,1)S(1)}, bf16[192,768]{1,0:T(8,128)(2,1)}, u32[]{:S(2)}) copy-start(bf16[192,768]{1,0:T(8,128)(2,1)} %copy-done.19) | copy-start | bytes 884740
  250.0 8.0 %copy-start.22 = (bf16[192,768]{1,0:T(8,128)(2,1)S(1)}, bf16[192,768]{1,0:T(8,128)(2,1)}, u32[]{:S(2)}) copy-start(bf16[192,768]{1,0:T(8,128)(2,1)} %copy-done.21) | copy-start | bytes 884740
  250.0 8.8 %copy-start.24 = (bf16[192,768]{1,0:T(8,128)(2,1)S(1)}, bf16[192,768]{1,0:T(8,128)(2,1)}, u32[]{:S(2)}) copy-start(bf16[192,768]{1,0:T(8,128)(2,1)} %copy-done.23) | copy-start | bytes 884740
  268.6 13.2 %copy-start.18 = (bf16[192,1024]{1,0:T(8,128)(2,1)S(1)}, bf16[192,1024]{1,0:T(8,128)(2,1)}, u32[]{:S(2)}) copy-start(bf16[192,1024]{1,0:T(8,128)(2,1)} %copy-done.17) | copy-start | bytes 1179652
  272.7 35.7 %all-to-all-start.5 = ((bf16[32,104,256]{2,1,0:T(8,128)(2,1)}), bf16[32,104,256]{2,1,0:T(8,128)(2,1)S(1)}, u32[]{:S(2)}, u32[]{:S(2)}) async-start(bf16[32,104,256]{2,1,0:T(8,128)(2,1)} %project.9), calls=%async_computation.9 | async-start | bytes 3407872 | tf_op jit(solution)/shard_map/all_to_all | solution.py:390
  281.7 13.7 %collective-permute-start.9 = (bf16[192,1024]{1,0:T(8,128)(2,1)}, bf16[192,1024]{1,0:T(8,128)(2,1)S(1)}, u32[]{:S(2)}, u32[]{:S(2)}) collective-permute-start(bf16[192,1024]{1,0:T(8,128)(2,1)} %get-tuple-element.108), channel_id=1, source_target_pairs={{0,32},{32,64},{64,96},{96,0},{1,33},{33,65},{65,97},{97,1},{2,34}... | collective-permute-start | bytes 1179656 | tf_op jit(solution)/shard_map/ppermute | solution.py:410
  282.6 21.4 %collective-permute-start.10 = (bf16[192,1024]{1,0:T(8,128)(2,1)}, bf16[192,1024]{1,0:T(8,128)(2,1)S(1)}, u32[]{:S(2)}, u32[]{:S(2)}) collective-permute-start(bf16[192,1024]{1,0:T(8,128)(2,1)} %get-tuple-element.109), channel_id=1, source_target_pairs={{0,64},{32,96},{64,0},{96,32},{1,65},{33,97},{65,1},{97,33},{2,66}... | collective-permute-start | bytes 1179656 | tf_op jit(solution)/shard_map/ppermute | solution.py:410
  284.3 20.5 %collective-permute-start.11 = (bf16[192,1024]{1,0:T(8,128)(2,1)}, bf16[192,1024]{1,0:T(8,128)(2,1)S(1)}, u32[]{:S(2)}, u32[]{:S(2)}) collective-permute-start(bf16[192,1024]{1,0:T(8,128)(2,1)} %get-tuple-element.110), channel_id=1, source_target_pairs={{0,96},{32,0},{64,32},{96,64},{1,97},{33,1},{65,33},{97,65},{2,98}... | collective-permute-start | bytes 1179656 | tf_op jit(solution)/shard_map/ppermute | solution.py:410
  307.8 13.2 %collective-permute-start.12 = (bf16[192,1024]{1,0:T(8,128)(2,1)}, bf16[192,1024]{1,0:T(8,128)(2,1)}, u32[]{:S(2)}, u32[]{:S(2)}) collective-permute-start(bf16[192,1024]{1,0:T(8,128)(2,1)} %get-tuple-element.122), channel_id=1, source_target_pairs={{0,32},{32,64},{64,96},{96,0},{1,33},{33,65},{65,97},{97,1},{2,34}... | collective-permute-start | bytes 1179656 | tf_op jit(solution)/shard_map/ppermute | solution.py:410
  308.4 1.4 copy-start.14
  314.7 14.3 %collective-permute-start.13 = (bf16[192,1024]{1,0:T(8,128)(2,1)}, bf16[192,1024]{1,0:T(8,128)(2,1)S(1)}, u32[]{:S(2)}, u32[]{:S(2)}) collective-permute-start(bf16[192,1024]{1,0:T(8,128)(2,1)} %get-tuple-element.121), channel_id=1, source_target_pairs={{0,64},{32,96},{64,0},{96,32},{1,65},{33,97},{65,1},{97,33},{2,66}... | collective-permute-start | bytes 1179656 | tf_op jit(solution)/shard_map/ppermute | solution.py:410
  317.7 18.0 %collective-permute-start.14 = (bf16[192,1024]{1,0:T(8,128)(2,1)}, bf16[192,1024]{1,0:T(8,128)(2,1)S(1)}, u32[]{:S(2)}, u32[]{:S(2)}) collective-permute-start(bf16[192,1024]{1,0:T(8,128)(2,1)} %get-tuple-element.120), channel_id=1, source_target_pairs={{0,96},{32,0},{64,32},{96,64},{1,97},{33,1},{65,33},{97,65},{2,98}... | collective-permute-start | bytes 1179656 | tf_op jit(solution)/shard_map/ppermute | solution.py:410
Sparse Core Ops, SparseCore 0:
  65.9 25.0 reduce-scatter.5
  93.4 35.8 reduce-scatter.9
  140.3 49.0 reduce-scatter.7
  191.7 54.8 reduce-scatter.11
  250.2 38.7 reduce-scatter.13
where the time goes:
time: 344 us; the launch traced here: 343 us
  waiting for transfers between devices  141 us (41%)
  Pallas kernels  65.8 us (19%)
  starting transfers between devices  61.5 us (18%)
  local copies, waits for them, and re-layouts  43.2 us (13%)
  between operations  16.9 us (5%)
  other arithmetic  14.9 us (4%)
    ppermute x15, waiting for transfers between devices, moved(): lax.ppermute(sends[d], 'grp', hops[d])  74.3 us
    all_to_all x6, waiting for transfers between devices, exchange(): return lax.all_to_all(v, 'sp', 0, 0, tiled=True)  62.4 us
    all_to_all x6, starting transfers between devices, exchange(): return lax.all_to_all(v, 'sp', 0, 0, tiled=True)  36.2 us
    pallas_call x5, Pallas kernels, project(): pl.pallas_call(functools.partial(project_kernel, skip, parts, state is no...  29.4 us
    ppermute x15, starting transfers between devices, moved(): lax.ppermute(sends[d], 'grp', hops[d])  25.1 us
    pallas_call x4, Pallas kernels, weight_rest(): pl.pallas_call(functools.partial(weight_kernel, parts), grid=(parts,), in...  22.2 us
    unnamed x65, local copies, waits for them, and re-layouts  20.5 us
    dynamic_update_slice x19, local copies, waits for them, and re-layouts, place(): own = lax.dynamic_update_slice(own, blocks[d], (source * quarter, at))  17.1 us
  transfers between devices with their start and end apart: 26, of which 15 were waited for; matrix products, arithmetic and copies ran while one was open for 10% of the time, Pallas kernels for 18%

commit v1 on v0

--- a/solution.py
+++ b/solution.py
@@ -9,13 +9,12 @@
 
 V = 256
 MAIN = 32
-TAIL = 8
 SHIFT = 6
 MASK = (1 << SHIFT) - 1
-CHUNKS = (1, 3, 4, 4, 4)
+CHUNKS = (5, 6, 5)
 BF16 = jnp.bfloat16
 F32 = jnp.float32
-VMEM = 48 * 1024 * 1024
+MIB = 1024 * 1024
 
 
 def tie(first, second):
@@ -30,16 +29,28 @@
     return pl.CostEstimate(flops=int(flops), bytes_accessed=int(bytes_accessed), transcendentals=0)
 
 
-def params():
-    return pltpu.CompilerParams(vmem_limit_bytes=VMEM)
+def params(mib):
+    return pltpu.CompilerParams(vmem_limit_bytes=mib * MIB)
+
+
+def resident():
+    return pl.BlockSpec(memory_space=pltpu.VMEM)
+
+
+def in_hbm(x):
+    return pltpu.with_memory_space_constraint(x, pltpu.HBM)
 
 
 def whole(shape):
     return pl.BlockSpec(shape, lambda *_: (0,) * len(shape))
 
 
+def tail_size(n):
+    return (2 * n + 7) // 8 * 8
+
+
 def block_rows(n):
-    return MAIN * n + TAIL
+    return MAIN * n + tail_size(n)
 
 
 SEND_STEP = 8
@@ -50,10 +61,10 @@
     return ((first + i // MAIN) << SHIFT) + i % MAIN
 
 
-def tail_ids(first, part):
-    i = lax.broadcasted_iota(jnp.int32, (SEND_STEP * TAIL, 1), 0)
-    r = i % TAIL
-    return jnp.where(r // 2 == part, ((first + i // TAIL) << SHIFT) + MAIN + r % 2, -1)
+def tail_ids(first, size, part):
+    i = lax.broadcasted_iota(jnp.int32, (SEND_STEP * size, 1), 0)
+    r = i % size
+    return jnp.where(r // 2 == part, ((first + i // size) << SHIFT) + MAIN + r % 2, -1)
 
 
 def hits(ids, codes):
@@ -73,33 +84,36 @@
     ids = main_ids(first, SEND_STEP * MAIN)
     pick = jnp.where(ids == flat, prob, 0.0).astype(BF16)
     act_parts = act_ref.shape[1] // V
-    tail = jnp.zeros((SEND_STEP * TAIL, V), F32)
+    grad = grad_ref[...]
+    parts = grad.shape[1] // V
+    size = tail_size(act_parts + parts)
+    tail = jnp.zeros((SEND_STEP * size, V), F32)
     for p in range(act_parts):
         act = act_ref[:, p * V : (p + 1) * V]
         store_main(out_ref, p, dot(pick, act))
-        tail += dot(jnp.where(tail_ids(first, p) == flat, prob, 0.0).astype(BF16), act)
-    grad = grad_ref[...]
+        tail += dot(jnp.where(tail_ids(first, size, p) == flat, prob, 0.0).astype(BF16), act)
     grads = hits(ids, codes)
-    for p in range(grad.shape[1] // V):
+    for p in range(parts):
         part = grad[:, p * V : (p + 1) * V]
         store_main(out_ref, act_parts + p, dot(grads, part))
-        tail += dot(hits(tail_ids(first, act_parts + p), codes), part)
-    out_ref[:, out_ref.shape[1] - TAIL :, :] = tail.astype(BF16).reshape(SEND_STEP, TAIL, V)
-
-
-def send_kernel(chunks, codes_ref, grad_ref, *out_refs):
+        tail += dot(hits(tail_ids(first, size, act_parts + p), codes), part)
+    out_ref[:, out_ref.shape[1] - size :, :] = tail.astype(BF16).reshape(SEND_STEP, size, V)
+
+
+def send_kernel(start, chunks, codes_ref, grad_ref, *out_refs):
     first = pl.program_id(0) * SEND_STEP
     codes = codes_ref[...]
     grads = hits(main_ids(first, SEND_STEP * MAIN), codes)
-    at = 0
+    at = start * V
     for n, out_ref in zip(chunks, out_refs):
-        tail = jnp.zeros((SEND_STEP * TAIL, V), F32)
+        size = tail_size(n)
+        tail = jnp.zeros((SEND_STEP * size, V), F32)
         for p in range(n):
             part = grad_ref[:, at : at + V]
             store_main(out_ref, p, dot(grads, part))
-            tail += dot(hits(tail_ids(first, p), codes), part)
+            tail += dot(hits(tail_ids(first, size, p), codes), part)
             at += V
-        out_ref[:, MAIN * n :, :] = tail.astype(BF16).reshape(SEND_STEP, TAIL, V)
+        out_ref[:, MAIN * n :, :] = tail.astype(BF16).reshape(SEND_STEP, size, V)
 
 
 def send_first(codes, flat, prob, act, grad, columns, parts):
@@ -118,46 +132,43 @@
         ],
         out_specs=pl.BlockSpec((SEND_STEP, rows, V), lambda i: (i, 0, 0)),
         out_shape=jax.ShapeDtypeStruct((columns, rows, V), BF16),
-        compiler_params=params(),
+        compiler_params=params(24),
         cost_estimate=cost(2 * columns * MAIN * routes * hidden, 2 * columns * rows * V + 2 * routes * hidden),
         name="send_first",
     )(codes, flat, prob, act, grad)
 
 
-def send_rest(codes, grad, columns, chunks):
+def send_rest(codes, grad, columns, start, chunks):
     tok, width = grad.shape
     shapes = [(columns, block_rows(n), V) for n in chunks]
     return pl.pallas_call(
-        functools.partial(send_kernel, chunks),
+        functools.partial(send_kernel, start, chunks),
         grid=(columns // SEND_STEP,),
         in_specs=[whole(codes.shape), whole(grad.shape)],
         out_specs=[pl.BlockSpec((SEND_STEP, s[1], V), lambda i: (i, 0, 0)) for s in shapes],
         out_shape=[jax.ShapeDtypeStruct(s, BF16) for s in shapes],
-        compiler_params=params(),
+        compiler_params=params(24),
         cost_estimate=cost(2 * columns * MAIN * tok * width, 2 * columns * 34 * width + 2 * tok * width),
         name="send_rest",
     )(codes, grad)
 
 
 def sorted_tail(got_ref):
-    sources = got_ref.shape[0]
-    tail = got_ref[:, got_ref.shape[1] - TAIL :, :].astype(F32).reshape(sources * TAIL, V).astype(BF16)
-    size = sources * TAIL
+    sources, rows, _ = got_ref.shape
+    n = rows // MAIN
+    tail = tail_size(n)
+    size = sources * tail
+    values = got_ref[:, n * MAIN :, :].astype(F32).reshape(size, V).astype(BF16)
     i = lax.broadcasted_iota(jnp.int32, (size, size), 0)
     j = lax.broadcasted_iota(jnp.int32, (size, size), 1)
-    order = (i % sources == j // TAIL) & (i // sources == j % TAIL)
-    return dot(jnp.where(order, 1.0, 0.0).astype(BF16), tail).astype(BF16)
+    order = (i % sources == j // tail) & (i // sources == j % tail)
+    return dot(jnp.where(order, 1.0, 0.0).astype(BF16), values).astype(BF16)
 
 
 def main_rows(got_ref, part, expert):
     half = MAIN // 2
     rows = got_ref[:, pl.ds(part * MAIN + expert * half, half), :]
     return rows.reshape(got_ref.shape[0] * half, V)
-
-
-def tail_rows(tail, sources, part, expert):
-    at = (2 * part + expert) * sources
-    return tail[at : at + sources, :]
 
 
 def weight_step(acts, rows, more, out_ref, expert):
@@ -168,18 +179,24 @@
         out_ref[q, expert] = total[q * size : (q + 1) * size].astype(BF16)
 
 
-def weight_first_kernel(act_parts, got_ref, acts_ref, out_ref):
+def weight_first_kernel(act_parts, got_ref, acts_ref, out_ref, tail_ref):
     sources = got_ref.shape[0]
-    tail = sorted_tail(got_ref)
+    part = pl.program_id(0)
+
+    @pl.when(part == 0)
+    def _():
+        tail_ref[...] = sorted_tail(got_ref)
+        for e in range(2):
+            for p in range(act_parts):
+                block = main_rows(got_ref, p, e)
+                more = tail_ref[(2 * p + e) * sources : (2 * p + e + 1) * sources, :]
+                acts_ref[e, p * V : (p + 1) * V, : block.shape[0]] = block.astype(F32).T.astype(BF16)
+                acts_ref[e, p * V : (p + 1) * V, block.shape[0] :] = more.astype(F32).T.astype(BF16)
+
     for e in range(2):
-        for p in range(act_parts):
-            block = main_rows(got_ref, p, e)
-            more = tail_rows(tail, sources, p, e)
-            acts_ref[e, p * V : (p + 1) * V, : block.shape[0]] = block.astype(F32).T.astype(BF16)
-            acts_ref[e, p * V : (p + 1) * V, block.shape[0] :] = more.astype(F32).T.astype(BF16)
-        weight_step(
-            acts_ref[e], main_rows(got_ref, act_parts, e), tail_rows(tail, sources, act_parts, e), out_ref, e
-        )
+        at = pl.multiple_of((2 * (act_parts + part) + e) * sources, sources)
+        more = tail_ref[pl.ds(at, sources), :]
+        weight_step(acts_ref[e], main_rows(got_ref, act_parts + part, e), more, out_ref, e)
 
 
 def weight_kernel(parts, acts_ref, got_ref, out_ref, tail_ref):
@@ -195,20 +212,24 @@
         weight_step(acts_ref[e], main_rows(got_ref, part, e), more, out_ref, e)
 
 
-def weight_first(got, hidden, groups):
+def weight_first(got, hidden, parts, groups):
     sources = got.shape[0]
     depth = sources * (MAIN // 2 + 1)
     return pl.pallas_call(
         functools.partial(weight_first_kernel, hidden // V),
-        grid=(1,),
-        in_specs=[whole(got.shape)],
-        out_specs=[whole((2, hidden, depth)), whole((groups, 2, hidden // groups, V))],
+        grid=(parts,),
+        in_specs=[resident()],
+        out_specs=[
+            whole((2, hidden, depth)),
+            pl.BlockSpec((groups, 2, hidden // groups, V), lambda p: (0, 0, 0, p)),
+        ],
         out_shape=[
-            jax.ShapeDtypeStruct((2, hidden, depth), BF16),
-            jax.ShapeDtypeStruct((groups, 2, hidden // groups, V), BF16),
+            pltpu.HBM((2, hidden, depth), BF16),
+            pltpu.HBM((groups, 2, hidden // groups, parts * V), BF16),
         ],
-        compiler_params=params(),
-        cost_estimate=cost(4 * depth * hidden * V, 2 * (got.size + 4 * depth * hidden)),
+        scratch_shapes=[pltpu.VMEM((sources * (got.shape[1] % MAIN), V), BF16)],
+        compiler_params=params(16),
+        cost_estimate=cost(4 * depth * hidden * V * parts, 2 * (got.size + 4 * depth * hidden)),
         name="weight_first",
     )(got)
 
@@ -218,14 +239,14 @@
     return pl.pallas_call(
         functools.partial(weight_kernel, parts),
         grid=(parts,),
-        in_specs=[whole(acts.shape), whole(got.shape)],
+        in_specs=[whole(acts.shape), resident()],
         out_specs=pl.BlockSpec((groups, 2, hidden // groups, V), lambda p: (0, 0, 0, p)),
-        out_shape=jax.ShapeDtypeStruct((groups, 2, hidden // groups, parts * V), BF16),
-        scratch_shapes=[pltpu.VMEM((got.shape[0] * TAIL, V), BF16)],
-        compiler_params=params(),
+        out_shape=pltpu.HBM((groups, 2, hidden // groups, parts * V), BF16),
+        scratch_shapes=[pltpu.VMEM((got.shape[0] * (got.shape[1] % MAIN), V), BF16)],
+        compiler_params=params(16),
         cost_estimate=cost(4 * depth * hidden * V * parts, 2 * (got.size + acts.size + 2 * hidden * V * parts)),
         name="weight_rest",
-    )(acts, got)
+    )(in_hbm(acts), got)
 
 
 def project_kernel(skip, parts, chained, final, *refs):
@@ -266,7 +287,8 @@
         def _():
             hidden = weight_ref.shape[1]
             n = hidden // V
-            size = sources * TAIL
+            rows = tail_size(n)
+            size = sources * rows
             i = lax.broadcasted_iota(jnp.int32, (size, sources), 0)
             j = lax.broadcasted_iota(jnp.int32, (size, sources), 1)
             tail = jnp.zeros((size, V), F32)
@@ -275,10 +297,10 @@
                     block = main_acc[e, :, p * V : (p + 1) * V].astype(BF16)
                     at = p * MAIN + e * half
                     out_ref[:, at : at + half, :] = block.reshape(sources, half, V)
-                    order = (i // TAIL == j) & (i % TAIL == 2 * p + e)
+                    order = (i // rows == j) & (i % rows == 2 * p + e)
                     more = tail_acc[e, :, p * V : (p + 1) * V].astype(BF16)
                     tail += dot(jnp.where(order, 1.0, 0.0).astype(BF16), more)
-            out_ref[:, n * MAIN :, :] = tail.reshape(sources, TAIL, V).astype(BF16)
+            out_ref[:, n * MAIN :, :] = tail.reshape(sources, rows, V).astype(BF16)
 
 
 def project(got, weight, at, skip, parts, state, final):
@@ -286,18 +308,18 @@
     hidden = weight.shape[1]
     half = MAIN // 2
     main_shape, tail_shape = (2, sources * half, hidden), (2, sources, hidden)
-    in_specs = [whole(got.shape), pl.BlockSpec((2, hidden, V), lambda p: (0, 0, at + p))]
-    args = [got, weight]
+    in_specs = [resident(), pl.BlockSpec((2, hidden, V), lambda p: (0, 0, at + p))]
+    args = [got, in_hbm(weight)]
     if state is not None:
-        in_specs += [whole(main_shape), whole(tail_shape)]
+        in_specs += [resident(), resident()]
         args += list(state)
-    scratch = [pltpu.VMEM((sources * TAIL, V), BF16)]
+    scratch = [pltpu.VMEM((sources * (got.shape[1] % MAIN), V), BF16)]
     if final:
         shape = (sources, block_rows(hidden // V), V)
-        out_specs, out_shape = whole(shape), jax.ShapeDtypeStruct(shape, BF16)
+        out_specs, out_shape = resident(), jax.ShapeDtypeStruct(shape, BF16)
         scratch = [pltpu.VMEM(main_shape, F32), pltpu.VMEM(tail_shape, F32)] + scratch
     else:
-        out_specs = [whole(main_shape), whole(tail_shape)]
+        out_specs = [resident(), resident()]
         out_shape = [jax.ShapeDtypeStruct(main_shape, F32), jax.ShapeDtypeStruct(tail_shape, F32)]
     return pl.pallas_call(
         functools.partial(project_kernel, skip, parts, state is not None, final),
@@ -306,7 +328,7 @@
         out_specs=out_specs,
         out_shape=out_shape,
         scratch_shapes=scratch,
-        compiler_params=params(),
+        compiler_params=params(20),
         cost_estimate=cost(4 * sources * 17 * hidden * V * parts, 2 * got.size + 4 * hidden * V * parts + 16 * sources * 17 * hidden),
         name="project",
     )(*args)
@@ -325,13 +347,14 @@
     main_id = jnp.where(row < MAIN, column * MAIN + row, -1)
     lanes = lax.broadcasted_iota(jnp.int32, (steps, sources * MAIN), 1)
     pick = jnp.where(lanes == main_id, 1.0, 0.0).astype(BF16)
-    tail = back_ref[:, n * MAIN :, :].astype(F32).reshape(sources * TAIL, V).astype(BF16)
-    lanes = lax.broadcasted_iota(jnp.int32, (steps, sources * TAIL), 1)
+    rows = tail_size(n)
+    tail = back_ref[:, n * MAIN :, :].astype(F32).reshape(sources * rows, V).astype(BF16)
+    lanes = lax.broadcasted_iota(jnp.int32, (steps, sources * rows), 1)
     prob = prob_ref[...]
     total = jnp.zeros((steps, 1), F32)
     for p in range(n):
         main = back_ref[:, p * MAIN : (p + 1) * MAIN, :].reshape(sources * MAIN, V)
-        tail_id = jnp.where(row >= MAIN, column * TAIL + 2 * p + (row - MAIN), -1)
+        tail_id = jnp.where(row >= MAIN, column * rows + 2 * p + (row - MAIN), -1)
         proj = dot(pick, main) + dot(jnp.where(lanes == tail_id, 1.0, 0.0).astype(BF16), tail)
         act = act_ref[:, p * V : (p + 1) * V].astype(F32)
         total += jnp.sum(act * proj, axis=1, keepdims=True)
@@ -346,13 +369,45 @@
     return pl.pallas_call(
         finish_kernel,
         grid=(routes // FINISH_STEP,),
-        in_specs=[one, one, rows, whole(back.shape)],
+        in_specs=[one, one, rows, resident()],
         out_specs=[rows, one],
         out_shape=[jax.ShapeDtypeStruct((routes, hidden), BF16), jax.ShapeDtypeStruct((routes, 1), F32)],
-        compiler_params=params(),
+        compiler_params=params(24),
         cost_estimate=cost(2 * routes * routes * hidden, 2 * (back.size + 2 * routes * hidden)),
         name="finish",
     )(code, prob, act, back)
+
+
+def place_kernel(column, first, sources_ref, *refs):
+    blocks, (out_ref, sems) = refs[:4], refs[-2:]
+    copies = []
+    for d, block in enumerate(blocks):
+        rows, size = block.shape
+        row = pl.multiple_of(sources_ref[d] * rows, rows)
+        copies.append(
+            pltpu.make_async_copy(block, out_ref.at[pl.ds(row, rows), pl.ds(column, size)], sems.at[d])
+        )
+    for copy in copies:
+        copy.start()
+    for copy in copies:
+        copy.wait()
+
+
+def place(sources, blocks, own, hidden, width, column):
+    first = own is None
+    args = [sources, *blocks] + ([] if first else [own])
+    anywhere = pl.BlockSpec(memory_space=pl.ANY)
+    return pl.pallas_call(
+        functools.partial(place_kernel, column, first),
+        in_specs=[pl.BlockSpec(memory_space=pltpu.SMEM)] + [anywhere] * (len(args) - 1),
+        out_specs=anywhere,
+        out_shape=jax.ShapeDtypeStruct((hidden, width), BF16),
+        scratch_shapes=[pltpu.SemaphoreType.DMA((len(blocks),))],
+        input_output_aliases={} if first else {len(args) - 1: 0},
+        compiler_params=params(4),
+        cost_estimate=cost(0, 4 * hidden * blocks[0].shape[1]),
+        name="place",
+    )(*args)
 
 
 def route_codes(routes, columns):
@@ -404,49 +459,43 @@
             out.append(jnp.where(which == 0, mine[0], mine[1]))
         return out
 
-    own = jnp.zeros((hidden, width), BF16)
-
     def moved(sends):
         return [lax.ppermute(sends[d], "grp", hops[d]) if d else sends[d] for d in range(groups)]
 
-    def place(own, blocks, at):
-        for d in range(groups):
-            source = (my_group + groups - d) % groups
-            own = lax.dynamic_update_slice(own, blocks[d], (source * quarter, at))
-        return own
+    sources = jnp.stack([(my_group + groups - d) % groups for d in range(groups)]).astype(jnp.int32)
 
     codes_t = codes.T
     first = send_first(codes_t, flat, prob.reshape(1, tok * top), act, grad_out, columns, CHUNKS[0])
     got = {0: exchange(first)}
-    outs = send_rest(codes_t, grad_out[:, CHUNKS[0] * V :], columns, CHUNKS[1:])
+    outs = send_rest(codes_t, grad_out, columns, CHUNKS[0], CHUNKS[1:])
+    got[0], outs = tie(got[0], outs)
     outs = dict(enumerate(outs, 1))
 
     starts = [sum(CHUNKS[:c]) for c in range(last + 1)]
-    mine, sends, blocks = {}, {}, {}
+    mine, sends = {}, {}
     state = None
-    acts, part = weight_first(got[0], hidden, groups)
+    acts, part = weight_first(got[0], hidden, CHUNKS[0], groups)
     for c in range(last + 1):
         if c:
             if c == last:
-                got[c], state = tie(got[c], state)
-            if c >= 2:
-                got[c], blocks[c - 2] = tie(got[c], moved(sends[c - 2]))
+                sends[c - 2] = wanted(mine[c - 2])
+                got[c], state, blocks = lax.optimization_barrier((got[c], state, moved(sends[c - 2])))
             part = weight_rest(acts, got[c], CHUNKS[c], groups)
         mine[c] = reduced(part)
         if c < last:
-            if c >= 1:
-                outs[c + 1], sends[c - 1] = tie(outs[c + 1], wanted(mine[c - 1]))
             got[c + 1] = exchange(outs[c + 1])
             skip = act_parts if c == 0 else 0
             state = project(got[c], down_weight, starts[c], skip, CHUNKS[c], state, False)
     proj = project(got[last], down_weight, starts[last], 0, CHUNKS[last], state, True)
     proj, sends[last - 1] = tie(proj, wanted(mine[last - 1]))
     back = exchange(proj)
-    sends[last] = wanted(mine[last])
+    grad_act, grad_prob = finish(codes.reshape(tok * top, 1), prob.reshape(tok * top, 1), act, back)
+    mine[last], grad_act, grad_prob = lax.optimization_barrier((mine[last], grad_act, grad_prob))
+    own = None
     for c in range(last + 1):
-        own = place(own, blocks[c] if c in blocks else moved(sends[c]), starts[c] * V)
-
-    grad_act, grad_prob = finish(codes.reshape(tok * top, 1), prob.reshape(tok * top, 1), act, back)
+        if c not in sends:
+            sends[c] = wanted(mine[c])
+        own = place(sources, moved(sends[c]) if c else blocks, own, hidden, width, starts[c] * V)
     return (
         grad_act.reshape(tok, top, hidden),
         grad_prob.reshape(tok, top),

time: 344 us -> 420 us (1.22)
  Pallas kernels: 65.8 us -> 174 us
  blocking collectives: 0 us -> 46.7 us
  waiting for transfers between devices: 141 us -> 113 us
  starting transfers between devices: 61.5 us -> 37.2 us
  local copies, waits for them, and re-layouts: 43.2 us -> 21 us
  other arithmetic: 14.9 us -> 10.5 us
    pallas_call x1 -> x4, Pallas kernels: 4.42 us -> 118 us  [the longest x3 115 us: place(): pl.pallas_call(functools.partial(place_kernel, column, first), in_specs=[...]
    ppermute x15 -> x9, waiting for transfers between devices: 74.3 us -> 16.3 us  [moved(): lax.ppermute(sends[d], 'grp', hops[d])]
    all_to_all x0 -> x1, blocking collectives: none -> 46.7 us  [exchange(): return lax.all_to_all(v, 'sp', 0, 0, tiled=True)]
    dynamic_update_slice x19 -> x0, local copies, waits for them, and re-layouts: 17.1 us -> none  [place(): own = lax.dynamic_update_slice(own, blocks[d], (source * quarter, at))]
    all_to_all x6 -> x3, starting transfers between devices: 36.2 us -> 19.8 us  [exchange(): return lax.all_to_all(v, 'sp', 0, 0, tiled=True)]
    all_to_all x6 -> x3, waiting for transfers between devices: 62.4 us -> 77.9 us  [exchange(): return lax.all_to_all(v, 'sp', 0, 0, tiled=True)]
    reduce_scatter x5 -> x3, waiting for transfers between devices: 3.76 us -> 18.8 us  [reduced(): lax.psum_scatter(flat_part, 'grp', scatter_dimension=0, tiled=True)]
    ppermute x15 -> x9, starting transfers between devices: 25.1 us -> 17.2 us  [moved(): lax.ppermute(sends[d], 'grp', hops[d])]
  transfers between devices with their start and end apart: 26 -> 15, of which waited for: 15 -> 5; matrix products, arithmetic and copies ran while one was open for 10% -> 3% of each run, Pallas kernels for 18% -> 31%
where the time goes in v1:
time: 420 us; the launch traced here: 419 us
  Pallas kernels  174 us (41%)
  waiting for transfers between devices  113 us (27%)
  blocking collectives  46.7 us (11%)
  starting transfers between devices  37.2 us (9%)
  local copies, waits for them, and re-layouts  21 us (5%)
  between operations  16.5 us (4%)
  other arithmetic  10.5 us (2%)
    pallas_call x3, Pallas kernels, place(): pl.pallas_call(functools.partial(place_kernel, column, first), in_specs=[...  115 us
    all_to_all x3, waiting for transfers between devices, exchange(): return lax.all_to_all(v, 'sp', 0, 0, tiled=True)  77.9 us
    all_to_all x1, blocking collectives, exchange(): return lax.all_to_all(v, 'sp', 0, 0, tiled=True)  46.7 us
    pallas_call x3, Pallas kernels, project(): pl.pallas_call(functools.partial(project_kernel, skip, parts, state is no...  23.6 us
    all_to_all x3, starting transfers between devices, exchange(): return lax.all_to_all(v, 'sp', 0, 0, tiled=True)  19.8 us
    reduce_scatter x3, waiting for transfers between devices, reduced(): lax.psum_scatter(flat_part, 'grp', scatter_dimension=0, tiled=True)  18.8 us
    unnamed x35, local copies, waits for them, and re-layouts  17.3 us
    ppermute x9, starting transfers between devices, moved(): lax.ppermute(sends[d], 'grp', hops[d])  17.2 us
  transfers between devices with their start and end apart: 15, of which 5 were waited for; matrix products, arithmetic and copies ran while one was open for 3% of the time, Pallas kernels for 31%

profile of v1, /device:TPU:0, one launch (start us, length us, event | category | flops | bytes accessed | tf_op | source)
XLA Modules:
  0.0 419.2 jit_solution(11687656811903257553)
XLA Ops:
  7.2 0.7 fusion
  7.9 0.1 fusion.1
  8.0 0.7 select_reduce_fusion
  8.8 0.7 fusion.3
  9.5 0.1 copy.26
  9.6 0.1 reshape.88.flat_ref
  9.7 0.8 copy.27
  10.5 0.1 reshape.89.prob_ref
  10.6 1.4 copy-done.6
  12.0 1.2 copy-done.8
  13.2 4.6 %send_first.1 = bf16[32,272,256]{2,1,0:T(8,128)(2,1)S(1)} custom-call(s32[8,128]{1,0:T(8,128)S(1)} %bitcast.27, s32[1,1024]{1,0:T(1,128)S(1)} %reshape.88.flat_ref, f32[1,1024]{1,0:T(1,128)S(1)} %reshape.89.prob_ref, bf16[1024,768]{1,0:T(8,128)(2,1)S(1)} %bitcast.25, bf16[128,4096]{1,0:T(8,128)(2,1)S(1)} %copy-done.8), custom_call_target="tpu_custom_call" | custom-call | flops 1610612736 | bytes 6029312 | tf_op jit(solution)/shard_map/send_first/pallas_call | solution.py:123
  17.8 2.1 copy-done
  19.9 7.6 %all-to-all-start = ((bf16[32,272,256]{2,1,0:T(8,128)(2,1)}), bf16[32,272,256]{2,1,0:T(8,128)(2,1)}, u32[]{:S(2)}, u32[]{:S(2)}) async-start(bf16[32,272,256]{2,1,0:T(8,128)(2,1)} %copy-done), calls=%async_computation | async-start | bytes 8912896 | tf_op jit(solution)/shard_map/all_to_all | solution.py:445
  27.6 0.0 reduce-scatter.4.cloned.1.call-start
  27.6 3.2 send_rest.1
  30.9 1.7 copy-done.1
  32.6 1.6 copy-done.4
  34.1 50.2 %all-to-all-done.got_ref.refs_0_ = bf16[32,272,256]{2,1,0:T(8,128)(2,1)} async-done(((bf16[32,272,256]{2,1,0:T(8,128)(2,1)}), bf16[32,272,256]{2,1,0:T(8,128)(2,1)}, u32[]{:S(2)}, u32[]{:S(2)}) %all-to-all-start) | async-done | bytes 4456480 | tf_op jit(solution)/shard_map/all_to_all | solution.py:445
  84.3 8.1 %weight_first.1 = (bf16[2,768,544]{2,1,0:T(8,128)(2,1)}, bf16[4,2,192,1280]{3,2,1,0:T(8,128)(2,1)}) custom-call(bf16[32,272,256]{2,1,0:T(8,128)(2,1)} %all-to-all-done.got_ref.refs_0_), custom_call_target="tpu_custom_call" | custom-call | flops 2139095040 | bytes 7798784 | tf_op jit(solution)/shard_map/weight_first/pallas_call | solution.py:218
  92.4 0.0 reduce-scatter.8.cloned.1.call-start
  92.5 46.7 %all_to_all.20.refs_0_.got_ref = bf16[32,208,256]{2,1,0:T(8,128)(2,1)S(1)} all-to-all(bf16[32,208,256]{2,1,0:T(8,128)(2,1)} %copy-done.1), channel_id=1, replica_groups=mesh['grp'=4,'sp'=32] {'sp'}, dimensions={0} | all-to-all | bytes 6815744 | tf_op jit(solution)/shard_map/all_to_all | solution.py:445
  139.2 7.5 %weight_rest.3 = bf16[4,2,192,1536]{3,2,1,0:T(8,128)(2,1)} custom-call(bf16[2,768,544]{2,1,0:T(8,128)(2,1)} %get-tuple-element.34.acts_ref, bf16[32,208,256]{2,1,0:T(8,128)(2,1)S(1)} %all_to_all.20.refs_0_.got_ref), custom_call_target="tpu_custom_call" | custom-call | flops 2566914048 | bytes 9797632 | tf_op jit(solution)/shard_map/weight_rest/pallas_call | solution.py:239
  146.7 4.8 %all-to-all-start.1 = ((bf16[32,176,256]{2,1,0:T(8,128)(2,1)}), bf16[32,176,256]{2,1,0:T(8,128)(2,1)}, u32[]{:S(2)}, u32[]{:S(2)}) async-start(bf16[32,176,256]{2,1,0:T(8,128)(2,1)} %copy-done.4), calls=%async_computation.1 | async-start | bytes 5767168 | tf_op jit(solution)/shard_map/all_to_all | solution.py:445
  151.6 0.0 reduce-scatter.6.cloned.1.call-start
  151.7 0.1 dynamic-slice_subtract_fusion
  151.8 0.6 constant_dynamic-slice_fusion
  154.8 0.0 reduce-scatter.4.cloned.1.call-done
  154.9 2.8 broadcast_select_fusion.4
  157.7 1.8 collective-permute-start
  159.6 3.5 collective-permute-start.1
  163.0 1.0 collective-permute-start.2
  164.1 7.6 %project.3 = (f32[2,512,768]{2,1,0:T(8,128)S(1)}, f32[2,32,768]{2,1,0:T(8,128)S(1)}) custom-call(bf16[32,272,256]{2,1,0:T(8,128)(2,1)} %all-to-all-done.got_ref.refs_0_, bf16[2,768,4096]{2,1,0:T(8,128)(2,1)} %refs_1_.5), custom_call_target="tpu_custom_call" | custom-call | flops 2139095040 | bytes 15073280 | tf_op jit(solution)/shard_map/project/pallas_call | solution.py:324
  171.7 7.1 %project.4 = (f32[2,512,768]{2,1,0:T(8,128)S(1)}, f32[2,32,768]{2,1,0:T(8,128)S(1)}) custom-call(bf16[32,208,256]{2,1,0:T(8,128)(2,1)S(1)} %all_to_all.20.refs_0_.got_ref, bf16[2,768,4096]{2,1,0:T(8,128)(2,1)} %refs_1_.5, f32[2,512,768]{2,1,0:T(8,128)S(1)} %get-tuple-element.37.refs_2_, f32[2,32,768]{2,1,0:T(8,128)S(1)} %get-tuple-element.38.refs_3_), custom_call_target="tpu_custom_call" | custom-call | flops 2566914048 | bytes 14811136 | tf_op jit(solution)/shard_map/project/pallas_call | solution.py:324
  178.8 1.7 copy-done.2
  180.5 0.7 copy-done.14
  181.2 9.2 %all-to-all-done.1.got_ref.refs_0_ = bf16[32,176,256]{2,1,0:T(8,128)(2,1)} async-done(((bf16[32,176,256]{2,1,0:T(8,128)(2,1)}), bf16[32,176,256]{2,1,0:T(8,128)(2,1)}, u32[]{:S(2)}, u32[]{:S(2)}) %all-to-all-start.1) | async-done | bytes 2883616 | tf_op jit(solution)/shard_map/all_to_all | solution.py:445
  190.4 16.3 %collective-permute-done.1.refs_2_ = bf16[192,1280]{1,0:T(8,128)(2,1)} collective-permute-done((bf16[192,1280]{1,0:T(8,128)(2,1)}, bf16[192,1280]{1,0:T(8,128)(2,1)}, u32[]{:S(2)}, u32[]{:S(2)}) %collective-permute-start.1) | collective-permute-done | bytes 491552 | tf_op jit(solution)/shard_map/ppermute | solution.py:463
  206.7 7.9 %weight_rest.2 = bf16[4,2,192,1280]{3,2,1,0:T(8,128)(2,1)} custom-call(bf16[2,768,544]{2,1,0:T(8,128)(2,1)} %get-tuple-element.34.acts_ref, bf16[32,176,256]{2,1,0:T(8,128)(2,1)} %all-to-all-done.1.got_ref.refs_0_), custom_call_target="tpu_custom_call" | custom-call | flops 2139095040 | bytes 8486912 | tf_op jit(solution)/shard_map/weight_rest/pallas_call | solution.py:239
  214.7 1.9 copy-done.3
  216.6 8.9 %project.5 = bf16[32,104,256]{2,1,0:T(8,128)(2,1)} custom-call(bf16[32,176,256]{2,1,0:T(8,128)(2,1)} %all-to-all-done.1.got_ref.refs_0_, bf16[2,768,4096]{2,1,0:T(8,128)(2,1)} %refs_1_.5, f32[2,512,768]{2,1,0:T(8,128)S(1)} %copy-done.3, f32[2,32,768]{2,1,0:T(8,128)S(1)} %copy-done.15), custom_call_target="tpu_custom_call" | custom-call | flops 2139095040 | bytes 13500416 | tf_op jit(solution)/shard_map/project/pallas_call | solution.py:324
  225.5 2.6 broadcast_select_fusion
  228.1 7.3 %all-to-all-start.3 = ((bf16[32,104,256]{2,1,0:T(8,128)(2,1)}), bf16[32,104,256]{2,1,0:T(8,128)(2,1)S(1)}, u32[]{:S(2)}, u32[]{:S(2)}) async-start(bf16[32,104,256]{2,1,0:T(8,128)(2,1)} %project.5), calls=%async_computation.6 | async-start | bytes 3407872 | tf_op jit(solution)/shard_map/all_to_all | solution.py:445
  235.5 1.0 reshape.100.code_ref
  236.4 1.0 reshape.101.prob_ref
  237.4 2.3 collective-permute-start.7
  239.8 2.6 collective-permute-start.8
  242.4 18.5 %all-to-all-done.3.back_ref = bf16[32,104,256]{2,1,0:T(8,128)(2,1)S(1)} async-done(((bf16[32,104,256]{2,1,0:T(8,128)(2,1)}), bf16[32,104,256]{2,1,0:T(8,128)(2,1)S(1)}, u32[]{:S(2)}, u32[]{:S(2)}) %all-to-all-start.3) | async-done | bytes 1703968 | tf_op jit(solution)/shard_map/all_to_all | solution.py:445
  260.9 1.4 copy-done.7
  262.3 1.1 copy-done.12
  263.3 1.0 copy-done.13
  264.4 3.9 finish.1
  268.3 0.8 copy-done.10
  269.1 18.8 %reduce-scatter.6.cloned.1.call-done = bf16[384,1280]{1,0:T(8,128)(2,1)} async-done(((bf16[1536,1280]{1,0:T(8,128)(2,1)}), bf16[384,1280]{1,0:T(8,128)(2,1)}) %reduce-scatter.6.cloned.1.call-update) | async-done | bytes 983056 | tf_op jit(solution)/shard_map/reduce_scatter | solution.py:453
  287.9 2.5 select_bitcast_fusion
  290.4 2.8 collective-permute-start.3
  293.1 1.3 collective-permute-start.4
  294.5 1.8 collective-permute-start.5
  296.3 0.1 pad_add_fusion.sources_ref
  296.4 46.4 %place.3.refs_4_ = bf16[768,4096]{1,0:T(8,128)(2,1)} custom-call(s32[4]{0:T(128)S(1)} %pad_add_fusion.sources_ref, bf16[192,1280]{1,0:T(8,128)(2,1)S(1)} %copy-done.5, bf16[192,1280]{1,0:T(8,128)(2,1)} %collective-permute-done.refs_1_, bf16[192,1280]{1,0:T(8,128)(2,1)} %collective-permute-done.1.refs_2_, bf16[192,1280]{1,0:T(8,128)(2,1)} %collective-permute-done.2.refs_3_), custom_call_target="tpu_custom_call" | custom-call | bytes 3932160 | tf_op jit(solution)/shard_map/place/pallas_call | solution.py:400
  342.8 37.4 %place.4.refs_4_ = bf16[768,4096]{1,0:T(8,128)(2,1)} custom-call(s32[4]{0:T(128)S(1)} %pad_add_fusion.sources_ref, bf16[192,1536]{1,0:T(8,128)(2,1)S(1)} %get-tuple-element.51.refs_0_, bf16[192,1536]{1,0:T(8,128)(2,1)S(1)} %collective-permute-done.6.refs_1_, bf16[192,1536]{1,0:T(8,128)(2,1)} %collective-permute-done.7.refs_2_, ...), custom_call_target="tpu_custom_call", output_to_operand_aliasing={{}: (5, {})} | custom-call | bytes 4718592 | tf_op jit(solution)/shard_map/place/pallas_call | solution.py:400
  380.2 0.2 reduce
  380.4 0.1 reshape.98
  380.5 0.7 copy.32
  381.2 31.5 %place.5 = bf16[768,4096]{1,0:T(8,128)(2,1)} custom-call(s32[4]{0:T(128)S(1)} %pad_add_fusion.sources_ref, bf16[192,1280]{1,0:T(8,128)(2,1)S(1)} %get-tuple-element.74.refs_0_, bf16[192,1280]{1,0:T(8,128)(2,1)S(1)} %collective-permute-done.3.refs_1_, bf16[192,1280]{1,0:T(8,128)(2,1)} %collective-permute-done.4.refs_2_, ...), custom_call_target="tpu_custom_call", output_to_operand_aliasing={{}: (5, {})} | custom-call | bytes 3932160 | tf_op jit(solution)/shard_map/place/pallas_call | solution.py:400
  (35 shorter events, 0.1 us)
Async XLA Ops:
  10.6 1.4 copy-start.6
  12.0 1.2 copy-start.8
  17.8 2.1 copy-start
  19.9 7.7 %copy-start.9 = (bf16[128,4096]{1,0:T(8,128)(2,1)S(1)}, bf16[128,4096]{1,0:T(8,128)(2,1)}, u32[]{:S(2)}) copy-start(bf16[128,4096]{1,0:T(8,128)(2,1)} %grad_ref.3) | copy-start | bytes 3145732
  19.9 64.4 %all-to-all-start = ((bf16[32,272,256]{2,1,0:T(8,128)(2,1)}), bf16[32,272,256]{2,1,0:T(8,128)(2,1)}, u32[]{:S(2)}, u32[]{:S(2)}) async-start(bf16[32,272,256]{2,1,0:T(8,128)(2,1)} %copy-done), calls=%async_computation | async-start | bytes 8912896 | tf_op jit(solution)/shard_map/all_to_all | solution.py:445
  27.6 127.3 %reduce-scatter.4.cloned.1.call-start = ((), (), s32[]{:S(2)}) async-start(), calls=%async_computation.7 | async-start | bytes 4915200 | tf_op jit(solution)/shard_map/reduce_scatter | solution.py:453
  30.9 1.7 copy-start.1
  32.6 1.6 copy-start.4
  92.4 133.0 %reduce-scatter.8.cloned.1.call-start = ((), (), s32[]{:S(2)}) async-start(), calls=%async_computation.9 | async-start | bytes 5898240 | tf_op jit(solution)/shard_map/reduce_scatter | solution.py:453
  146.7 5.0 %copy-start.16 = (s32[4,32]{1,0:T(4,128)S(1)}, s32[4,32]{1,0:T(4,128)}, u32[]{:S(2)}) copy-start(s32[4,32]{1,0:T(4,128)} %param.10) | copy-start | bytes 1540
  146.7 43.7 %all-to-all-start.1 = ((bf16[32,176,256]{2,1,0:T(8,128)(2,1)}), bf16[32,176,256]{2,1,0:T(8,128)(2,1)}, u32[]{:S(2)}, u32[]{:S(2)}) async-start(bf16[32,176,256]{2,1,0:T(8,128)(2,1)} %copy-done.4), calls=%async_computation.1 | async-start | bytes 5767168 | tf_op jit(solution)/shard_map/all_to_all | solution.py:445
  151.6 136.3 %reduce-scatter.6.cloned.1.call-start = ((), (), s32[]{:S(2)}) async-start(), calls=%async_computation.8 | async-start | bytes 4915200 | tf_op jit(solution)/shard_map/reduce_scatter | solution.py:453
  157.7 32.7 %collective-permute-start = (bf16[192,1280]{1,0:T(8,128)(2,1)}, bf16[192,1280]{1,0:T(8,128)(2,1)}, u32[]{:S(2)}, u32[]{:S(2)}) collective-permute-start(bf16[192,1280]{1,0:T(8,128)(2,1)} %get-tuple-element.79), channel_id=1, source_target_pairs={{0,32},{32,64},{64,96},{96,0},{1,33},{33,65},{65,97},{97,1},{2,34}... | collective-permute-start | bytes 1474568 | tf_op jit(solution)/shard_map/ppermute | solution.py:463
  159.6 47.1 %collective-permute-start.1 = (bf16[192,1280]{1,0:T(8,128)(2,1)}, bf16[192,1280]{1,0:T(8,128)(2,1)}, u32[]{:S(2)}, u32[]{:S(2)}) collective-permute-start(bf16[192,1280]{1,0:T(8,128)(2,1)} %get-tuple-element.77), channel_id=1, source_target_pairs={{0,64},{32,96},{64,0},{96,32},{1,65},{33,97},{65,1},{97,33},{2,66}... | collective-permute-start | bytes 1474568 | tf_op jit(solution)/shard_map/ppermute | solution.py:463
  163.0 43.7 %collective-permute-start.2 = (bf16[192,1280]{1,0:T(8,128)(2,1)}, bf16[192,1280]{1,0:T(8,128)(2,1)}, u32[]{:S(2)}, u32[]{:S(2)}) collective-permute-start(bf16[192,1280]{1,0:T(8,128)(2,1)} %get-tuple-element.76), channel_id=1, source_target_pairs={{0,96},{32,0},{64,32},{96,64},{1,97},{33,1},{65,33},{97,65},{2,98}... | collective-permute-start | bytes 1474568 | tf_op jit(solution)/shard_map/ppermute | solution.py:463
  178.8 1.7 copy-start.2
  180.5 0.7 copy-start.14
  214.6 2.0 copy-start.3
  214.6 2.0 copy-start.15
  228.1 32.8 %all-to-all-start.3 = ((bf16[32,104,256]{2,1,0:T(8,128)(2,1)}), bf16[32,104,256]{2,1,0:T(8,128)(2,1)S(1)}, u32[]{:S(2)}, u32[]{:S(2)}) async-start(bf16[32,104,256]{2,1,0:T(8,128)(2,1)} %project.5), calls=%async_computation.6 | async-start | bytes 3407872 | tf_op jit(solution)/shard_map/all_to_all | solution.py:445
  237.4 58.9 %copy-start.5 = (bf16[192,1280]{1,0:T(8,128)(2,1)S(1)}, bf16[192,1280]{1,0:T(8,128)(2,1)}, u32[]{:S(2)}) copy-start(bf16[192,1280]{1,0:T(8,128)(2,1)} %get-tuple-element.55.refs_0_) | copy-start | bytes 1474564
  237.4 57.1 %collective-permute-start.6 = (bf16[192,1536]{1,0:T(8,128)(2,1)}, bf16[192,1536]{1,0:T(8,128)(2,1)S(1)}, u32[]{:S(2)}, u32[]{:S(2)}) collective-permute-start(bf16[192,1536]{1,0:T(8,128)(2,1)} %get-tuple-element.52), channel_id=1, source_target_pairs={{0,32},{32,64},{64,96},{96,0},{1,33},{33,65},{65,97},{97,1},{2,34}... | collective-permute-start | bytes 1769480 | tf_op jit(solution)/shard_map/ppermute | solution.py:463
  237.4 105.3 %collective-permute-start.7 = (bf16[192,1536]{1,0:T(8,128)(2,1)}, bf16[192,1536]{1,0:T(8,128)(2,1)}, u32[]{:S(2)}, u32[]{:S(2)}) collective-permute-start(bf16[192,1536]{1,0:T(8,128)(2,1)} %get-tuple-element.53), channel_id=1, source_target_pairs={{0,64},{32,96},{64,0},{96,32},{1,65},{33,97},{65,1},{97,33},{2,66}... | collective-permute-start | bytes 1769480 | tf_op jit(solution)/shard_map/ppermute | solution.py:463
  239.8 103.0 %collective-permute-start.8 = (bf16[192,1536]{1,0:T(8,128)(2,1)}, bf16[192,1536]{1,0:T(8,128)(2,1)}, u32[]{:S(2)}, u32[]{:S(2)}) collective-permute-start(bf16[192,1536]{1,0:T(8,128)(2,1)} %get-tuple-element.54), channel_id=1, source_target_pairs={{0,96},{32,0},{64,32},{96,64},{1,97},{33,1},{65,33},{97,65},{2,98}... | collective-permute-start | bytes 1769480 | tf_op jit(solution)/shard_map/ppermute | solution.py:463
  260.8 1.4 copy-start.7
  262.3 1.1 copy-start.12
  263.3 1.0 copy-start.13
  268.3 0.8 copy-start.10
  290.4 90.8 %collective-permute-start.3 = (bf16[192,1280]{1,0:T(8,128)(2,1)}, bf16[192,1280]{1,0:T(8,128)(2,1)S(1)}, u32[]{:S(2)}, u32[]{:S(2)}) collective-permute-start(bf16[192,1280]{1,0:T(8,128)(2,1)} %get-tuple-element.75), channel_id=1, source_target_pairs={{0,32},{32,64},{64,96},{96,0},{1,33},{33,65},{65,97},{97,1},{2,34}... | collective-permute-start | bytes 1474568 | tf_op jit(solution)/shard_map/ppermute | solution.py:463
  293.1 88.0 %collective-permute-start.4 = (bf16[192,1280]{1,0:T(8,128)(2,1)}, bf16[192,1280]{1,0:T(8,128)(2,1)}, u32[]{:S(2)}, u32[]{:S(2)}) collective-permute-start(bf16[192,1280]{1,0:T(8,128)(2,1)} %get-tuple-element.73), channel_id=1, source_target_pairs={{0,64},{32,96},{64,0},{96,32},{1,65},{33,97},{65,1},{97,33},{2,66}... | collective-permute-start | bytes 1474568 | tf_op jit(solution)/shard_map/ppermute | solution.py:463
  294.5 86.7 %collective-permute-start.5 = (bf16[192,1280]{1,0:T(8,128)(2,1)}, bf16[192,1280]{1,0:T(8,128)(2,1)}, u32[]{:S(2)}, u32[]{:S(2)}) collective-permute-start(bf16[192,1280]{1,0:T(8,128)(2,1)} %get-tuple-element.72), channel_id=1, source_target_pairs={{0,96},{32,0},{64,32},{96,64},{1,97},{33,1},{65,33},{97,65},{2,98}... | collective-permute-start | bytes 1474568 | tf_op jit(solution)/shard_map/ppermute | solution.py:463
  342.7 37.5 %copy-start.11 = (f32[1024,1]{1,0:T(8,128)S(1)}, f32[1024,1]{1,0:T(8,128)}, u32[]{:S(2)}) copy-start(f32[1024,1]{1,0:T(8,128)} %copy-done.10) | copy-start | bytes 12292
Sparse Core Ops, SparseCore 0:
  92.6 42.4 reduce-scatter.3
  146.8 71.4 reduce-scatter.7
  220.7 67.1 reduce-scatter.5

commit v2 on v1

--- a/solution.py
+++ b/solution.py
@@ -9,9 +9,11 @@
 
 V = 256
 MAIN = 32
+LANES = 128
 SHIFT = 6
 MASK = (1 << SHIFT) - 1
-CHUNKS = (5, 6, 5)
+CHUNKS = (4, 6, 6)
+DEFER = False
 BF16 = jnp.bfloat16
 F32 = jnp.float32
 MIB = 1024 * 1024
@@ -153,16 +155,18 @@
     )(codes, grad)
 
 
-def sorted_tail(got_ref):
+def load_tail(got_ref, tail_ref):
     sources, rows, _ = got_ref.shape
     n = rows // MAIN
-    tail = tail_size(n)
-    size = sources * tail
-    values = got_ref[:, n * MAIN :, :].astype(F32).reshape(size, V).astype(BF16)
-    i = lax.broadcasted_iota(jnp.int32, (size, size), 0)
-    j = lax.broadcasted_iota(jnp.int32, (size, size), 1)
-    order = (i % sources == j // tail) & (i // sources == j % tail)
-    return dot(jnp.where(order, 1.0, 0.0).astype(BF16), values).astype(BF16)
+    for h in range(V // LANES):
+        part = got_ref[:, n * MAIN :, h * LANES : (h + 1) * LANES].astype(F32)
+        tail_ref[h] = part.reshape(tail_ref.shape[1:])
+
+
+def tail_rows(tail_ref, sources, part, expert):
+    size = tail_ref.shape[1] // sources
+    rows = [tail_ref[h, pl.ds(2 * part + expert, sources, stride=size), :] for h in range(V // LANES)]
+    return jnp.concatenate(rows, axis=1).astype(BF16)
 
 
 def main_rows(got_ref, part, expert):
@@ -171,78 +175,88 @@
     return rows.reshape(got_ref.shape[0] * half, V)
 
 
-def weight_step(acts, rows, more, out_ref, expert):
+def weight_step(acts, rows, more, keep_ref, send_ref, expert):
     depth = rows.shape[0]
     total = dot(acts[:, :depth], rows) + dot(acts[:, depth:], more)
-    quarters, _, size, _ = out_ref.shape
-    for q in range(quarters):
-        out_ref[q, expert] = total[q * size : (q + 1) * size].astype(BF16)
-
-
-def weight_first_kernel(act_parts, got_ref, acts_ref, out_ref, tail_ref):
+    half = total.shape[0] // 2
+    keep_ref[expert] = total[:half].astype(BF16)
+    send_ref[...] = total[half:].astype(BF16)
+
+
+def weight_first_kernel(act_parts, order_ref, got_ref, acts_ref, keep_ref, low_ref, high_ref, tail_ref, plain_ref):
     sources = got_ref.shape[0]
     part = pl.program_id(0)
 
     @pl.when(part == 0)
     def _():
-        tail_ref[...] = sorted_tail(got_ref)
+        load_tail(got_ref, tail_ref)
+        quarters = order_ref.shape[1]
+        size = acts_ref.shape[1] // quarters
         for e in range(2):
             for p in range(act_parts):
                 block = main_rows(got_ref, p, e)
-                more = tail_ref[(2 * p + e) * sources : (2 * p + e + 1) * sources, :]
-                acts_ref[e, p * V : (p + 1) * V, : block.shape[0]] = block.astype(F32).T.astype(BF16)
-                acts_ref[e, p * V : (p + 1) * V, block.shape[0] :] = more.astype(F32).T.astype(BF16)
-
-    for e in range(2):
-        at = pl.multiple_of((2 * (act_parts + part) + e) * sources, sources)
-        more = tail_ref[pl.ds(at, sources), :]
-        weight_step(acts_ref[e], main_rows(got_ref, act_parts + part, e), more, out_ref, e)
-
-
-def weight_kernel(parts, acts_ref, got_ref, out_ref, tail_ref):
+                more = tail_rows(tail_ref, sources, p, e)
+                plain_ref[p * V : (p + 1) * V, : block.shape[0]] = block.astype(F32).T.astype(BF16)
+                plain_ref[p * V : (p + 1) * V, block.shape[0] :] = more.astype(F32).T.astype(BF16)
+            for q in range(quarters):
+                at = pl.multiple_of(order_ref[e, q] * size, size)
+                acts_ref[e, q * size : (q + 1) * size, :] = plain_ref[pl.ds(at, size), :]
+
+    for e, send_ref in enumerate((low_ref, high_ref)):
+        more = tail_rows(tail_ref, sources, act_parts + part, e)
+        weight_step(acts_ref[e], main_rows(got_ref, act_parts + part, e), more, keep_ref, send_ref, e)
+
+
+def weight_kernel(acts_ref, got_ref, keep_ref, low_ref, high_ref, tail_ref):
     sources = got_ref.shape[0]
     part = pl.program_id(0)
 
     @pl.when(part == 0)
     def _():
-        tail_ref[...] = sorted_tail(got_ref)
-
-    for e in range(2):
-        more = tail_ref[pl.ds(pl.multiple_of((2 * part + e) * sources, sources), sources), :]
-        weight_step(acts_ref[e], main_rows(got_ref, part, e), more, out_ref, e)
-
-
-def weight_first(got, hidden, parts, groups):
-    sources = got.shape[0]
-    depth = sources * (MAIN // 2 + 1)
+        load_tail(got_ref, tail_ref)
+
+    for e, send_ref in enumerate((low_ref, high_ref)):
+        more = tail_rows(tail_ref, sources, part, e)
+        weight_step(acts_ref[e], main_rows(got_ref, part, e), more, keep_ref, send_ref, e)
+
+
+def sum_specs(hidden, parts):
+    half = hidden // 2
+    specs = [pl.BlockSpec((2, half, V), lambda p: (0, 0, p))] + [pl.BlockSpec((half, V), lambda p: (0, p))] * 2
+    shapes = [pltpu.HBM((2, half, parts * V), BF16)] + [pltpu.HBM((half, parts * V), BF16)] * 2
+    return specs, shapes
+
+
+def tail_scratch(got):
+    return pltpu.VMEM((V // LANES, got.shape[0] * (got.shape[1] % MAIN), LANES), F32)
+
+
+def weight_first(order, got, hidden, parts):
+    depth = got.shape[0] * (MAIN // 2 + 1)
+    specs, shapes = sum_specs(hidden, parts)
     return pl.pallas_call(
         functools.partial(weight_first_kernel, hidden // V),
         grid=(parts,),
-        in_specs=[resident()],
-        out_specs=[
-            whole((2, hidden, depth)),
-            pl.BlockSpec((groups, 2, hidden // groups, V), lambda p: (0, 0, 0, p)),
-        ],
-        out_shape=[
-            pltpu.HBM((2, hidden, depth), BF16),
-            pltpu.HBM((groups, 2, hidden // groups, parts * V), BF16),
-        ],
-        scratch_shapes=[pltpu.VMEM((sources * (got.shape[1] % MAIN), V), BF16)],
+        in_specs=[pl.BlockSpec(memory_space=pltpu.SMEM), resident()],
+        out_specs=[whole((2, hidden, depth))] + specs,
+        out_shape=[pltpu.HBM((2, hidden, depth), BF16)] + shapes,
+        scratch_shapes=[tail_scratch(got), pltpu.VMEM((hidden, depth), BF16)],
         compiler_params=params(16),
         cost_estimate=cost(4 * depth * hidden * V * parts, 2 * (got.size + 4 * depth * hidden)),
         name="weight_first",
-    )(got)
-
-
-def weight_rest(acts, got, parts, groups):
+    )(order, got)
+
+
+def weight_rest(acts, got, parts):
     hidden, depth = acts.shape[1:]
-    return pl.pallas_call(
-        functools.partial(weight_kernel, parts),
+    specs, shapes = sum_specs(hidden, parts)
+    return pl.pallas_call(
+        weight_kernel,
         grid=(parts,),
         in_specs=[whole(acts.shape), resident()],
-        out_specs=pl.BlockSpec((groups, 2, hidden // groups, V), lambda p: (0, 0, 0, p)),
-        out_shape=pltpu.HBM((groups, 2, hidden // groups, parts * V), BF16),
-        scratch_shapes=[pltpu.VMEM((got.shape[0] * (got.shape[1] % MAIN), V), BF16)],
+        out_specs=specs,
+        out_shape=shapes,
+        scratch_shapes=[tail_scratch(got)],
         compiler_params=params(16),
         cost_estimate=cost(4 * depth * hidden * V * parts, 2 * (got.size + acts.size + 2 * hidden * V * parts)),
         name="weight_rest",
@@ -266,7 +280,7 @@
 
     @pl.when(part == 0)
     def _():
-        tail_ref[...] = sorted_tail(got_ref)
+        load_tail(got_ref, tail_ref)
         if chained:
             main_acc[...] = main_in[...]
             tail_acc[...] = tail_in[...]
@@ -278,7 +292,7 @@
         weight = weight_ref[e]
         rows = main_rows(got_ref, part + skip, e)
         main_acc[e] += dot(rows, weight, ((1,), (1,)))
-        more = tail_ref[pl.ds(pl.multiple_of((2 * (part + skip) + e) * sources, sources), sources), :]
+        more = tail_rows(tail_ref, sources, part + skip, e)
         tail_acc[e] += dot(more, weight, ((1,), (1,)))
 
     if final:
@@ -313,7 +327,7 @@
     if state is not None:
         in_specs += [resident(), resident()]
         args += list(state)
-    scratch = [pltpu.VMEM((sources * (got.shape[1] % MAIN), V), BF16)]
+    scratch = [pltpu.VMEM((V // LANES, sources * (got.shape[1] % MAIN), LANES), F32)]
     if final:
         shape = (sources, block_rows(hidden // V), V)
         out_specs, out_shape = resident(), jax.ShapeDtypeStruct(shape, BF16)
@@ -378,7 +392,7 @@
     )(code, prob, act, back)
 
 
-def place_kernel(column, first, sources_ref, *refs):
+def place_kernel(column, sources_ref, *refs):
     blocks, (out_ref, sems) = refs[:4], refs[-2:]
     copies = []
     for d, block in enumerate(blocks):
@@ -396,12 +410,12 @@
 def place(sources, blocks, own, hidden, width, column):
     first = own is None
     args = [sources, *blocks] + ([] if first else [own])
-    anywhere = pl.BlockSpec(memory_space=pl.ANY)
-    return pl.pallas_call(
-        functools.partial(place_kernel, column, first),
-        in_specs=[pl.BlockSpec(memory_space=pltpu.SMEM)] + [anywhere] * (len(args) - 1),
-        out_specs=anywhere,
-        out_shape=jax.ShapeDtypeStruct((hidden, width), BF16),
+    own_spec = pl.BlockSpec(memory_space=pltpu.HBM)
+    return pl.pallas_call(
+        functools.partial(place_kernel, column),
+        in_specs=[pl.BlockSpec(memory_space=pltpu.SMEM)] + [resident()] * len(blocks) + [own_spec] * (not first),
+        out_specs=own_spec,
+        out_shape=pltpu.HBM((hidden, width), BF16),
         scratch_shapes=[pltpu.SemaphoreType.DMA((len(blocks),))],
         input_output_aliases={} if first else {len(args) - 1: 0},
         compiler_params=params(4),
@@ -447,10 +461,27 @@
     held = lax.dynamic_index_in_dim(placement, my_column, 1, keepdims=False) - 2 * my_column
     hops = [[(i, (i + d) % groups) for i in range(groups)] for d in range(groups)]
 
-    def reduced(part):
-        size = part.shape[-1]
-        flat_part = part.reshape(groups * 2 * quarter, size)
-        return lax.psum_scatter(flat_part, "grp", scatter_dimension=0, tiled=True).reshape(2, quarter, size)
+    near = [(0, 1), (1, 0), (2, 3), (3, 2)]
+    far = [(0, 3), (3, 0), (1, 2), (2, 1)]
+    g = my_group.astype(jnp.int32)
+    order = jnp.stack(
+        [jnp.stack([g, 3 - g, g ^ 1, 3 - (g ^ 1)]), jnp.stack([g, g ^ 1, 3 - g, 3 - (g ^ 1)])]
+    )
+
+    def first_round(low, high):
+        return lax.ppermute(low, "grp", near), lax.ppermute(high, "grp", far)
+
+    def forwarded(keep, came):
+        return [(keep[e, quarter:].astype(F32) + came[e][quarter:].astype(F32)).astype(BF16) for e in range(2)]
+
+    def second_round(low, high):
+        return lax.ppermute(low, "grp", far), lax.ppermute(high, "grp", near)
+
+    def completed(keep, came, last_came):
+        return [
+            (keep[e, :quarter].astype(F32) + came[e][:quarter].astype(F32) + last_came[e].astype(F32)).astype(BF16)
+            for e in range(2)
+        ]
 
     def wanted(mine):
         out = []
@@ -472,30 +503,42 @@
     outs = dict(enumerate(outs, 1))
 
     starts = [sum(CHUNKS[:c]) for c in range(last + 1)]
-    mine, sends = {}, {}
+    sends, blocks = {}, {}
     state = None
-    acts, part = weight_first(got[0], hidden, CHUNKS[0], groups)
+    barrier = lax.optimization_barrier
     for c in range(last + 1):
-        if c:
+        if c == 0:
+            acts, keep, low, high = weight_first(order, got[0], hidden, CHUNKS[0])
+        else:
+            got[c], sends[c - 1] = barrier((got[c], sends[c - 1]))
             if c == last:
-                sends[c - 2] = wanted(mine[c - 2])
-                got[c], state, blocks = lax.optimization_barrier((got[c], state, moved(sends[c - 2])))
-            part = weight_rest(acts, got[c], CHUNKS[c], groups)
-        mine[c] = reduced(part)
+                got[c], state = barrier((got[c], state))
+            keep, low, high = weight_rest(acts, got[c], CHUNKS[c])
         if c < last:
+            outs[c + 1], low, high = barrier((outs[c + 1], low, high))
             got[c + 1] = exchange(outs[c + 1])
             skip = act_parts if c == 0 else 0
             state = project(got[c], down_weight, starts[c], skip, CHUNKS[c], state, False)
-    proj = project(got[last], down_weight, starts[last], 0, CHUNKS[last], state, True)
-    proj, sends[last - 1] = tie(proj, wanted(mine[last - 1]))
-    back = exchange(proj)
-    grad_act, grad_prob = finish(codes.reshape(tok * top, 1), prob.reshape(tok * top, 1), act, back)
-    mine[last], grad_act, grad_prob = lax.optimization_barrier((mine[last], grad_act, grad_prob))
+        came = first_round(low, high)
+        if c == last:
+            proj = project(got[last], down_weight, starts[last], 0, CHUNKS[last], state, True)
+            back = exchange(proj)
+            grad_act, grad_prob = finish(codes.reshape(tok * top, 1), prob.reshape(tok * top, 1), act, back)
+        if c >= 2:
+            came, blocks[c - 2] = barrier((came, blocks[c - 2]))
+        passed = forwarded(keep, came)
+        if c >= 1:
+            if DEFER:
+                passed, sends[c - 1] = barrier((passed, sends[c - 1]))
+            blocks[c - 1] = moved(sends[c - 1])
+        last_came = second_round(*passed)
+        if c == last:
+            last_came, grad_act, grad_prob = barrier((last_came, grad_act, grad_prob))
+        sends[c] = wanted(completed(keep, came, last_came))
+    blocks[last] = moved(sends[last])
     own = None
     for c in range(last + 1):
-        if c not in sends:
-            sends[c] = wanted(mine[c])
-        own = place(sources, moved(sends[c]) if c else blocks, own, hidden, width, starts[c] * V)
+        own = place(sources, blocks[c], own, hidden, width, starts[c] * V)
     return (
         grad_act.reshape(tok, top, hidden),
         grad_prob.reshape(tok, top),

time: 420 us -> 316 us (0.75)
  Pallas kernels: 174 us -> 64.1 us
  blocking collectives: 46.7 us -> 0 us
  waiting for transfers between devices: 113 us -> 146 us
  starting transfers between devices: 37.2 us -> 54 us
  between operations: 16.5 us -> 3.6 us
  other arithmetic: 10.5 us -> 23 us
    pallas_call x5, Pallas kernels: 131 us -> 22.3 us  [the longest x2 15.3 us: weight_rest(): pl.pallas_call(weight_kernel, grid=(parts,), in_specs=[whole(acts.shape),...]
    ppermute x0 -> x12, waiting for transfers between devices: none -> 54.5 us  [the longest x6 37.4 us: first_round(): return (lax.ppermute(low, 'grp', near), lax.ppermute(high, 'grp', far))]
    all_to_all x1 -> x0, blocking collectives: 46.7 us -> none  [exchange(): return lax.all_to_all(v, 'sp', 0, 0, tiled=True)]
    all_to_all x3 -> x4, waiting for transfers between devices: 77.9 us -> 48.7 us  [exchange(): return lax.all_to_all(v, 'sp', 0, 0, tiled=True)]
    ppermute x9, waiting for transfers between devices: 16.3 us -> 42.3 us  [moved(): lax.ppermute(sends[d], 'grp', hops[d])]
    reduce_scatter x3 -> x0, waiting for transfers between devices: 18.8 us -> none  [reduced(): lax.psum_scatter(flat_part, 'grp', scatter_dimension=0, tiled=True)]
    ppermute x0 -> x12, starting transfers between devices: none -> 16.8 us  [the longest x6 10.6 us: first_round(): return (lax.ppermute(low, 'grp', near), lax.ppermute(high, 'grp', far))]
    convert_element_type x0 -> x3, other arithmetic: none -> 7.77 us  [forwarded(): (keep[e, quarter:].astype(F32) + came[e][quarter:].astype(F32)).astype(BF16)]
  transfers between devices with their start and end apart: 15 -> 25, of which waited for: 5 -> 13; matrix products, arithmetic and copies ran while one was open for 3% -> 8% of each run, Pallas kernels for 31% -> 11%
where the time goes in v2:
time: 316 us; the launch traced here: 311 us
  waiting for transfers between devices  146 us (46%)
  Pallas kernels  64.1 us (20%)
  starting transfers between devices  54 us (17%)
  other arithmetic  23 us (7%)
  local copies, waits for them, and re-layouts  21.1 us (7%)
  between operations  3.6 us (1%)
    all_to_all x4, waiting for transfers between devices, exchange(): return lax.all_to_all(v, 'sp', 0, 0, tiled=True)  48.7 us
    ppermute x9, waiting for transfers between devices, moved(): lax.ppermute(sends[d], 'grp', hops[d])  42.3 us
    ppermute x6, waiting for transfers between devices, first_round(): return (lax.ppermute(low, 'grp', near), lax.ppermute(high, 'grp', far))  37.4 us
    pallas_call x3, Pallas kernels, project(): pl.pallas_call(functools.partial(project_kernel, skip, parts, state is no...  23.1 us
    all_to_all x4, starting transfers between devices, exchange(): return lax.all_to_all(v, 'sp', 0, 0, tiled=True)  20.8 us
    ppermute x6, waiting for transfers between devices, second_round(): return (lax.ppermute(low, 'grp', far), lax.ppermute(high, 'grp', near))  17.1 us
    unnamed x57, local copies, waits for them, and re-layouts  16.5 us
    ppermute x9, starting transfers between devices, moved(): lax.ppermute(sends[d], 'grp', hops[d])  16.4 us
  transfers between devices with their start and end apart: 25, of which 13 were waited for; matrix products, arithmetic and copies ran while one was open for 8% of the time, Pallas kernels for 11%

profile of v2, /device:TPU:0, one launch (start us, length us, event | category | flops | bytes accessed | tf_op | source)
XLA Modules:
  0.0 311.4 jit_solution(8445947644390305032)
XLA Ops:
  4.6 1.4 copy-done.6
  6.0 1.2 copy-done.8
  7.2 4.4 %send_first.1 = bf16[32,240,256]{2,1,0:T(8,128)(2,1)S(1)} custom-call(s32[8,128]{1,0:T(8,128)S(1)} %bitcast.65, s32[1,1024]{1,0:T(1,128)S(1)} %reshape.82.flat_ref, f32[1,1024]{1,0:T(1,128)S(1)} %reshape.83.prob_ref, bf16[1024,768]{1,0:T(8,128)(2,1)S(1)} %bitcast.63, bf16[128,4096]{1,0:T(8,128)(2,1)S(1)} %copy-done.8), custom_call_target="tpu_custom_call" | custom-call | flops 1610612736 | bytes 5505024 | tf_op jit(solution)/shard_map/send_first/pallas_call | solution.py:125
  11.6 1.9 copy-done
  13.5 7.6 %all-to-all-start = ((bf16[32,240,256]{2,1,0:T(8,128)(2,1)}), bf16[32,240,256]{2,1,0:T(8,128)(2,1)}, u32[]{:S(2)}, u32[]{:S(2)}) async-start(bf16[32,240,256]{2,1,0:T(8,128)(2,1)} %copy-done), calls=%async_computation | async-start | bytes 7864320 | tf_op jit(solution)/shard_map/all_to_all | solution.py:459
  21.2 3.4 %send_rest.1 = (bf16[32,208,256]{2,1,0:T(8,128)(2,1)S(1)}, bf16[32,208,256]{2,1,0:T(8,128)(2,1)S(1)}) custom-call(s32[8,128]{1,0:T(8,128)S(1)} %bitcast.66, bf16[128,4096]{1,0:T(8,128)(2,1)S(1)} %copy-done.9), custom_call_target="tpu_custom_call" | custom-call | flops 1073741824 | bytes 9961472 | tf_op jit(solution)/shard_map/send_rest/pallas_call | solution.py:146
  24.6 1.7 copy-done.1
  26.3 1.8 copy-done.2
  28.2 43.6 %all-to-all-done.got_ref.refs_0_ = bf16[32,240,256]{2,1,0:T(8,128)(2,1)} async-done(((bf16[32,240,256]{2,1,0:T(8,128)(2,1)}), bf16[32,240,256]{2,1,0:T(8,128)(2,1)}, u32[]{:S(2)}, u32[]{:S(2)}) %all-to-all-start) | async-done | bytes 3932192 | tf_op jit(solution)/shard_map/all_to_all | solution.py:459
  71.8 6.9 %weight_first.1 = (bf16[2,768,544]{2,1,0:T(8,128)(2,1)}, bf16[2,384,1024]{2,1,0:T(8,128)(2,1)}, bf16[384,1024]{1,0:T(8,128)(2,1)}, bf16[384,1024]{1,0:T(8,128)(2,1)}) custom-call(s32[2,4]{1,0:T(2,128)S(1)} %pad_add_fusion.order_ref, bf16[32,240,256]{2,1,0:T(8,128)(2,1)} %all-to-all-done.got_ref.refs_0_), custom_call_target="tpu_custom_call" | custom-call | flops 1711276032 | bytes 7274496 | tf_op jit(solution)/shard_map/weight_first/pallas_call | solution.py:237
  78.7 4.1 %all-to-all-start.1 = ((bf16[32,208,256]{2,1,0:T(8,128)(2,1)}), bf16[32,208,256]{2,1,0:T(8,128)(2,1)S(1)}, u32[]{:S(2)}, u32[]{:S(2)}) async-start(bf16[32,208,256]{2,1,0:T(8,128)(2,1)} %copy-done.2), calls=%async_computation.1 | async-start | bytes 6815744 | tf_op jit(solution)/shard_map/all_to_all | solution.py:459
  82.8 2.0 collective-permute-start
  84.8 2.5 collective-permute-start.2
  87.3 15.6 %collective-permute-done = bf16[384,1024]{1,0:T(8,128)(2,1)S(1)} collective-permute-done((bf16[384,1024]{1,0:T(8,128)(2,1)}, bf16[384,1024]{1,0:T(8,128)(2,1)S(1)}, u32[]{:S(2)}, u32[]{:S(2)}) %collective-permute-start) | collective-permute-done | bytes 786464 | tf_op jit(solution)/shard_map/ppermute | solution.py:472
  102.8 2.7 collective-permute-done.2
  105.5 2.6 fusion.15
  108.1 2.5 collective-permute-start.1
  113.8 5.9 %collective-permute-done.1 = bf16[192,1024]{1,0:T(8,128)(2,1)} collective-permute-done((bf16[192,1024]{1,0:T(8,128)(2,1)}, bf16[192,1024]{1,0:T(8,128)(2,1)}, u32[]{:S(2)}, u32[]{:S(2)}) %collective-permute-start.1) | collective-permute-done | bytes 393248 | tf_op jit(solution)/shard_map/ppermute | solution.py:478
  119.7 1.0 collective-permute-done.3
  120.7 2.8 broadcast_select_fusion.8
  123.5 1.1 broadcast_select_fusion.9
  124.6 2.9 all-to-all-done.1.got_ref.refs_0_
  127.5 7.0 %weight_rest.2 = (bf16[2,384,1536]{2,1,0:T(8,128)(2,1)}, bf16[384,1536]{1,0:T(8,128)(2,1)}, bf16[384,1536]{1,0:T(8,128)(2,1)}) custom-call(bf16[2,768,544]{2,1,0:T(8,128)(2,1)} %get-tuple-element.56.acts_ref, bf16[32,208,256]{2,1,0:T(8,128)(2,1)S(1)} %all-to-all-done.1.got_ref.refs_0_), custom_call_target="tpu_custom_call" | custom-call | flops 2566914048 | bytes 9797632 | tf_op jit(solution)/shard_map/weight_rest/pallas_call | solution.py:253
  134.5 1.9 collective-permute-start.4
  136.5 2.5 collective-permute-start.6
  139.0 4.8 %all-to-all-start.2 = ((bf16[32,208,256]{2,1,0:T(8,128)(2,1)}), bf16[32,208,256]{2,1,0:T(8,128)(2,1)}, u32[]{:S(2)}, u32[]{:S(2)}) async-start(bf16[32,208,256]{2,1,0:T(8,128)(2,1)} %copy-done.1), calls=%async_computation.2 | async-start | bytes 6815744 | tf_op jit(solution)/shard_map/all_to_all | solution.py:459
  143.8 16.5 %collective-permute-done.4 = bf16[384,1536]{1,0:T(8,128)(2,1)} collective-permute-done((bf16[384,1536]{1,0:T(8,128)(2,1)}, bf16[384,1536]{1,0:T(8,128)(2,1)}, u32[]{:S(2)}, u32[]{:S(2)}) %collective-permute-start.4) | collective-permute-done | bytes 1179680 | tf_op jit(solution)/shard_map/ppermute | solution.py:472
  160.3 2.7 collective-permute-done.6
  163.0 1.9 fusion.9
  164.8 2.6 collective-permute-start.5
  167.4 6.3 %project.3 = (f32[2,512,768]{2,1,0:T(8,128)S(1)}, f32[2,32,768]{2,1,0:T(8,128)S(1)}) custom-call(bf16[32,240,256]{2,1,0:T(8,128)(2,1)} %all-to-all-done.got_ref.refs_0_, bf16[2,768,4096]{2,1,0:T(8,128)(2,1)} %refs_1_.5), custom_call_target="tpu_custom_call" | custom-call | flops 1711276032 | bytes 13762560 | tf_op jit(solution)/shard_map/project/pallas_call | solution.py:338
  173.7 7.2 %project.4 = (f32[2,512,768]{2,1,0:T(8,128)S(1)}, f32[2,32,768]{2,1,0:T(8,128)S(1)}) custom-call(bf16[32,208,256]{2,1,0:T(8,128)(2,1)S(1)} %all-to-all-done.1.got_ref.refs_0_, bf16[2,768,4096]{2,1,0:T(8,128)(2,1)} %refs_1_.5, f32[2,512,768]{2,1,0:T(8,128)S(1)} %get-tuple-element.73.refs_2_, f32[2,32,768]{2,1,0:T(8,128)S(1)} %get-tuple-element.74.refs_3_), custom_call_target="tpu_custom_call" | custom-call | flops 2566914048 | bytes 14811136 | tf_op jit(solution)/shard_map/project/pallas_call | solution.py:338
  181.6 3.5 %broadcast_select_fusion.1 = (bf16[192,1536]{1,0:T(8,128)(2,1)}, bf16[192,1536]{1,0:T(8,128)(2,1)S(1)}, bf16[192,1536]{1,0:T(8,128)(2,1)S(1)}) fusion(pred[]{:T(512)} %bitcast.15, bf16[192,1536]{1,0:T(8,128)(2,1)S(1)} %collective-permute-done.7, bf16[384,1536]{1,0:T(8,128)(2,1)} %collective-permute-done.6, bf16[2,384,1536]{2,1,0:T(8,128)(2,1)S(1)} %copy-done.23, ...), kind=kLoop, calls=%fused_computation.31 | loop fusion | flops 3833856 | bytes 5308417 | tf_op jit(solution)/shard_map/jit(_where)/select_n | solution.py:490
  185.2 1.1 broadcast_select_fusion.3
  186.3 2.3 all-to-all-done.2.got_ref.refs_0_
  188.6 8.3 %weight_rest.3 = (bf16[2,384,1536]{2,1,0:T(8,128)(2,1)}, bf16[384,1536]{1,0:T(8,128)(2,1)}, bf16[384,1536]{1,0:T(8,128)(2,1)}) custom-call(bf16[2,768,544]{2,1,0:T(8,128)(2,1)} %get-tuple-element.56.acts_ref, bf16[32,208,256]{2,1,0:T(8,128)(2,1)} %all-to-all-done.2.got_ref.refs_0_), custom_call_target="tpu_custom_call" | custom-call | flops 2566914048 | bytes 9797632 | tf_op jit(solution)/shard_map/weight_rest/pallas_call | solution.py:253
  196.9 1.0 collective-permute-start.8
  198.5 9.6 %project.5 = bf16[32,104,256]{2,1,0:T(8,128)(2,1)} custom-call(bf16[32,208,256]{2,1,0:T(8,128)(2,1)} %all-to-all-done.2.got_ref.refs_0_, bf16[2,768,4096]{2,1,0:T(8,128)(2,1)} %refs_1_.5, f32[2,512,768]{2,1,0:T(8,128)S(1)} %copy-done.4, f32[2,32,768]{2,1,0:T(8,128)S(1)} %copy-done.21), custom_call_target="tpu_custom_call" | custom-call | flops 2566914048 | bytes 14811136 | tf_op jit(solution)/shard_map/project/pallas_call | solution.py:338
  208.2 4.3 %all-to-all-start.3 = ((bf16[32,104,256]{2,1,0:T(8,128)(2,1)}), bf16[32,104,256]{2,1,0:T(8,128)(2,1)S(1)}, u32[]{:S(2)}, u32[]{:S(2)}) async-start(bf16[32,104,256]{2,1,0:T(8,128)(2,1)} %project.5), calls=%async_computation.3 | async-start | bytes 3407872 | tf_op jit(solution)/shard_map/all_to_all | solution.py:459
  212.7 3.7 %collective-permute-start.11 = (bf16[192,1024]{1,0:T(8,128)(2,1)}, bf16[192,1024]{1,0:T(8,128)(2,1)S(1)}, u32[]{:S(2)}, u32[]{:S(2)}) collective-permute-start(bf16[192,1024]{1,0:T(8,128)(2,1)} %get-tuple-element.83), channel_id=1, source_target_pairs={{0,64},{32,96},{64,0},{96,32},{1,65},{33,97},{65,1},{97,33},{2,66}... | collective-permute-start | bytes 1179656 | tf_op jit(solution)/shard_map/ppermute | solution.py:494
  217.3 23.8 %collective-permute-done.10.refs_1_ = bf16[192,1024]{1,0:T(8,128)(2,1)S(1)} collective-permute-done((bf16[192,1024]{1,0:T(8,128)(2,1)}, bf16[192,1024]{1,0:T(8,128)(2,1)S(1)}, u32[]{:S(2)}, u32[]{:S(2)}) %collective-permute-start.10) | collective-permute-done | bytes 393248 | tf_op jit(solution)/shard_map/ppermute | solution.py:494
  241.2 3.3 %fusion.4 = (bf16[192,1536]{1,0:T(8,128)(2,1)}, bf16[192,1536]{1,0:T(8,128)(2,1)}) fusion(bf16[384,1536]{1,0:T(8,128)(2,1)} %collective-permute-done.9, bf16[2,384,1536]{2,1,0:T(8,128)(2,1)} %get-tuple-element.78, bf16[384,1536]{1,0:T(8,128)(2,1)} %collective-permute-done.8), kind=kLoop, calls=%fused_computation.7 | loop fusion | flops 2359296 | bytes 3538944 | tf_op jit(solution)/shard_map/convert_element_type | solution.py:475
  244.6 1.0 collective-permute-start.13
  245.6 1.8 reshape.103.prob_ref
  248.4 1.0 collective-permute-start.18
  249.4 2.8 collective-permute-start.19
  252.2 1.9 collective-permute-start.20
  254.1 1.4 copy-done.7
  255.5 1.0 copy-done.12
  256.5 1.0 copy-done.13
  257.6 3.9 %finish.1 = (bf16[1024,768]{1,0:T(8,128)(2,1)}, f32[1024,1]{1,0:T(8,128)S(1)}) custom-call(s32[1024,1]{1,0:T(8,128)S(1)} %copy-done.13, f32[1024,1]{1,0:T(8,128)S(1)} %copy-done.12, bf16[1024,768]{1,0:T(8,128)(2,1)S(1)} %bitcast.64, bf16[32,104,256]{2,1,0:T(8,128)(2,1)S(1)} %all-to-all-done.3.back_ref), custom_call_target="tpu_custom_call" | custom-call | flops 1610612736 | bytes 4849664 | tf_op jit(solution)/shard_map/finish/pallas_call | solution.py:383
  261.5 10.3 %collective-permute-done.13 = bf16[192,1536]{1,0:T(8,128)(2,1)} collective-permute-done((bf16[192,1536]{1,0:T(8,128)(2,1)}, bf16[192,1536]{1,0:T(8,128)(2,1)}, u32[]{:S(2)}, u32[]{:S(2)}) %collective-permute-start.13) | collective-permute-done | bytes 589856 | tf_op jit(solution)/shard_map/ppermute | solution.py:478
  271.8 2.9 broadcast_select_fusion
  274.7 4.2 %collective-permute-start.17 = (bf16[192,1536]{1,0:T(8,128)(2,1)}, bf16[192,1536]{1,0:T(8,128)(2,1)S(1)}, u32[]{:S(2)}, u32[]{:S(2)}) collective-permute-start(bf16[192,1536]{1,0:T(8,128)(2,1)} %get-tuple-element.112), channel_id=1, source_target_pairs={{0,96},{32,0},{64,32},{96,64},{1,97},{33,1},{65,33},{97,65},{2,98}... | collective-permute-start | bytes 1769480 | tf_op jit(solution)/shard_map/ppermute | solution.py:494
  278.9 1.1 broadcast_select_fusion.2
  280.0 1.6 collective-permute-start.16
  281.7 15.5 %collective-permute-done.18.refs_1_ = bf16[192,1536]{1,0:T(8,128)(2,1)S(1)} collective-permute-done((bf16[192,1536]{1,0:T(8,128)(2,1)}, bf16[192,1536]{1,0:T(8,128)(2,1)S(1)}, u32[]{:S(2)}, u32[]{:S(2)}) %collective-permute-start.18) | collective-permute-done | bytes 589856 | tf_op jit(solution)/shard_map/ppermute | solution.py:494
  297.2 1.0 copy-done.15
  298.2 1.0 copy-done.17
  299.2 1.0 copy-done.19
  300.2 1.7 place.3.refs_4_
  302.0 2.6 place.4.refs_4_
  305.5 3.0 collective-permute-done.15.refs_1_
  308.5 2.7 place.5
  (81 shorter events, 9.3 us)
Async XLA Ops:
  3.9 0.6 copy-start.26
  4.6 1.4 copy-start.6
  6.0 1.2 copy-start.8
  11.6 1.9 copy-start
  13.5 7.7 %copy-start.9 = (bf16[128,4096]{1,0:T(8,128)(2,1)S(1)}, bf16[128,4096]{1,0:T(8,128)(2,1)}, u32[]{:S(2)}) copy-start(bf16[128,4096]{1,0:T(8,128)(2,1)} %grad_ref.3) | copy-start | bytes 3145732
  13.5 58.3 %all-to-all-start = ((bf16[32,240,256]{2,1,0:T(8,128)(2,1)}), bf16[32,240,256]{2,1,0:T(8,128)(2,1)}, u32[]{:S(2)}, u32[]{:S(2)}) async-start(bf16[32,240,256]{2,1,0:T(8,128)(2,1)} %copy-done), calls=%async_computation | async-start | bytes 7864320 | tf_op jit(solution)/shard_map/all_to_all | solution.py:459
  24.6 1.7 copy-start.1
  26.3 1.8 copy-start.2
  78.7 48.8 %all-to-all-start.1 = ((bf16[32,208,256]{2,1,0:T(8,128)(2,1)}), bf16[32,208,256]{2,1,0:T(8,128)(2,1)S(1)}, u32[]{:S(2)}, u32[]{:S(2)}) async-start(bf16[32,208,256]{2,1,0:T(8,128)(2,1)} %copy-done.2), calls=%async_computation.1 | async-start | bytes 6815744 | tf_op jit(solution)/shard_map/all_to_all | solution.py:459
  82.8 20.1 %collective-permute-start = (bf16[384,1024]{1,0:T(8,128)(2,1)}, bf16[384,1024]{1,0:T(8,128)(2,1)S(1)}, u32[]{:S(2)}, u32[]{:S(2)}) collective-permute-start(bf16[384,1024]{1,0:T(8,128)(2,1)} %get-tuple-element.63), channel_id=1, source_target_pairs={{0,32},{32,0},{64,96},{96,64},{1,33},{33,1},{65,97},{97,65},{2,34}... | collective-permute-start | bytes 2359304 | tf_op jit(solution)/shard_map/ppermute | solution.py:472
  84.8 20.7 %collective-permute-start.2 = (bf16[384,1024]{1,0:T(8,128)(2,1)}, bf16[384,1024]{1,0:T(8,128)(2,1)S(1)}, u32[]{:S(2)}, u32[]{:S(2)}) collective-permute-start(bf16[384,1024]{1,0:T(8,128)(2,1)} %get-tuple-element.64), channel_id=1, source_target_pairs={{0,96},{96,0},{32,64},{64,32},{1,97},{97,1},{33,65},{65,33},{2,98}... | collective-permute-start | bytes 2359304 | tf_op jit(solution)/shard_map/ppermute | solution.py:472
  102.8 5.3 %copy-start.24 = (bf16[384,1024]{1,0:T(8,128)(2,1)}, bf16[384,1024]{1,0:T(8,128)(2,1)S(1)}, u32[]{:S(2)}) copy-start(bf16[384,1024]{1,0:T(8,128)(2,1)S(1)} %collective-permute-done) | copy-start | bytes 2359300
  105.5 2.6 copy-start.25
  105.5 5.1 %copy-start.27 = (s32[4,32]{1,0:T(4,128)S(1)}, s32[4,32]{1,0:T(4,128)}, u32[]{:S(2)}) copy-start(s32[4,32]{1,0:T(4,128)} %param.10) | copy-start | bytes 1540
  108.1 11.6 %collective-permute-start.1 = (bf16[192,1024]{1,0:T(8,128)(2,1)}, bf16[192,1024]{1,0:T(8,128)(2,1)}, u32[]{:S(2)}, u32[]{:S(2)}) collective-permute-start(bf16[192,1024]{1,0:T(8,128)(2,1)} %get-tuple-element.125), channel_id=1, source_target_pairs={{0,96},{96,0},{32,64},{64,32},{1,97},{97,1},{33,65},{65,33},{2,98}... | collective-permute-start | bytes 1179656 | tf_op jit(solution)/shard_map/ppermute | solution.py:478
  110.7 10.1 %collective-permute-start.3 = (bf16[192,1024]{1,0:T(8,128)(2,1)}, bf16[192,1024]{1,0:T(8,128)(2,1)}, u32[]{:S(2)}, u32[]{:S(2)}) collective-permute-start(bf16[192,1024]{1,0:T(8,128)(2,1)} %get-tuple-element.126), channel_id=1, source_target_pairs={{0,32},{32,0},{64,96},{96,64},{1,33},{33,1},{65,97},{97,65},{2,34}... | collective-permute-start | bytes 1179656 | tf_op jit(solution)/shard_map/ppermute | solution.py:478
  134.5 25.7 %collective-permute-start.4 = (bf16[384,1536]{1,0:T(8,128)(2,1)}, bf16[384,1536]{1,0:T(8,128)(2,1)}, u32[]{:S(2)}, u32[]{:S(2)}) collective-permute-start(bf16[384,1536]{1,0:T(8,128)(2,1)} %get-tuple-element.70), channel_id=1, source_target_pairs={{0,32},{32,0},{64,96},{96,64},{1,33},{33,1},{65,97},{97,65},{2,34}... | collective-permute-start | bytes 3538952 | tf_op jit(solution)/shard_map/ppermute | solution.py:472
  136.5 26.5 %collective-permute-start.6 = (bf16[384,1536]{1,0:T(8,128)(2,1)}, bf16[384,1536]{1,0:T(8,128)(2,1)}, u32[]{:S(2)}, u32[]{:S(2)}) collective-permute-start(bf16[384,1536]{1,0:T(8,128)(2,1)} %get-tuple-element.71), channel_id=1, source_target_pairs={{0,96},{96,0},{32,64},{64,32},{1,97},{97,1},{33,65},{65,33},{2,98}... | collective-permute-start | bytes 3538952 | tf_op jit(solution)/shard_map/ppermute | solution.py:472
  139.0 49.6 %all-to-all-start.2 = ((bf16[32,208,256]{2,1,0:T(8,128)(2,1)}), bf16[32,208,256]{2,1,0:T(8,128)(2,1)}, u32[]{:S(2)}, u32[]{:S(2)}) async-start(bf16[32,208,256]{2,1,0:T(8,128)(2,1)} %copy-done.1), calls=%async_computation.2 | async-start | bytes 6815744 | tf_op jit(solution)/shard_map/all_to_all | solution.py:459
  164.8 16.8 %collective-permute-start.5 = (bf16[192,1536]{1,0:T(8,128)(2,1)S(1)}, bf16[192,1536]{1,0:T(8,128)(2,1)S(1)}, u32[]{:S(2)}, u32[]{:S(2)}) collective-permute-start(bf16[192,1536]{1,0:T(8,128)(2,1)S(1)} %get-tuple-element.123), channel_id=1, source_target_pairs={{0,96},{96,0},{32,64},{64,32},{1,97},{97,1},{33,65},{65,33},{2,98}... | collective-permute-start | bytes 1769480 | tf_op jit(solution)/shard_map/ppermute | solution.py:478
  167.4 14.2 %collective-permute-start.7 = (bf16[192,1536]{1,0:T(8,128)(2,1)S(1)}, bf16[192,1536]{1,0:T(8,128)(2,1)S(1)}, u32[]{:S(2)}, u32[]{:S(2)}) collective-permute-start(bf16[192,1536]{1,0:T(8,128)(2,1)S(1)} %get-tuple-element.124), channel_id=1, source_target_pairs={{0,32},{32,0},{64,96},{96,64},{1,33},{33,1},{65,97},{97,65},{2,34}... | collective-permute-start | bytes 1769480 | tf_op jit(solution)/shard_map/ppermute | solution.py:478
  173.7 7.9 %copy-start.23 = (bf16[2,384,1536]{2,1,0:T(8,128)(2,1)S(1)}, bf16[2,384,1536]{2,1,0:T(8,128)(2,1)}, u32[]{:S(2)}) copy-start(bf16[2,384,1536]{2,1,0:T(8,128)(2,1)} %get-tuple-element.69) | copy-start | bytes 7077892
  180.9 0.7 copy-start.20
  181.6 3.5 %copy-start.3 = (f32[2,512,768]{2,1,0:T(8,128)}, f32[2,512,768]{2,1,0:T(8,128)S(1)}, u32[]{:S(2)}) copy-start(f32[2,512,768]{2,1,0:T(8,128)S(1)} %get-tuple-element.87.refs_2_) | copy-start | bytes 9437188
  188.6 10.0 %copy-start.4 = (f32[2,512,768]{2,1,0:T(8,128)S(1)}, f32[2,512,768]{2,1,0:T(8,128)}, u32[]{:S(2)}) copy-start(f32[2,512,768]{2,1,0:T(8,128)} %copy-done.3) | copy-start | bytes 9437188
  188.6 10.0 %copy-start.21 = (f32[2,32,768]{2,1,0:T(8,128)S(1)}, f32[2,32,768]{2,1,0:T(8,128)}, u32[]{:S(2)}) copy-start(f32[2,32,768]{2,1,0:T(8,128)} %copy-done.20) | copy-start | bytes 589828
  196.9 44.3 %collective-permute-start.8 = (bf16[384,1536]{1,0:T(8,128)(2,1)}, bf16[384,1536]{1,0:T(8,128)(2,1)}, u32[]{:S(2)}, u32[]{:S(2)}) collective-permute-start(bf16[384,1536]{1,0:T(8,128)(2,1)} %get-tuple-element.79), channel_id=1, source_target_pairs={{0,32},{32,0},{64,96},{96,64},{1,33},{33,1},{65,97},{97,65},{2,34}... | collective-permute-start | bytes 3538952 | tf_op jit(solution)/shard_map/ppermute | solution.py:472
  197.9 43.3 %collective-permute-start.9 = (bf16[384,1536]{1,0:T(8,128)(2,1)}, bf16[384,1536]{1,0:T(8,128)(2,1)}, u32[]{:S(2)}, u32[]{:S(2)}) collective-permute-start(bf16[384,1536]{1,0:T(8,128)(2,1)} %get-tuple-element.80), channel_id=1, source_target_pairs={{0,96},{96,0},{32,64},{64,32},{1,97},{97,1},{33,65},{65,33},{2,98}... | collective-permute-start | bytes 3538952 | tf_op jit(solution)/shard_map/ppermute | solution.py:472
  208.2 45.9 %all-to-all-start.3 = ((bf16[32,104,256]{2,1,0:T(8,128)(2,1)}), bf16[32,104,256]{2,1,0:T(8,128)(2,1)S(1)}, u32[]{:S(2)}, u32[]{:S(2)}) async-start(bf16[32,104,256]{2,1,0:T(8,128)(2,1)} %project.5), calls=%async_computation.3 | async-start | bytes 3407872 | tf_op jit(solution)/shard_map/all_to_all | solution.py:459
  212.4 28.7 %collective-permute-start.10 = (bf16[192,1024]{1,0:T(8,128)(2,1)}, bf16[192,1024]{1,0:T(8,128)(2,1)S(1)}, u32[]{:S(2)}, u32[]{:S(2)}) collective-permute-start(bf16[192,1024]{1,0:T(8,128)(2,1)} %get-tuple-element.82), channel_id=1, source_target_pairs={{0,32},{32,64},{64,96},{96,0},{1,33},{33,65},{65,97},{97,1},{2,34}... | collective-permute-start | bytes 1179656 | tf_op jit(solution)/shard_map/ppermute | solution.py:494
  212.7 28.4 %collective-permute-start.11 = (bf16[192,1024]{1,0:T(8,128)(2,1)}, bf16[192,1024]{1,0:T(8,128)(2,1)S(1)}, u32[]{:S(2)}, u32[]{:S(2)}) collective-permute-start(bf16[192,1024]{1,0:T(8,128)(2,1)} %get-tuple-element.83), channel_id=1, source_target_pairs={{0,64},{32,96},{64,0},{96,32},{1,65},{33,97},{65,1},{97,33},{2,66}... | collective-permute-start | bytes 1179656 | tf_op jit(solution)/shard_map/ppermute | solution.py:494
  216.5 24.7 %collective-permute-start.12 = (bf16[192,1024]{1,0:T(8,128)(2,1)}, bf16[192,1024]{1,0:T(8,128)(2,1)S(1)}, u32[]{:S(2)}, u32[]{:S(2)}) collective-permute-start(bf16[192,1024]{1,0:T(8,128)(2,1)} %get-tuple-element.84), channel_id=1, source_target_pairs={{0,96},{32,0},{64,32},{96,64},{1,97},{33,1},{65,33},{97,65},{2,98}... | collective-permute-start | bytes 1179656 | tf_op jit(solution)/shard_map/ppermute | solution.py:494
  241.1 3.3 %copy-start.14 = (bf16[192,1024]{1,0:T(8,128)(2,1)}, bf16[192,1024]{1,0:T(8,128)(2,1)S(1)}, u32[]{:S(2)}) copy-start(bf16[192,1024]{1,0:T(8,128)(2,1)S(1)} %collective-permute-done.10.refs_1_) | copy-start | bytes 1179652
  241.1 3.3 %copy-start.16 = (bf16[192,1024]{1,0:T(8,128)(2,1)}, bf16[192,1024]{1,0:T(8,128)(2,1)S(1)}, u32[]{:S(2)}) copy-start(bf16[192,1024]{1,0:T(8,128)(2,1)S(1)} %collective-permute-done.11.refs_2_) | copy-start | bytes 1179652
  241.1 3.3 %copy-start.18 = (bf16[192,1024]{1,0:T(8,128)(2,1)}, bf16[192,1024]{1,0:T(8,128)(2,1)S(1)}, u32[]{:S(2)}) copy-start(bf16[192,1024]{1,0:T(8,128)(2,1)S(1)} %collective-permute-done.12.refs_3_) | copy-start | bytes 1179652
  244.5 17.1 %collective-permute-start.14 = (bf16[192,1536]{1,0:T(8,128)(2,1)}, bf16[192,1536]{1,0:T(8,128)(2,1)}, u32[]{:S(2)}, u32[]{:S(2)}) collective-permute-start(bf16[192,1536]{1,0:T(8,128)(2,1)} %get-tuple-element.121), channel_id=1, source_target_pairs={{0,32},{32,0},{64,96},{96,64},{1,33},{33,1},{65,97},{97,65},{2,34}... | collective-permute-start | bytes 1769480 | tf_op jit(solution)/shard_map/ppermute | solution.py:478
  244.6 27.2 %collective-permute-start.13 = (bf16[192,1536]{1,0:T(8,128)(2,1)}, bf16[192,1536]{1,0:T(8,128)(2,1)}, u32[]{:S(2)}, u32[]{:S(2)}) collective-permute-start(bf16[192,1536]{1,0:T(8,128)(2,1)} %get-tuple-element.122), channel_id=1, source_target_pairs={{0,96},{96,0},{32,64},{64,32},{1,97},{97,1},{33,65},{65,33},{2,98}... | collective-permute-start | bytes 1769480 | tf_op jit(solution)/shard_map/ppermute | solution.py:478
  248.4 48.8 %collective-permute-start.18 = (bf16[192,1536]{1,0:T(8,128)(2,1)}, bf16[192,1536]{1,0:T(8,128)(2,1)S(1)}, u32[]{:S(2)}, u32[]{:S(2)}) collective-permute-start(bf16[192,1536]{1,0:T(8,128)(2,1)} %get-tuple-element.96), channel_id=1, source_target_pairs={{0,32},{32,64},{64,96},{96,0},{1,33},{33,65},{65,97},{97,1},{2,34}... | collective-permute-start | bytes 1769480 | tf_op jit(solution)/shard_map/ppermute | solution.py:494
  249.4 52.5 %collective-permute-start.19 = (bf16[192,1536]{1,0:T(8,128)(2,1)}, bf16[192,1536]{1,0:T(8,128)(2,1)S(1)}, u32[]{:S(2)}, u32[]{:S(2)}) collective-permute-start(bf16[192,1536]{1,0:T(8,128)(2,1)} %get-tuple-element.97), channel_id=1, source_target_pairs={{0,64},{32,96},{64,0},{96,32},{1,65},{33,97},{65,1},{97,33},{2,66}... | collective-permute-start | bytes 1769480 | tf_op jit(solution)/shard_map/ppermute | solution.py:494
  252.2 49.8 %collective-permute-start.20 = (bf16[192,1536]{1,0:T(8,128)(2,1)}, bf16[192,1536]{1,0:T(8,128)(2,1)}, u32[]{:S(2)}, u32[]{:S(2)}) collective-permute-start(bf16[192,1536]{1,0:T(8,128)(2,1)} %get-tuple-element.98), channel_id=1, source_target_pairs={{0,96},{32,0},{64,32},{96,64},{1,97},{33,1},{65,33},{97,65},{2,98}... | collective-permute-start | bytes 1769480 | tf_op jit(solution)/shard_map/ppermute | solution.py:494
  254.1 1.4 copy-start.7
  255.5 1.0 copy-start.12
  256.5 1.0 copy-start.13
  257.6 14.2 %copy-start.22 = (bf16[2,384,1536]{2,1,0:T(8,128)(2,1)S(1)}, bf16[2,384,1536]{2,1,0:T(8,128)(2,1)}, u32[]{:S(2)}) copy-start(bf16[2,384,1536]{2,1,0:T(8,128)(2,1)} %get-tuple-element.78) | copy-start | bytes 7077892
  261.5 13.2 %copy-start.10 = (f32[1024,1]{1,0:T(8,128)}, f32[1024,1]{1,0:T(8,128)S(1)}, u32[]{:S(2)}) copy-start(f32[1024,1]{1,0:T(8,128)S(1)} %get-tuple-element.92) | copy-start | bytes 12292
  274.7 30.8 %collective-permute-start.17 = (bf16[192,1536]{1,0:T(8,128)(2,1)}, bf16[192,1536]{1,0:T(8,128)(2,1)S(1)}, u32[]{:S(2)}, u32[]{:S(2)}) collective-permute-start(bf16[192,1536]{1,0:T(8,128)(2,1)} %get-tuple-element.112), channel_id=1, source_target_pairs={{0,96},{32,0},{64,32},{96,64},{1,97},{33,1},{65,33},{97,65},{2,98}... | collective-permute-start | bytes 1769480 | tf_op jit(solution)/shard_map/ppermute | solution.py:494
  278.9 18.3 %copy-start.5 = (bf16[192,1024]{1,0:T(8,128)(2,1)S(1)}, bf16[192,1024]{1,0:T(8,128)(2,1)}, u32[]{:S(2)}) copy-start(bf16[192,1024]{1,0:T(8,128)(2,1)} %get-tuple-element.99.refs_0_) | copy-start | bytes 1179652
  280.0 25.5 %collective-permute-start.16 = (bf16[192,1536]{1,0:T(8,128)(2,1)}, bf16[192,1536]{1,0:T(8,128)(2,1)}, u32[]{:S(2)}, u32[]{:S(2)}) collective-permute-start(bf16[192,1536]{1,0:T(8,128)(2,1)} %get-tuple-element.127), channel_id=1, source_target_pairs={{0,64},{32,96},{64,0},{96,32},{1,65},{33,97},{65,1},{97,33},{2,66}... | collective-permute-start | bytes 1769480 | tf_op jit(solution)/shard_map/ppermute | solution.py:494
  297.1 11.4 %collective-permute-start.15 = (bf16[192,1536]{1,0:T(8,128)(2,1)}, bf16[192,1536]{1,0:T(8,128)(2,1)}, u32[]{:S(2)}, u32[]{:S(2)}) collective-permute-start(bf16[192,1536]{1,0:T(8,128)(2,1)} %get-tuple-element.128), channel_id=1, source_target_pairs={{0,32},{32,64},{64,96},{96,0},{1,33},{33,65},{65,97},{97,1},{2,34}... | collective-permute-start | bytes 1769480 | tf_op jit(solution)/shard_map/ppermute | solution.py:494
  297.2 1.0 copy-start.15
  298.2 1.0 copy-start.17
  299.2 1.0 copy-start.19
  301.9 2.6 copy-start.11

commit v3 on v2

--- a/solution.py
+++ b/solution.py
@@ -13,7 +13,6 @@
 SHIFT = 6
 MASK = (1 << SHIFT) - 1
 CHUNKS = (4, 6, 6)
-DEFER = False
 BF16 = jnp.bfloat16
 F32 = jnp.float32
 MIB = 1024 * 1024
@@ -133,11 +132,11 @@
             pl.BlockSpec((tok, parts * V), lambda i: (0, 0)),
         ],
         out_specs=pl.BlockSpec((SEND_STEP, rows, V), lambda i: (i, 0, 0)),
-        out_shape=jax.ShapeDtypeStruct((columns, rows, V), BF16),
+        out_shape=pltpu.HBM((columns, rows, V), BF16),
         compiler_params=params(24),
         cost_estimate=cost(2 * columns * MAIN * routes * hidden, 2 * columns * rows * V + 2 * routes * hidden),
         name="send_first",
-    )(codes, flat, prob, act, grad)
+    )(codes, flat, prob, in_hbm(act), in_hbm(grad))
 
 
 def send_rest(codes, grad, columns, start, chunks):
@@ -148,11 +147,11 @@
         grid=(columns // SEND_STEP,),
         in_specs=[whole(codes.shape), whole(grad.shape)],
         out_specs=[pl.BlockSpec((SEND_STEP, s[1], V), lambda i: (i, 0, 0)) for s in shapes],
-        out_shape=[jax.ShapeDtypeStruct(s, BF16) for s in shapes],
+        out_shape=[pltpu.HBM(s, BF16) for s in shapes],
         compiler_params=params(24),
         cost_estimate=cost(2 * columns * MAIN * tok * width, 2 * columns * 34 * width + 2 * tok * width),
         name="send_rest",
-    )(codes, grad)
+    )(codes, in_hbm(grad))
 
 
 def load_tail(got_ref, tail_ref):
@@ -175,12 +174,21 @@
     return rows.reshape(got_ref.shape[0] * half, V)
 
 
-def weight_step(acts, rows, more, keep_ref, send_ref, expert):
+def parts_a_step(parts):
+    return 2 if parts % 2 == 0 else 1
+
+
+def weight_step(acts, got_ref, tail_ref, part, count, keep_ref, send_ref, expert):
+    sources = got_ref.shape[0]
+    rows = jnp.concatenate([main_rows(got_ref, part + i, expert) for i in range(count)], axis=1)
+    more = jnp.concatenate([tail_rows(tail_ref, sources, part + i, expert) for i in range(count)], axis=1)
     depth = rows.shape[0]
     total = dot(acts[:, :depth], rows) + dot(acts[:, depth:], more)
     half = total.shape[0] // 2
-    keep_ref[expert] = total[:half].astype(BF16)
-    send_ref[...] = total[half:].astype(BF16)
+    size = count * V
+    at = pl.multiple_of(pl.program_id(0) * size, size)
+    keep_ref[expert, :, pl.ds(at, size)] = total[:half].astype(BF16)
+    send_ref[:, pl.ds(at, size)] = total[half:].astype(BF16)
 
 
 def weight_first_kernel(act_parts, order_ref, got_ref, acts_ref, keep_ref, low_ref, high_ref, tail_ref, plain_ref):
@@ -202,28 +210,27 @@
                 at = pl.multiple_of(order_ref[e, q] * size, size)
                 acts_ref[e, q * size : (q + 1) * size, :] = plain_ref[pl.ds(at, size), :]
 
+    count = parts_a_step(low_ref.shape[1] // V)
     for e, send_ref in enumerate((low_ref, high_ref)):
-        more = tail_rows(tail_ref, sources, act_parts + part, e)
-        weight_step(acts_ref[e], main_rows(got_ref, act_parts + part, e), more, keep_ref, send_ref, e)
+        weight_step(acts_ref[e], got_ref, tail_ref, act_parts + part * count, count, keep_ref, send_ref, e)
 
 
 def weight_kernel(acts_ref, got_ref, keep_ref, low_ref, high_ref, tail_ref):
-    sources = got_ref.shape[0]
     part = pl.program_id(0)
 
     @pl.when(part == 0)
     def _():
         load_tail(got_ref, tail_ref)
 
+    count = parts_a_step(low_ref.shape[1] // V)
     for e, send_ref in enumerate((low_ref, high_ref)):
-        more = tail_rows(tail_ref, sources, part, e)
-        weight_step(acts_ref[e], main_rows(got_ref, part, e), more, keep_ref, send_ref, e)
+        weight_step(acts_ref[e], got_ref, tail_ref, part * count, count, keep_ref, send_ref, e)
 
 
 def sum_specs(hidden, parts):
     half = hidden // 2
-    specs = [pl.BlockSpec((2, half, V), lambda p: (0, 0, p))] + [pl.BlockSpec((half, V), lambda p: (0, p))] * 2
-    shapes = [pltpu.HBM((2, half, parts * V), BF16)] + [pltpu.HBM((half, parts * V), BF16)] * 2
+    specs = [resident()] * 3
+    shapes = [jax.ShapeDtypeStruct(s, BF16) for s in ((2, half, parts * V), (half, parts * V), (half, parts * V))]
     return specs, shapes
 
 
@@ -236,7 +243,7 @@
     specs, shapes = sum_specs(hidden, parts)
     return pl.pallas_call(
         functools.partial(weight_first_kernel, hidden // V),
-        grid=(parts,),
+        grid=(parts // parts_a_step(parts),),
         in_specs=[pl.BlockSpec(memory_space=pltpu.SMEM), resident()],
         out_specs=[whole((2, hidden, depth))] + specs,
         out_shape=[pltpu.HBM((2, hidden, depth), BF16)] + shapes,
@@ -252,7 +259,7 @@
     specs, shapes = sum_specs(hidden, parts)
     return pl.pallas_call(
         weight_kernel,
-        grid=(parts,),
+        grid=(parts // parts_a_step(parts),),
         in_specs=[whole(acts.shape), resident()],
         out_specs=specs,
         out_shape=shapes,
@@ -490,8 +497,8 @@
             out.append(jnp.where(which == 0, mine[0], mine[1]))
         return out
 
-    def moved(sends):
-        return [lax.ppermute(sends[d], "grp", hops[d]) if d else sends[d] for d in range(groups)]
+    def hop(sends, d):
+        return lax.ppermute(sends[d], "grp", hops[d]) if d else sends[0]
 
     sources = jnp.stack([(my_group + groups - d) % groups for d in range(groups)]).astype(jnp.int32)
 
@@ -511,11 +518,11 @@
             acts, keep, low, high = weight_first(order, got[0], hidden, CHUNKS[0])
         else:
             got[c], sends[c - 1] = barrier((got[c], sends[c - 1]))
-            if c == last:
-                got[c], state = barrier((got[c], state))
             keep, low, high = weight_rest(acts, got[c], CHUNKS[c])
+            pre = lax.ppermute(sends[c - 1][2], "grp", hops[2])
+            low, high, pre = barrier((low, high, pre))
+            blocks[c - 1] = [sends[c - 1][0], hop(sends[c - 1], 1), pre, hop(sends[c - 1], 3)]
         if c < last:
-            outs[c + 1], low, high = barrier((outs[c + 1], low, high))
             got[c + 1] = exchange(outs[c + 1])
             skip = act_parts if c == 0 else 0
             state = project(got[c], down_weight, starts[c], skip, CHUNKS[c], state, False)
@@ -524,18 +531,16 @@
             proj = project(got[last], down_weight, starts[last], 0, CHUNKS[last], state, True)
             back = exchange(proj)
             grad_act, grad_prob = finish(codes.reshape(tok * top, 1), prob.reshape(tok * top, 1), act, back)
-        if c >= 2:
-            came, blocks[c - 2] = barrier((came, blocks[c - 2]))
+        if c >= 1:
+            came, blocks[c - 1] = barrier((came, blocks[c - 1]))
+        if c == last - 1:
+            came, state = barrier((came, state))
         passed = forwarded(keep, came)
-        if c >= 1:
-            if DEFER:
-                passed, sends[c - 1] = barrier((passed, sends[c - 1]))
-            blocks[c - 1] = moved(sends[c - 1])
         last_came = second_round(*passed)
         if c == last:
             last_came, grad_act, grad_prob = barrier((last_came, grad_act, grad_prob))
         sends[c] = wanted(completed(keep, came, last_came))
-    blocks[last] = moved(sends[last])
+    blocks[last] = [hop(sends[last], d) for d in range(groups)]
     own = None
     for c in range(last + 1):
         own = place(sources, blocks[c], own, hidden, width, starts[c] * V)

time: 316 us -> 295 us (0.934)
  waiting for transfers between devices: 146 us -> 130 us
  local copies, waits for them, and re-layouts: 21.1 us -> 15.6 us
  Pallas kernels: 64.1 us -> 68.2 us
  other arithmetic: 23 us -> 19.8 us
    ppermute x6, waiting for transfers between devices: 37.4 us -> 18 us  [first_round(): return (lax.ppermute(low, 'grp', near), lax.ppermute(high, 'grp', far))]
    ppermute x9, waiting for transfers between devices: 42.3 us -> 48.9 us  [the longest x7 44.8 us: hop(): return lax.ppermute(sends[d], 'grp', hops[d]) if d else sends[0]]
    unnamed x57, local copies, waits for them, and re-layouts: 16.5 us -> 10.1 us
    all_to_all x4, starting transfers between devices: 20.8 us -> 25.1 us  [exchange(): return lax.all_to_all(v, 'sp', 0, 0, tiled=True)]
    all_to_all x4, waiting for transfers between devices: 48.7 us -> 44.9 us  [exchange(): return lax.all_to_all(v, 'sp', 0, 0, tiled=True)]
  transfers between devices with their start and end apart: 25 -> 25, of which waited for: 13 -> 12; matrix products, arithmetic and copies ran while one was open for 8% -> 7% of each run, Pallas kernels for 11% -> 20%
where the time goes in v3:
time: 295 us; the launch traced here: 292 us
  waiting for transfers between devices  130 us (44%)
  Pallas kernels  68.2 us (23%)
  starting transfers between devices  55 us (19%)
  other arithmetic  19.8 us (7%)
  local copies, waits for them, and re-layouts  15.6 us (5%)
  between operations  3.56 us (1%)
    all_to_all x4, waiting for transfers between devices, exchange(): return lax.all_to_all(v, 'sp', 0, 0, tiled=True)  44.9 us
    ppermute x7, waiting for transfers between devices, hop(): return lax.ppermute(sends[d], 'grp', hops[d]) if d else sends[0]  44.8 us
    all_to_all x4, starting transfers between devices, exchange(): return lax.all_to_all(v, 'sp', 0, 0, tiled=True)  25.1 us
    pallas_call x3, Pallas kernels, project(): pl.pallas_call(functools.partial(project_kernel, skip, parts, state is no...  23.1 us
    ppermute x6, waiting for transfers between devices, second_round(): return (lax.ppermute(low, 'grp', far), lax.ppermute(high, 'grp', near))  18.2 us
    ppermute x6, waiting for transfers between devices, first_round(): return (lax.ppermute(low, 'grp', near), lax.ppermute(high, 'grp', far))  18 us
    pallas_call x2, Pallas kernels, weight_rest(): pl.pallas_call(weight_kernel, grid=(parts // parts_a_step(parts),), in_sp...  14.8 us
    select_n x6, other arithmetic, wanted(): out.append(jnp.where(which == 0, mine[0], mine[1]))  11.9 us
  transfers between devices with their start and end apart: 25, of which 12 were waited for; matrix products, arithmetic and copies ran while one was open for 7% of the time, Pallas kernels for 20%

profile of v3, /device:TPU:0, one launch (start us, length us, event | category | flops | bytes accessed | tf_op | source)
XLA Modules:
  0.0 292.4 jit_solution(6187516061030694029)
XLA Ops:
  4.6 6.8 %send_first.1 = bf16[32,240,256]{2,1,0:T(8,128)(2,1)} custom-call(s32[8,128]{1,0:T(8,128)S(1)} %bitcast.65, s32[1,1024]{1,0:T(1,128)S(1)} %reshape.82.flat_ref, f32[1,1024]{1,0:T(1,128)S(1)} %reshape.83.prob_ref, bf16[1024,768]{1,0:T(8,128)(2,1)} %bitcast.63, bf16[128,4096]{1,0:T(8,128)(2,1)} %grad_ref.3), custom_call_target="tpu_custom_call" | custom-call | flops 1610612736 | bytes 5505024 | tf_op jit(solution)/shard_map/send_first/pallas_call | solution.py:124
  11.3 7.5 %all-to-all-start = ((bf16[32,240,256]{2,1,0:T(8,128)(2,1)}), bf16[32,240,256]{2,1,0:T(8,128)(2,1)}, u32[]{:S(2)}, u32[]{:S(2)}) async-start(bf16[32,240,256]{2,1,0:T(8,128)(2,1)} %send_first.1), calls=%async_computation | async-start | bytes 7864320 | tf_op jit(solution)/shard_map/all_to_all | solution.py:466
  18.9 5.7 %send_rest.1 = (bf16[32,208,256]{2,1,0:T(8,128)(2,1)}, bf16[32,208,256]{2,1,0:T(8,128)(2,1)}) custom-call(s32[8,128]{1,0:T(8,128)S(1)} %bitcast.66, bf16[128,4096]{1,0:T(8,128)(2,1)} %grad_ref.3), custom_call_target="tpu_custom_call" | custom-call | flops 1073741824 | bytes 9961472 | tf_op jit(solution)/shard_map/send_rest/pallas_call | solution.py:145
  24.6 44.9 %all-to-all-done.got_ref.refs_0_ = bf16[32,240,256]{2,1,0:T(8,128)(2,1)} async-done(((bf16[32,240,256]{2,1,0:T(8,128)(2,1)}), bf16[32,240,256]{2,1,0:T(8,128)(2,1)}, u32[]{:S(2)}, u32[]{:S(2)}) %all-to-all-start) | async-done | bytes 3932192 | tf_op jit(solution)/shard_map/all_to_all | solution.py:466
  69.5 4.1 %all-to-all-start.2 = ((bf16[32,208,256]{2,1,0:T(8,128)(2,1)}), bf16[32,208,256]{2,1,0:T(8,128)(2,1)S(1)}, u32[]{:S(2)}, u32[]{:S(2)}) async-start(bf16[32,208,256]{2,1,0:T(8,128)(2,1)} %get-tuple-element.65), calls=%async_computation.2 | async-start | bytes 6815744 | tf_op jit(solution)/shard_map/all_to_all | solution.py:466
  73.6 5.9 %weight_first.1 = (bf16[2,768,544]{2,1,0:T(8,128)(2,1)}, bf16[2,384,1024]{2,1,0:T(8,128)(2,1)S(1)}, bf16[384,1024]{1,0:T(8,128)(2,1)S(1)}, bf16[384,1024]{1,0:T(8,128)(2,1)S(1)}) custom-call(s32[2,4]{1,0:T(2,128)S(1)} %pad_add_fusion.order_ref, bf16[32,240,256]{2,1,0:T(8,128)(2,1)} %all-to-all-done.got_ref.refs_0_), custom_call_target="tpu_custom_call" | custom-call | flops 1711276032 | bytes 7274496 | tf_op jit(solution)/shard_map/weight_first/pallas_call | solution.py:244
  79.5 1.9 collective-permute-start
  81.4 2.5 collective-permute-start.2
  84.0 15.3 %collective-permute-done = bf16[384,1024]{1,0:T(8,128)(2,1)S(1)} collective-permute-done((bf16[384,1024]{1,0:T(8,128)(2,1)S(1)}, bf16[384,1024]{1,0:T(8,128)(2,1)S(1)}, u32[]{:S(2)}, u32[]{:S(2)}) %collective-permute-start) | collective-permute-done | bytes 786464 | tf_op jit(solution)/shard_map/ppermute | solution.py:479
  99.3 2.7 collective-permute-done.2
  102.0 1.2 fusion.15
  103.2 2.6 collective-permute-start.1
  109.0 5.8 %collective-permute-done.1 = bf16[192,1024]{1,0:T(8,128)(2,1)} collective-permute-done((bf16[192,1024]{1,0:T(8,128)(2,1)}, bf16[192,1024]{1,0:T(8,128)(2,1)}, u32[]{:S(2)}, u32[]{:S(2)}) %collective-permute-start.1) | collective-permute-done | bytes 393248 | tf_op jit(solution)/shard_map/ppermute | solution.py:485
  114.8 1.0 collective-permute-done.3
  115.8 2.8 broadcast_select_fusion.8
  118.6 1.1 broadcast_select_fusion.9
  119.7 2.4 collective-permute-start.4
  122.2 6.8 %weight_rest.2 = (bf16[2,384,1536]{2,1,0:T(8,128)(2,1)S(1)}, bf16[384,1536]{1,0:T(8,128)(2,1)}, bf16[384,1536]{1,0:T(8,128)(2,1)}) custom-call(bf16[2,768,544]{2,1,0:T(8,128)(2,1)} %get-tuple-element.63.acts_ref, bf16[32,208,256]{2,1,0:T(8,128)(2,1)S(1)} %all-to-all-done.2.got_ref.refs_0_), custom_call_target="tpu_custom_call" | custom-call | flops 2566914048 | bytes 9797632 | tf_op jit(solution)/shard_map/weight_rest/pallas_call | solution.py:260
  128.9 1.5 copy-done.2
  131.2 1.0 collective-permute-start.5
  132.2 1.3 collective-permute-start.6
  133.6 6.8 %all-to-all-start.1 = ((bf16[32,208,256]{2,1,0:T(8,128)(2,1)}), bf16[32,208,256]{2,1,0:T(8,128)(2,1)}, u32[]{:S(2)}, u32[]{:S(2)}) async-start(bf16[32,208,256]{2,1,0:T(8,128)(2,1)} %get-tuple-element.64), calls=%async_computation.1 | async-start | bytes 6815744 | tf_op jit(solution)/shard_map/all_to_all | solution.py:466
  140.4 1.4 collective-permute-start.7
  141.8 1.9 collective-permute-start.8
  143.7 6.3 %project.3 = (f32[2,512,768]{2,1,0:T(8,128)S(1)}, f32[2,32,768]{2,1,0:T(8,128)S(1)}) custom-call(bf16[32,240,256]{2,1,0:T(8,128)(2,1)} %all-to-all-done.got_ref.refs_0_, bf16[2,768,4096]{2,1,0:T(8,128)(2,1)} %refs_1_.5), custom_call_target="tpu_custom_call" | custom-call | flops 1711276032 | bytes 13762560 | tf_op jit(solution)/shard_map/project/pallas_call | solution.py:345
  150.0 7.2 %project.4 = (f32[2,512,768]{2,1,0:T(8,128)S(1)}, f32[2,32,768]{2,1,0:T(8,128)S(1)}) custom-call(bf16[32,208,256]{2,1,0:T(8,128)(2,1)S(1)} %all-to-all-done.2.got_ref.refs_0_, bf16[2,768,4096]{2,1,0:T(8,128)(2,1)} %refs_1_.5, f32[2,512,768]{2,1,0:T(8,128)S(1)} %get-tuple-element.82.refs_2_, f32[2,32,768]{2,1,0:T(8,128)S(1)} %get-tuple-element.83.refs_3_), custom_call_target="tpu_custom_call" | custom-call | flops 2566914048 | bytes 14811136 | tf_op jit(solution)/shard_map/project/pallas_call | solution.py:345
  157.9 8.9 %collective-permute-done.7.refs_1_ = bf16[192,1024]{1,0:T(8,128)(2,1)S(1)} collective-permute-done((bf16[192,1024]{1,0:T(8,128)(2,1)}, bf16[192,1024]{1,0:T(8,128)(2,1)S(1)}, u32[]{:S(2)}, u32[]{:S(2)}) %collective-permute-start.7) | collective-permute-done | bytes 393248 | tf_op jit(solution)/shard_map/ppermute | solution.py:501
  166.7 0.8 copy-done.19
  167.5 1.6 fusion.9
  169.1 1.1 collective-permute-start.9
  170.3 11.4 %collective-permute-done.9 = bf16[192,1536]{1,0:T(8,128)(2,1)S(1)} collective-permute-done((bf16[192,1536]{1,0:T(8,128)(2,1)S(1)}, bf16[192,1536]{1,0:T(8,128)(2,1)S(1)}, u32[]{:S(2)}, u32[]{:S(2)}) %collective-permute-start.9) | collective-permute-done | bytes 589856 | tf_op jit(solution)/shard_map/ppermute | solution.py:485
  181.6 2.6 broadcast_select_fusion.1
  184.2 1.1 broadcast_select_fusion.3
  185.4 1.9 collective-permute-start.11
  187.3 8.0 %weight_rest.3 = (bf16[2,384,1536]{2,1,0:T(8,128)(2,1)S(1)}, bf16[384,1536]{1,0:T(8,128)(2,1)}, bf16[384,1536]{1,0:T(8,128)(2,1)}) custom-call(bf16[2,768,544]{2,1,0:T(8,128)(2,1)} %get-tuple-element.63.acts_ref, bf16[32,208,256]{2,1,0:T(8,128)(2,1)} %all-to-all-done.1.got_ref.refs_0_), custom_call_target="tpu_custom_call" | custom-call | flops 2566914048 | bytes 9797632 | tf_op jit(solution)/shard_map/weight_rest/pallas_call | solution.py:260
  195.3 4.1 %collective-permute-done.11.refs_2_ = bf16[192,1536]{1,0:T(8,128)(2,1)S(1)} collective-permute-done((bf16[192,1536]{1,0:T(8,128)(2,1)}, bf16[192,1536]{1,0:T(8,128)(2,1)S(1)}, u32[]{:S(2)}, u32[]{:S(2)}) %collective-permute-start.11) | collective-permute-done | bytes 589856 | tf_op jit(solution)/shard_map/ppermute | solution.py:522
  199.4 1.7 collective-permute-start.12
  201.1 1.1 collective-permute-start.13
  202.3 9.7 %project.5 = bf16[32,104,256]{2,1,0:T(8,128)(2,1)} custom-call(bf16[32,208,256]{2,1,0:T(8,128)(2,1)} %all-to-all-done.1.got_ref.refs_0_, bf16[2,768,4096]{2,1,0:T(8,128)(2,1)} %refs_1_.5, f32[2,512,768]{2,1,0:T(8,128)S(1)} %copy-done.1, f32[2,32,768]{2,1,0:T(8,128)S(1)} %copy-done.22), custom_call_target="tpu_custom_call" | custom-call | flops 2566914048 | bytes 14811136 | tf_op jit(solution)/shard_map/project/pallas_call | solution.py:345
  211.9 6.7 %all-to-all-start.3 = ((bf16[32,104,256]{2,1,0:T(8,128)(2,1)}), bf16[32,104,256]{2,1,0:T(8,128)(2,1)}, u32[]{:S(2)}, u32[]{:S(2)}) async-start(bf16[32,104,256]{2,1,0:T(8,128)(2,1)} %project.5), calls=%async_computation.3 | async-start | bytes 3407872 | tf_op jit(solution)/shard_map/all_to_all | solution.py:466
  218.7 1.0 collective-permute-start.14
  219.7 2.3 collective-permute-start.15
  222.0 16.8 %collective-permute-done.14.refs_1_ = bf16[192,1536]{1,0:T(8,128)(2,1)S(1)} collective-permute-done((bf16[192,1536]{1,0:T(8,128)(2,1)}, bf16[192,1536]{1,0:T(8,128)(2,1)S(1)}, u32[]{:S(2)}, u32[]{:S(2)}) %collective-permute-start.14) | collective-permute-done | bytes 589856 | tf_op jit(solution)/shard_map/ppermute | solution.py:501
  238.8 0.8 copy-done.7
  239.7 0.8 copy-done.9
  240.5 2.6 fusion.4
  243.1 1.4 collective-permute-start.16
  244.4 1.9 reshape.103.prob_ref
  246.3 1.8 reshape.102.code_ref
  248.1 1.4 copy-done.5
  249.5 1.0 copy-done.13
  250.6 1.0 copy-done.14
  251.6 5.4 %finish.1 = (bf16[1024,768]{1,0:T(8,128)(2,1)}, f32[1024,1]{1,0:T(8,128)S(1)}) custom-call(s32[1024,1]{1,0:T(8,128)S(1)} %copy-done.14, f32[1024,1]{1,0:T(8,128)S(1)} %copy-done.13, bf16[1024,768]{1,0:T(8,128)(2,1)S(1)} %bitcast.64, bf16[32,104,256]{2,1,0:T(8,128)(2,1)} %all-to-all-done.3.back_ref), custom_call_target="tpu_custom_call" | custom-call | flops 1610612736 | bytes 4849664 | tf_op jit(solution)/shard_map/finish/pallas_call | solution.py:390
  257.0 3.1 %broadcast_select_fusion = (bf16[192,1536]{1,0:T(8,128)(2,1)}, bf16[192,1536]{1,0:T(8,128)(2,1)S(1)}, bf16[192,1536]{1,0:T(8,128)(2,1)S(1)}) fusion(pred[]{:T(512)} %bitcast.15, bf16[192,1536]{1,0:T(8,128)(2,1)} %collective-permute-done.17, bf16[384,1536]{1,0:T(8,128)(2,1)} %collective-permute-done.13, bf16[2,384,1536]{2,1,0:T(8,128)(2,1)S(1)} %get-tuple-element.89, ...), kind=kLoop, calls=%fused_computation.30 | loop fusion | flops 3833856 | bytes 5308417 | tf_op jit(solution)/shard_map/jit(_where)/select_n | solution.py:497
  260.1 1.9 collective-permute-start.20
  262.0 1.1 broadcast_select_fusion.2
  263.2 0.9 collective-permute-start.19
  264.1 1.4 collective-permute-start.18
  265.6 1.7 place.3.refs_4_
  267.3 2.0 place.4.refs_4_
  270.3 6.4 %collective-permute-done.20.refs_3_ = bf16[192,1536]{1,0:T(8,128)(2,1)} collective-permute-done((bf16[192,1536]{1,0:T(8,128)(2,1)}, bf16[192,1536]{1,0:T(8,128)(2,1)}, u32[]{:S(2)}, u32[]{:S(2)}) %collective-permute-start.20) | collective-permute-done | bytes 589856 | tf_op jit(solution)/shard_map/ppermute | solution.py:501
  276.7 4.5 %collective-permute-done.19.refs_2_ = bf16[192,1536]{1,0:T(8,128)(2,1)} collective-permute-done((bf16[192,1536]{1,0:T(8,128)(2,1)}, bf16[192,1536]{1,0:T(8,128)(2,1)}, u32[]{:S(2)}, u32[]{:S(2)}) %collective-permute-start.19) | collective-permute-done | bytes 589856 | tf_op jit(solution)/shard_map/ppermute | solution.py:501
  281.3 8.1 %collective-permute-done.18.refs_1_ = bf16[192,1536]{1,0:T(8,128)(2,1)} collective-permute-done((bf16[192,1536]{1,0:T(8,128)(2,1)}, bf16[192,1536]{1,0:T(8,128)(2,1)}, u32[]{:S(2)}, u32[]{:S(2)}) %collective-permute-start.18) | collective-permute-done | bytes 589856 | tf_op jit(solution)/shard_map/ppermute | solution.py:501
  289.4 2.9 place.5
  (81 shorter events, 7.3 us)
Async XLA Ops:
  3.1 0.6 copy-start.25
  4.5 6.9 %copy-start.26 = (f32[128,8]{1,0:T(8,128)}, f32[128,8]{1,0:T(8,128)S(1)}, u32[]{:S(2)}) copy-start(f32[128,8]{1,0:T(8,128)S(1)} %copy.27) | copy-start | bytes 12292
  11.3 58.1 %all-to-all-start = ((bf16[32,240,256]{2,1,0:T(8,128)(2,1)}), bf16[32,240,256]{2,1,0:T(8,128)(2,1)}, u32[]{:S(2)}, u32[]{:S(2)}) async-start(bf16[32,240,256]{2,1,0:T(8,128)(2,1)} %send_first.1), calls=%async_computation | async-start | bytes 7864320 | tf_op jit(solution)/shard_map/all_to_all | solution.py:466
  69.5 50.3 %all-to-all-start.2 = ((bf16[32,208,256]{2,1,0:T(8,128)(2,1)}), bf16[32,208,256]{2,1,0:T(8,128)(2,1)S(1)}, u32[]{:S(2)}, u32[]{:S(2)}) async-start(bf16[32,208,256]{2,1,0:T(8,128)(2,1)} %get-tuple-element.65), calls=%async_computation.2 | async-start | bytes 6815744 | tf_op jit(solution)/shard_map/all_to_all | solution.py:466
  79.5 23.6 %copy-start.6 = (bf16[2,384,1024]{2,1,0:T(8,128)(2,1)}, bf16[2,384,1024]{2,1,0:T(8,128)(2,1)S(1)}, u32[]{:S(2)}) copy-start(bf16[2,384,1024]{2,1,0:T(8,128)(2,1)S(1)} %get-tuple-element.66) | copy-start | bytes 4718596
  79.5 19.8 %collective-permute-start = (bf16[384,1024]{1,0:T(8,128)(2,1)S(1)}, bf16[384,1024]{1,0:T(8,128)(2,1)S(1)}, u32[]{:S(2)}, u32[]{:S(2)}) collective-permute-start(bf16[384,1024]{1,0:T(8,128)(2,1)S(1)} %get-tuple-element.67), channel_id=1, source_target_pairs={{0,32},{32,0},{64,96},{96,64},{1,33},{33,1},{65,97},{97,65},{2,34}... | collective-permute-start | bytes 2359304 | tf_op jit(solution)/shard_map/ppermute | solution.py:479
  81.4 20.5 %collective-permute-start.2 = (bf16[384,1024]{1,0:T(8,128)(2,1)S(1)}, bf16[384,1024]{1,0:T(8,128)(2,1)S(1)}, u32[]{:S(2)}, u32[]{:S(2)}) collective-permute-start(bf16[384,1024]{1,0:T(8,128)(2,1)S(1)} %get-tuple-element.68), channel_id=1, source_target_pairs={{0,96},{96,0},{32,64},{64,32},{1,97},{97,1},{33,65},{65,33},{2,98}... | collective-permute-start | bytes 2359304 | tf_op jit(solution)/shard_map/ppermute | solution.py:479
  99.3 3.9 %copy-start.23 = (bf16[384,1024]{1,0:T(8,128)(2,1)}, bf16[384,1024]{1,0:T(8,128)(2,1)S(1)}, u32[]{:S(2)}) copy-start(bf16[384,1024]{1,0:T(8,128)(2,1)S(1)} %collective-permute-done) | copy-start | bytes 2359300
  102.0 1.2 copy-start.24
  102.0 3.8 %copy-start.27 = (s32[4,32]{1,0:T(4,128)S(1)}, s32[4,32]{1,0:T(4,128)}, u32[]{:S(2)}) copy-start(s32[4,32]{1,0:T(4,128)} %param.10) | copy-start | bytes 1540
  103.2 11.6 %collective-permute-start.1 = (bf16[192,1024]{1,0:T(8,128)(2,1)}, bf16[192,1024]{1,0:T(8,128)(2,1)}, u32[]{:S(2)}, u32[]{:S(2)}) collective-permute-start(bf16[192,1024]{1,0:T(8,128)(2,1)} %get-tuple-element.139), channel_id=1, source_target_pairs={{0,96},{96,0},{32,64},{64,32},{1,97},{97,1},{33,65},{65,33},{2,98}... | collective-permute-start | bytes 1179656 | tf_op jit(solution)/shard_map/ppermute | solution.py:485
  105.8 10.1 %collective-permute-start.3 = (bf16[192,1024]{1,0:T(8,128)(2,1)}, bf16[192,1024]{1,0:T(8,128)(2,1)}, u32[]{:S(2)}, u32[]{:S(2)}) collective-permute-start(bf16[192,1024]{1,0:T(8,128)(2,1)} %get-tuple-element.140), channel_id=1, source_target_pairs={{0,32},{32,0},{64,96},{96,64},{1,33},{33,1},{65,97},{97,65},{2,34}... | collective-permute-start | bytes 1179656 | tf_op jit(solution)/shard_map/ppermute | solution.py:485
  119.7 10.7 %collective-permute-start.4 = (bf16[192,1024]{1,0:T(8,128)(2,1)}, bf16[192,1024]{1,0:T(8,128)(2,1)S(1)}, u32[]{:S(2)}, u32[]{:S(2)}) collective-permute-start(bf16[192,1024]{1,0:T(8,128)(2,1)} %get-tuple-element.73), channel_id=1, source_target_pairs={{0,64},{32,96},{64,0},{96,32},{1,65},{33,97},{65,1},{97,33},{2,66}... | collective-permute-start | bytes 1179656 | tf_op jit(solution)/shard_map/ppermute | solution.py:522
  128.9 1.5 copy-start.2
  130.4 0.8 copy-start.15
  131.2 36.3 %collective-permute-start.5 = (bf16[384,1536]{1,0:T(8,128)(2,1)}, bf16[384,1536]{1,0:T(8,128)(2,1)}, u32[]{:S(2)}, u32[]{:S(2)}) collective-permute-start(bf16[384,1536]{1,0:T(8,128)(2,1)} %get-tuple-element.74), channel_id=1, source_target_pairs={{0,32},{32,0},{64,96},{96,64},{1,33},{33,1},{65,97},{97,65},{2,34}... | collective-permute-start | bytes 3538952 | tf_op jit(solution)/shard_map/ppermute | solution.py:479
  132.2 35.3 %collective-permute-start.6 = (bf16[384,1536]{1,0:T(8,128)(2,1)}, bf16[384,1536]{1,0:T(8,128)(2,1)}, u32[]{:S(2)}, u32[]{:S(2)}) collective-permute-start(bf16[384,1536]{1,0:T(8,128)(2,1)} %get-tuple-element.75), channel_id=1, source_target_pairs={{0,96},{96,0},{32,64},{64,32},{1,97},{97,1},{33,65},{65,33},{2,98}... | collective-permute-start | bytes 3538952 | tf_op jit(solution)/shard_map/ppermute | solution.py:479
  133.6 51.8 %all-to-all-start.1 = ((bf16[32,208,256]{2,1,0:T(8,128)(2,1)}), bf16[32,208,256]{2,1,0:T(8,128)(2,1)}, u32[]{:S(2)}, u32[]{:S(2)}) async-start(bf16[32,208,256]{2,1,0:T(8,128)(2,1)} %get-tuple-element.64), calls=%async_computation.1 | async-start | bytes 6815744 | tf_op jit(solution)/shard_map/all_to_all | solution.py:466
  140.4 26.4 %collective-permute-start.7 = (bf16[192,1024]{1,0:T(8,128)(2,1)}, bf16[192,1024]{1,0:T(8,128)(2,1)S(1)}, u32[]{:S(2)}, u32[]{:S(2)}) collective-permute-start(bf16[192,1024]{1,0:T(8,128)(2,1)} %get-tuple-element.77), channel_id=1, source_target_pairs={{0,32},{32,64},{64,96},{96,0},{1,33},{33,65},{65,97},{97,1},{2,34}... | collective-permute-start | bytes 1179656 | tf_op jit(solution)/shard_map/ppermute | solution.py:501
  141.8 25.0 %collective-permute-start.8 = (bf16[192,1024]{1,0:T(8,128)(2,1)}, bf16[192,1024]{1,0:T(8,128)(2,1)S(1)}, u32[]{:S(2)}, u32[]{:S(2)}) collective-permute-start(bf16[192,1024]{1,0:T(8,128)(2,1)} %get-tuple-element.79), channel_id=1, source_target_pairs={{0,96},{32,0},{64,32},{96,64},{1,97},{33,1},{65,33},{97,65},{2,98}... | collective-permute-start | bytes 1179656 | tf_op jit(solution)/shard_map/ppermute | solution.py:501
  149.9 17.6 %copy-start.3 = (bf16[2,384,1536]{2,1,0:T(8,128)(2,1)S(1)}, bf16[2,384,1536]{2,1,0:T(8,128)(2,1)}, u32[]{:S(2)}) copy-start(bf16[2,384,1536]{2,1,0:T(8,128)(2,1)} %copy-done.2) | copy-start | bytes 7077892
  157.2 0.7 copy-start.21
  157.9 11.2 %copy-start = (f32[2,512,768]{2,1,0:T(8,128)}, f32[2,512,768]{2,1,0:T(8,128)S(1)}, u32[]{:S(2)}) copy-start(f32[2,512,768]{2,1,0:T(8,128)S(1)} %get-tuple-element.101.refs_2_) | copy-start | bytes 9437188
  166.7 2.4 copy-start.17
  166.7 0.8 copy-start.19
  169.1 12.5 %collective-permute-start.9 = (bf16[192,1536]{1,0:T(8,128)(2,1)S(1)}, bf16[192,1536]{1,0:T(8,128)(2,1)S(1)}, u32[]{:S(2)}, u32[]{:S(2)}) collective-permute-start(bf16[192,1536]{1,0:T(8,128)(2,1)S(1)} %get-tuple-element.137), channel_id=1, source_target_pairs={{0,96},{96,0},{32,64},{64,32},{1,97},{97,1},{33,65},{65,33},{2,98}... | collective-permute-start | bytes 1769480 | tf_op jit(solution)/shard_map/ppermute | solution.py:485
  170.3 11.4 %collective-permute-start.10 = (bf16[192,1536]{1,0:T(8,128)(2,1)S(1)}, bf16[192,1536]{1,0:T(8,128)(2,1)S(1)}, u32[]{:S(2)}, u32[]{:S(2)}) collective-permute-start(bf16[192,1536]{1,0:T(8,128)(2,1)S(1)} %get-tuple-element.138), channel_id=1, source_target_pairs={{0,32},{32,0},{64,96},{96,64},{1,33},{33,1},{65,97},{97,65},{2,34}... | collective-permute-start | bytes 1769480 | tf_op jit(solution)/shard_map/ppermute | solution.py:485
  185.4 16.9 %copy-start.22 = (f32[2,32,768]{2,1,0:T(8,128)S(1)}, f32[2,32,768]{2,1,0:T(8,128)}, u32[]{:S(2)}) copy-start(f32[2,32,768]{2,1,0:T(8,128)} %copy-done.21) | copy-start | bytes 589828
  185.4 14.0 %collective-permute-start.11 = (bf16[192,1536]{1,0:T(8,128)(2,1)}, bf16[192,1536]{1,0:T(8,128)(2,1)S(1)}, u32[]{:S(2)}, u32[]{:S(2)}) collective-permute-start(bf16[192,1536]{1,0:T(8,128)(2,1)} %get-tuple-element.92), channel_id=1, source_target_pairs={{0,64},{32,96},{64,0},{96,32},{1,65},{33,97},{65,1},{97,33},{2,66}... | collective-permute-start | bytes 1769480 | tf_op jit(solution)/shard_map/ppermute | solution.py:522
  187.3 15.0 %copy-start.1 = (f32[2,512,768]{2,1,0:T(8,128)S(1)}, f32[2,512,768]{2,1,0:T(8,128)}, u32[]{:S(2)}) copy-start(f32[2,512,768]{2,1,0:T(8,128)} %copy-done) | copy-start | bytes 9437188
  199.4 41.1 %collective-permute-start.12 = (bf16[384,1536]{1,0:T(8,128)(2,1)}, bf16[384,1536]{1,0:T(8,128)(2,1)}, u32[]{:S(2)}, u32[]{:S(2)}) collective-permute-start(bf16[384,1536]{1,0:T(8,128)(2,1)} %get-tuple-element.93), channel_id=1, source_target_pairs={{0,32},{32,0},{64,96},{96,64},{1,33},{33,1},{65,97},{97,65},{2,34}... | collective-permute-start | bytes 3538952 | tf_op jit(solution)/shard_map/ppermute | solution.py:479
  201.1 39.3 %collective-permute-start.13 = (bf16[384,1536]{1,0:T(8,128)(2,1)}, bf16[384,1536]{1,0:T(8,128)(2,1)}, u32[]{:S(2)}, u32[]{:S(2)}) collective-permute-start(bf16[384,1536]{1,0:T(8,128)(2,1)} %get-tuple-element.94), channel_id=1, source_target_pairs={{0,96},{96,0},{32,64},{64,32},{1,97},{97,1},{33,65},{65,33},{2,98}... | collective-permute-start | bytes 3538952 | tf_op jit(solution)/shard_map/ppermute | solution.py:479
  211.9 36.2 %all-to-all-start.3 = ((bf16[32,104,256]{2,1,0:T(8,128)(2,1)}), bf16[32,104,256]{2,1,0:T(8,128)(2,1)}, u32[]{:S(2)}, u32[]{:S(2)}) async-start(bf16[32,104,256]{2,1,0:T(8,128)(2,1)} %project.5), calls=%async_computation.3 | async-start | bytes 3407872 | tf_op jit(solution)/shard_map/all_to_all | solution.py:466
  218.7 20.1 %collective-permute-start.14 = (bf16[192,1536]{1,0:T(8,128)(2,1)}, bf16[192,1536]{1,0:T(8,128)(2,1)S(1)}, u32[]{:S(2)}, u32[]{:S(2)}) collective-permute-start(bf16[192,1536]{1,0:T(8,128)(2,1)} %get-tuple-element.96), channel_id=1, source_target_pairs={{0,32},{32,64},{64,96},{96,0},{1,33},{33,65},{65,97},{97,1},{2,34}... | collective-permute-start | bytes 1769480 | tf_op jit(solution)/shard_map/ppermute | solution.py:501
  219.7 20.0 %collective-permute-start.15 = (bf16[192,1536]{1,0:T(8,128)(2,1)}, bf16[192,1536]{1,0:T(8,128)(2,1)S(1)}, u32[]{:S(2)}, u32[]{:S(2)}) collective-permute-start(bf16[192,1536]{1,0:T(8,128)(2,1)} %get-tuple-element.98), channel_id=1, source_target_pairs={{0,96},{32,0},{64,32},{96,64},{1,97},{33,1},{65,33},{97,65},{2,98}... | collective-permute-start | bytes 1769480 | tf_op jit(solution)/shard_map/ppermute | solution.py:501
  238.8 0.8 copy-start.7
  239.7 0.8 copy-start.9
  243.1 14.0 %collective-permute-start.17 = (bf16[192,1536]{1,0:T(8,128)(2,1)}, bf16[192,1536]{1,0:T(8,128)(2,1)}, u32[]{:S(2)}, u32[]{:S(2)}) collective-permute-start(bf16[192,1536]{1,0:T(8,128)(2,1)} %get-tuple-element.135), channel_id=1, source_target_pairs={{0,32},{32,0},{64,96},{96,64},{1,33},{33,1},{65,97},{97,65},{2,34}... | collective-permute-start | bytes 1769480 | tf_op jit(solution)/shard_map/ppermute | solution.py:485
  243.1 14.0 %collective-permute-start.16 = (bf16[192,1536]{1,0:T(8,128)(2,1)}, bf16[192,1536]{1,0:T(8,128)(2,1)}, u32[]{:S(2)}, u32[]{:S(2)}) collective-permute-start(bf16[192,1536]{1,0:T(8,128)(2,1)} %get-tuple-element.136), channel_id=1, source_target_pairs={{0,96},{96,0},{32,64},{64,32},{1,97},{97,1},{33,65},{65,33},{2,98}... | collective-permute-start | bytes 1769480 | tf_op jit(solution)/shard_map/ppermute | solution.py:485
  248.1 1.4 copy-start.5
  249.5 1.0 copy-start.13
  250.6 1.0 copy-start.14
  257.0 3.1 %copy-start.11 = (f32[1024,1]{1,0:T(8,128)}, f32[1024,1]{1,0:T(8,128)S(1)}, u32[]{:S(2)}) copy-start(f32[1024,1]{1,0:T(8,128)S(1)} %get-tuple-element.106) | copy-start | bytes 12292
  260.1 16.6 %collective-permute-start.20 = (bf16[192,1536]{1,0:T(8,128)(2,1)}, bf16[192,1536]{1,0:T(8,128)(2,1)}, u32[]{:S(2)}, u32[]{:S(2)}) collective-permute-start(bf16[192,1536]{1,0:T(8,128)(2,1)} %get-tuple-element.126), channel_id=1, source_target_pairs={{0,96},{32,0},{64,32},{96,64},{1,97},{33,1},{65,33},{97,65},{2,98}... | collective-permute-start | bytes 1769480 | tf_op jit(solution)/shard_map/ppermute | solution.py:501
  262.0 3.5 %copy-start.4 = (bf16[192,1024]{1,0:T(8,128)(2,1)S(1)}, bf16[192,1024]{1,0:T(8,128)(2,1)}, u32[]{:S(2)}) copy-start(bf16[192,1024]{1,0:T(8,128)(2,1)} %get-tuple-element.113.refs_0_) | copy-start | bytes 1179652
  262.0 3.5 %copy-start.16 = (bf16[192,1024]{1,0:T(8,128)(2,1)S(1)}, bf16[192,1024]{1,0:T(8,128)(2,1)}, u32[]{:S(2)}) copy-start(bf16[192,1024]{1,0:T(8,128)(2,1)} %copy-done.15) | copy-start | bytes 1179652
  262.0 3.5 %copy-start.18 = (bf16[192,1024]{1,0:T(8,128)(2,1)S(1)}, bf16[192,1024]{1,0:T(8,128)(2,1)}, u32[]{:S(2)}) copy-start(bf16[192,1024]{1,0:T(8,128)(2,1)} %copy-done.17) | copy-start | bytes 1179652
  262.0 3.5 %copy-start.20 = (bf16[192,1024]{1,0:T(8,128)(2,1)S(1)}, bf16[192,1024]{1,0:T(8,128)(2,1)}, u32[]{:S(2)}) copy-start(bf16[192,1024]{1,0:T(8,128)(2,1)} %copy-done.19) | copy-start | bytes 1179652
  263.2 18.1 %collective-permute-start.19 = (bf16[192,1536]{1,0:T(8,128)(2,1)}, bf16[192,1536]{1,0:T(8,128)(2,1)}, u32[]{:S(2)}, u32[]{:S(2)}) collective-permute-start(bf16[192,1536]{1,0:T(8,128)(2,1)} %get-tuple-element.141), channel_id=1, source_target_pairs={{0,64},{32,96},{64,0},{96,32},{1,65},{33,97},{65,1},{97,33},{2,66}... | collective-permute-start | bytes 1769480 | tf_op jit(solution)/shard_map/ppermute | solution.py:501
  264.1 25.3 %collective-permute-start.18 = (bf16[192,1536]{1,0:T(8,128)(2,1)}, bf16[192,1536]{1,0:T(8,128)(2,1)}, u32[]{:S(2)}, u32[]{:S(2)}) collective-permute-start(bf16[192,1536]{1,0:T(8,128)(2,1)} %get-tuple-element.142), channel_id=1, source_target_pairs={{0,32},{32,64},{64,96},{96,0},{1,33},{33,65},{65,97},{97,1},{2,34}... | collective-permute-start | bytes 1769480 | tf_op jit(solution)/shard_map/ppermute | solution.py:501
  265.5 1.7 copy-start.8
  265.6 1.7 copy-start.10
  267.3 2.0 copy-start.12

commit v4 on v3

--- a/solution.py
+++ b/solution.py
@@ -175,15 +175,14 @@
 
 
 def parts_a_step(parts):
-    return 2 if parts % 2 == 0 else 1
+    return parts // 2 if parts % 2 == 0 else parts
 
 
 def weight_step(acts, got_ref, tail_ref, part, count, keep_ref, send_ref, expert):
     sources = got_ref.shape[0]
     rows = jnp.concatenate([main_rows(got_ref, part + i, expert) for i in range(count)], axis=1)
     more = jnp.concatenate([tail_rows(tail_ref, sources, part + i, expert) for i in range(count)], axis=1)
-    depth = rows.shape[0]
-    total = dot(acts[:, :depth], rows) + dot(acts[:, depth:], more)
+    total = dot(acts, jnp.concatenate([rows, more], axis=0))
     half = total.shape[0] // 2
     size = count * V
     at = pl.multiple_of(pl.program_id(0) * size, size)
@@ -530,11 +529,13 @@
         if c == last:
             proj = project(got[last], down_weight, starts[last], 0, CHUNKS[last], state, True)
             back = exchange(proj)
-            grad_act, grad_prob = finish(codes.reshape(tok * top, 1), prob.reshape(tok * top, 1), act, back)
+            grad_act, grad_prob = finish(code_column, prob_column, act, back)
         if c >= 1:
             came, blocks[c - 1] = barrier((came, blocks[c - 1]))
         if c == last - 1:
-            came, state = barrier((came, state))
+            came, state, code_column, prob_column = barrier(
+                (came, state, codes.reshape(tok * top, 1), prob.reshape(tok * top, 1))
+            )
         passed = forwarded(keep, came)
         last_came = second_round(*passed)
         if c == last:

time: 295 us -> 293 us (level)
  transfers between devices with their start and end apart: 25 -> 25, of which waited for: 12 -> 13; matrix products, arithmetic and copies ran while one was open for 7% -> 6% of each run, Pallas kernels for 20% -> 20%
where the time goes in v4:
time: 293 us; the launch traced here: 290 us
  waiting for transfers between devices  131 us (45%)
  Pallas kernels  67.7 us (23%)
  starting transfers between devices  54 us (18%)
  other arithmetic  19.6 us (7%)
  local copies, waits for them, and re-layouts  14.5 us (5%)
  between operations  3.67 us (1%)
    ppermute x7, waiting for transfers between devices, hop(): return lax.ppermute(sends[d], 'grp', hops[d]) if d else sends[0]  45 us
    all_to_all x4, waiting for transfers between devices, exchange(): return lax.all_to_all(v, 'sp', 0, 0, tiled=True)  44.9 us
    all_to_all x4, starting transfers between devices, exchange(): return lax.all_to_all(v, 'sp', 0, 0, tiled=True)  23.7 us
    pallas_call x3, Pallas kernels, project(): pl.pallas_call(functools.partial(project_kernel, skip, parts, state is no...  23.1 us
    ppermute x6, waiting for transfers between devices, second_round(): return (lax.ppermute(low, 'grp', far), lax.ppermute(high, 'grp', near))  18.4 us
    ppermute x6, waiting for transfers between devices, first_round(): return (lax.ppermute(low, 'grp', near), lax.ppermute(high, 'grp', far))  18 us
    pallas_call x2, Pallas kernels, weight_rest(): pl.pallas_call(weight_kernel, grid=(parts // parts_a_step(parts),), in_sp...  14.5 us
    select_n x6, other arithmetic, wanted(): out.append(jnp.where(which == 0, mine[0], mine[1]))  11.7 us
  transfers between devices with their start and end apart: 25, of which 13 were waited for; matrix products, arithmetic and copies ran while one was open for 6% of the time, Pallas kernels for 20%

profile of v4, /device:TPU:0, one launch (start us, length us, event | category | flops | bytes accessed | tf_op | source)
XLA Modules:
  0.0 290.1 jit_solution(18041942869718200890)
XLA Ops:
  4.0 6.8 %send_first.1 = bf16[32,240,256]{2,1,0:T(8,128)(2,1)} custom-call(s32[8,128]{1,0:T(8,128)S(1)} %bitcast.65, s32[1,1024]{1,0:T(1,128)S(1)} %reshape.82.flat_ref, f32[1,1024]{1,0:T(1,128)S(1)} %reshape.83.prob_ref, bf16[1024,768]{1,0:T(8,128)(2,1)} %bitcast.63, bf16[128,4096]{1,0:T(8,128)(2,1)} %grad_ref.3), custom_call_target="tpu_custom_call" | custom-call | flops 1610612736 | bytes 5505024 | tf_op jit(solution)/shard_map/send_first/pallas_call | solution.py:124
  10.8 7.5 %all-to-all-start = ((bf16[32,240,256]{2,1,0:T(8,128)(2,1)}), bf16[32,240,256]{2,1,0:T(8,128)(2,1)}, u32[]{:S(2)}, u32[]{:S(2)}) async-start(bf16[32,240,256]{2,1,0:T(8,128)(2,1)} %send_first.1), calls=%async_computation | async-start | bytes 7864320 | tf_op jit(solution)/shard_map/all_to_all | solution.py:465
  18.3 5.7 %send_rest.1 = (bf16[32,208,256]{2,1,0:T(8,128)(2,1)}, bf16[32,208,256]{2,1,0:T(8,128)(2,1)}) custom-call(s32[8,128]{1,0:T(8,128)S(1)} %bitcast.66, bf16[128,4096]{1,0:T(8,128)(2,1)} %grad_ref.3), custom_call_target="tpu_custom_call" | custom-call | flops 1073741824 | bytes 9961472 | tf_op jit(solution)/shard_map/send_rest/pallas_call | solution.py:145
  24.0 44.9 %all-to-all-done.got_ref.refs_0_ = bf16[32,240,256]{2,1,0:T(8,128)(2,1)} async-done(((bf16[32,240,256]{2,1,0:T(8,128)(2,1)}), bf16[32,240,256]{2,1,0:T(8,128)(2,1)}, u32[]{:S(2)}, u32[]{:S(2)}) %all-to-all-start) | async-done | bytes 3932192 | tf_op jit(solution)/shard_map/all_to_all | solution.py:465
  68.9 4.1 %all-to-all-start.2 = ((bf16[32,208,256]{2,1,0:T(8,128)(2,1)}), bf16[32,208,256]{2,1,0:T(8,128)(2,1)S(1)}, u32[]{:S(2)}, u32[]{:S(2)}) async-start(bf16[32,208,256]{2,1,0:T(8,128)(2,1)} %get-tuple-element.67), calls=%async_computation.2 | async-start | bytes 6815744 | tf_op jit(solution)/shard_map/all_to_all | solution.py:465
  73.1 5.7 %weight_first.1 = (bf16[2,768,544]{2,1,0:T(8,128)(2,1)}, bf16[2,384,1024]{2,1,0:T(8,128)(2,1)S(1)}, bf16[384,1024]{1,0:T(8,128)(2,1)S(1)}, bf16[384,1024]{1,0:T(8,128)(2,1)S(1)}) custom-call(s32[2,4]{1,0:T(2,128)S(1)} %pad_add_fusion.order_ref, bf16[32,240,256]{2,1,0:T(8,128)(2,1)} %all-to-all-done.got_ref.refs_0_), custom_call_target="tpu_custom_call" | custom-call | flops 1711276032 | bytes 7274496 | tf_op jit(solution)/shard_map/weight_first/pallas_call | solution.py:243
  78.8 2.0 collective-permute-start
  80.8 2.5 collective-permute-start.2
  83.3 15.3 %collective-permute-done = bf16[384,1024]{1,0:T(8,128)(2,1)S(1)} collective-permute-done((bf16[384,1024]{1,0:T(8,128)(2,1)S(1)}, bf16[384,1024]{1,0:T(8,128)(2,1)S(1)}, u32[]{:S(2)}, u32[]{:S(2)}) %collective-permute-start) | collective-permute-done | bytes 786464 | tf_op jit(solution)/shard_map/ppermute | solution.py:478
  98.7 2.7 collective-permute-done.2
  101.3 1.2 fusion.15
  102.5 2.6 collective-permute-start.1
  108.4 5.8 %collective-permute-done.1 = bf16[192,1024]{1,0:T(8,128)(2,1)} collective-permute-done((bf16[192,1024]{1,0:T(8,128)(2,1)}, bf16[192,1024]{1,0:T(8,128)(2,1)}, u32[]{:S(2)}, u32[]{:S(2)}) %collective-permute-start.1) | collective-permute-done | bytes 393248 | tf_op jit(solution)/shard_map/ppermute | solution.py:484
  114.2 1.0 collective-permute-done.3
  115.2 2.8 broadcast_select_fusion.8
  118.0 1.1 broadcast_select_fusion.9
  119.1 2.5 collective-permute-start.4
  121.6 6.6 %weight_rest.2 = (bf16[2,384,1536]{2,1,0:T(8,128)(2,1)S(1)}, bf16[384,1536]{1,0:T(8,128)(2,1)}, bf16[384,1536]{1,0:T(8,128)(2,1)}) custom-call(bf16[2,768,544]{2,1,0:T(8,128)(2,1)} %get-tuple-element.65.acts_ref, bf16[32,208,256]{2,1,0:T(8,128)(2,1)S(1)} %all-to-all-done.2.got_ref.refs_0_), custom_call_target="tpu_custom_call" | custom-call | flops 2566914048 | bytes 9797632 | tf_op jit(solution)/shard_map/weight_rest/pallas_call | solution.py:259
  128.2 1.5 copy-done.2
  130.5 1.0 collective-permute-start.5
  131.5 1.5 collective-permute-start.6
  133.0 6.6 %all-to-all-start.1 = ((bf16[32,208,256]{2,1,0:T(8,128)(2,1)}), bf16[32,208,256]{2,1,0:T(8,128)(2,1)}, u32[]{:S(2)}, u32[]{:S(2)}) async-start(bf16[32,208,256]{2,1,0:T(8,128)(2,1)} %get-tuple-element.66), calls=%async_computation.1 | async-start | bytes 6815744 | tf_op jit(solution)/shard_map/all_to_all | solution.py:465
  139.8 1.5 collective-permute-start.7
  141.3 1.8 collective-permute-start.8
  143.2 6.3 %project.3 = (f32[2,512,768]{2,1,0:T(8,128)S(1)}, f32[2,32,768]{2,1,0:T(8,128)S(1)}) custom-call(bf16[32,240,256]{2,1,0:T(8,128)(2,1)} %all-to-all-done.got_ref.refs_0_, bf16[2,768,4096]{2,1,0:T(8,128)(2,1)} %refs_1_.5), custom_call_target="tpu_custom_call" | custom-call | flops 1711276032 | bytes 13762560 | tf_op jit(solution)/shard_map/project/pallas_call | solution.py:344
  149.4 7.2 %project.4 = (f32[2,512,768]{2,1,0:T(8,128)S(1)}, f32[2,32,768]{2,1,0:T(8,128)S(1)}) custom-call(bf16[32,208,256]{2,1,0:T(8,128)(2,1)S(1)} %all-to-all-done.2.got_ref.refs_0_, bf16[2,768,4096]{2,1,0:T(8,128)(2,1)} %refs_1_.5, f32[2,512,768]{2,1,0:T(8,128)S(1)} %get-tuple-element.84.refs_2_, f32[2,32,768]{2,1,0:T(8,128)S(1)} %get-tuple-element.85.refs_3_), custom_call_target="tpu_custom_call" | custom-call | flops 2566914048 | bytes 14811136 | tf_op jit(solution)/shard_map/project/pallas_call | solution.py:344
  157.4 8.7 %collective-permute-done.7.refs_1_ = bf16[192,1024]{1,0:T(8,128)(2,1)S(1)} collective-permute-done((bf16[192,1024]{1,0:T(8,128)(2,1)}, bf16[192,1024]{1,0:T(8,128)(2,1)S(1)}, u32[]{:S(2)}, u32[]{:S(2)}) %collective-permute-start.7) | collective-permute-done | bytes 393248 | tf_op jit(solution)/shard_map/ppermute | solution.py:500
  166.1 0.8 copy-done.21
  166.9 1.6 fusion.9
  168.4 1.1 collective-permute-start.9
  169.5 11.4 %collective-permute-done.9 = bf16[192,1536]{1,0:T(8,128)(2,1)S(1)} collective-permute-done((bf16[192,1536]{1,0:T(8,128)(2,1)S(1)}, bf16[192,1536]{1,0:T(8,128)(2,1)S(1)}, u32[]{:S(2)}, u32[]{:S(2)}) %collective-permute-start.9) | collective-permute-done | bytes 589856 | tf_op jit(solution)/shard_map/ppermute | solution.py:484
  180.9 2.6 broadcast_select_fusion.1
  183.5 1.1 broadcast_select_fusion.3
  184.7 2.0 collective-permute-start.11
  186.7 7.8 %weight_rest.3 = (bf16[2,384,1536]{2,1,0:T(8,128)(2,1)S(1)}, bf16[384,1536]{1,0:T(8,128)(2,1)}, bf16[384,1536]{1,0:T(8,128)(2,1)}) custom-call(bf16[2,768,544]{2,1,0:T(8,128)(2,1)} %get-tuple-element.65.acts_ref, bf16[32,208,256]{2,1,0:T(8,128)(2,1)} %all-to-all-done.1.got_ref.refs_0_), custom_call_target="tpu_custom_call" | custom-call | flops 2566914048 | bytes 9797632 | tf_op jit(solution)/shard_map/weight_rest/pallas_call | solution.py:259
  194.5 4.2 %collective-permute-done.11.refs_2_ = bf16[192,1536]{1,0:T(8,128)(2,1)S(1)} collective-permute-done((bf16[192,1536]{1,0:T(8,128)(2,1)}, bf16[192,1536]{1,0:T(8,128)(2,1)S(1)}, u32[]{:S(2)}, u32[]{:S(2)}) %collective-permute-start.11) | collective-permute-done | bytes 589856 | tf_op jit(solution)/shard_map/ppermute | solution.py:521
  198.7 0.8 copy-done.7
  199.5 1.4 collective-permute-start.12
  200.9 1.5 collective-permute-start.13
  202.4 9.7 %project.5 = bf16[32,104,256]{2,1,0:T(8,128)(2,1)} custom-call(bf16[32,208,256]{2,1,0:T(8,128)(2,1)} %all-to-all-done.1.got_ref.refs_0_, bf16[2,768,4096]{2,1,0:T(8,128)(2,1)} %refs_1_.5, f32[2,512,768]{2,1,0:T(8,128)S(1)} %copy-done.1, f32[2,32,768]{2,1,0:T(8,128)S(1)} %copy-done.24), custom_call_target="tpu_custom_call" | custom-call | flops 2566914048 | bytes 14811136 | tf_op jit(solution)/shard_map/project/pallas_call | solution.py:344
  212.1 5.5 %all-to-all-start.3 = ((bf16[32,104,256]{2,1,0:T(8,128)(2,1)}), bf16[32,104,256]{2,1,0:T(8,128)(2,1)}, u32[]{:S(2)}, u32[]{:S(2)}) async-start(bf16[32,104,256]{2,1,0:T(8,128)(2,1)} %project.5), calls=%async_computation.3 | async-start | bytes 3407872 | tf_op jit(solution)/shard_map/all_to_all | solution.py:465
  217.6 1.2 collective-permute-start.14
  218.8 2.1 collective-permute-start.15
  220.9 18.1 %collective-permute-done.14.refs_1_ = bf16[192,1536]{1,0:T(8,128)(2,1)S(1)} collective-permute-done((bf16[192,1536]{1,0:T(8,128)(2,1)}, bf16[192,1536]{1,0:T(8,128)(2,1)S(1)}, u32[]{:S(2)}, u32[]{:S(2)}) %collective-permute-start.14) | collective-permute-done | bytes 589856 | tf_op jit(solution)/shard_map/ppermute | solution.py:500
  239.0 0.8 copy-done.9
  239.9 0.8 copy-done.11
  240.7 2.6 fusion.4
  243.3 1.4 collective-permute-start.16
  244.7 1.0 copy.30.code_ref
  245.7 1.0 copy.31.prob_ref
  246.8 1.4 copy-done.5
  248.2 1.0 copy-done.15
  249.2 1.0 copy-done.16
  250.3 5.4 %finish.1 = (bf16[1024,768]{1,0:T(8,128)(2,1)}, f32[1024,1]{1,0:T(8,128)S(1)}) custom-call(s32[1024,1]{1,0:T(8,128)S(1)} %copy-done.15, f32[1024,1]{1,0:T(8,128)S(1)} %copy-done.16, bf16[1024,768]{1,0:T(8,128)(2,1)S(1)} %bitcast.64, bf16[32,104,256]{2,1,0:T(8,128)(2,1)} %all-to-all-done.3.back_ref), custom_call_target="tpu_custom_call" | custom-call | flops 1610612736 | bytes 4849664 | tf_op jit(solution)/shard_map/finish/pallas_call | solution.py:389
  255.9 2.9 %broadcast_select_fusion = (bf16[192,1536]{1,0:T(8,128)(2,1)}, bf16[192,1536]{1,0:T(8,128)(2,1)S(1)}, bf16[192,1536]{1,0:T(8,128)(2,1)S(1)}) fusion(pred[]{:T(512)} %bitcast.15, bf16[192,1536]{1,0:T(8,128)(2,1)} %collective-permute-done.17, bf16[384,1536]{1,0:T(8,128)(2,1)} %collective-permute-done.13, bf16[2,384,1536]{2,1,0:T(8,128)(2,1)S(1)} %get-tuple-element.91, ...), kind=kLoop, calls=%fused_computation.30 | loop fusion | flops 3833856 | bytes 5308417 | tf_op jit(solution)/shard_map/jit(_where)/select_n | solution.py:496
  258.8 2.1 collective-permute-start.20
  260.9 1.1 broadcast_select_fusion.2
  262.7 1.4 collective-permute-start.18
  264.2 1.7 place.3.refs_4_
  265.9 2.0 place.4.refs_4_
  268.9 6.5 %collective-permute-done.20.refs_3_ = bf16[192,1536]{1,0:T(8,128)(2,1)} collective-permute-done((bf16[192,1536]{1,0:T(8,128)(2,1)}, bf16[192,1536]{1,0:T(8,128)(2,1)}, u32[]{:S(2)}, u32[]{:S(2)}) %collective-permute-start.20) | collective-permute-done | bytes 589856 | tf_op jit(solution)/shard_map/ppermute | solution.py:500
  275.4 4.8 %collective-permute-done.19.refs_2_ = bf16[192,1536]{1,0:T(8,128)(2,1)} collective-permute-done((bf16[192,1536]{1,0:T(8,128)(2,1)}, bf16[192,1536]{1,0:T(8,128)(2,1)}, u32[]{:S(2)}, u32[]{:S(2)}) %collective-permute-start.19) | collective-permute-done | bytes 589856 | tf_op jit(solution)/shard_map/ppermute | solution.py:500
  280.1 7.0 %collective-permute-done.18.refs_1_ = bf16[192,1536]{1,0:T(8,128)(2,1)} collective-permute-done((bf16[192,1536]{1,0:T(8,128)(2,1)}, bf16[192,1536]{1,0:T(8,128)(2,1)}, u32[]{:S(2)}, u32[]{:S(2)}) %collective-permute-start.18) | collective-permute-done | bytes 589856 | tf_op jit(solution)/shard_map/ppermute | solution.py:500
  287.1 2.9 place.5
  (83 shorter events, 7.7 us)
Async XLA Ops:
  10.8 58.1 %all-to-all-start = ((bf16[32,240,256]{2,1,0:T(8,128)(2,1)}), bf16[32,240,256]{2,1,0:T(8,128)(2,1)}, u32[]{:S(2)}, u32[]{:S(2)}) async-start(bf16[32,240,256]{2,1,0:T(8,128)(2,1)} %send_first.1), calls=%async_computation | async-start | bytes 7864320 | tf_op jit(solution)/shard_map/all_to_all | solution.py:465
  68.9 50.2 %all-to-all-start.2 = ((bf16[32,208,256]{2,1,0:T(8,128)(2,1)}), bf16[32,208,256]{2,1,0:T(8,128)(2,1)S(1)}, u32[]{:S(2)}, u32[]{:S(2)}) async-start(bf16[32,208,256]{2,1,0:T(8,128)(2,1)} %get-tuple-element.67), calls=%async_computation.2 | async-start | bytes 6815744 | tf_op jit(solution)/shard_map/all_to_all | solution.py:465
  78.8 23.7 %copy-start.6 = (bf16[2,384,1024]{2,1,0:T(8,128)(2,1)}, bf16[2,384,1024]{2,1,0:T(8,128)(2,1)S(1)}, u32[]{:S(2)}) copy-start(bf16[2,384,1024]{2,1,0:T(8,128)(2,1)S(1)} %get-tuple-element.68) | copy-start | bytes 4718596
  78.8 19.9 %collective-permute-start = (bf16[384,1024]{1,0:T(8,128)(2,1)S(1)}, bf16[384,1024]{1,0:T(8,128)(2,1)S(1)}, u32[]{:S(2)}, u32[]{:S(2)}) collective-permute-start(bf16[384,1024]{1,0:T(8,128)(2,1)S(1)} %get-tuple-element.69), channel_id=1, source_target_pairs={{0,32},{32,0},{64,96},{96,64},{1,33},{33,1},{65,97},{97,65},{2,34}... | collective-permute-start | bytes 2359304 | tf_op jit(solution)/shard_map/ppermute | solution.py:478
  80.8 20.5 %collective-permute-start.2 = (bf16[384,1024]{1,0:T(8,128)(2,1)S(1)}, bf16[384,1024]{1,0:T(8,128)(2,1)S(1)}, u32[]{:S(2)}, u32[]{:S(2)}) collective-permute-start(bf16[384,1024]{1,0:T(8,128)(2,1)S(1)} %get-tuple-element.70), channel_id=1, source_target_pairs={{0,96},{96,0},{32,64},{64,32},{1,97},{97,1},{33,65},{65,33},{2,98}... | collective-permute-start | bytes 2359304 | tf_op jit(solution)/shard_map/ppermute | solution.py:478
  98.7 3.9 %copy-start.25 = (bf16[384,1024]{1,0:T(8,128)(2,1)}, bf16[384,1024]{1,0:T(8,128)(2,1)S(1)}, u32[]{:S(2)}) copy-start(bf16[384,1024]{1,0:T(8,128)(2,1)S(1)} %collective-permute-done) | copy-start | bytes 2359300
  101.3 1.2 copy-start.26
  101.3 3.8 %copy-start.27 = (s32[4,32]{1,0:T(4,128)S(1)}, s32[4,32]{1,0:T(4,128)}, u32[]{:S(2)}) copy-start(s32[4,32]{1,0:T(4,128)} %param.10) | copy-start | bytes 1540
  102.5 11.6 %collective-permute-start.1 = (bf16[192,1024]{1,0:T(8,128)(2,1)}, bf16[192,1024]{1,0:T(8,128)(2,1)}, u32[]{:S(2)}, u32[]{:S(2)}) collective-permute-start(bf16[192,1024]{1,0:T(8,128)(2,1)} %get-tuple-element.143), channel_id=1, source_target_pairs={{0,96},{96,0},{32,64},{64,32},{1,97},{97,1},{33,65},{65,33},{2,98}... | collective-permute-start | bytes 1179656 | tf_op jit(solution)/shard_map/ppermute | solution.py:484
  105.1 10.1 %collective-permute-start.3 = (bf16[192,1024]{1,0:T(8,128)(2,1)}, bf16[192,1024]{1,0:T(8,128)(2,1)}, u32[]{:S(2)}, u32[]{:S(2)}) collective-permute-start(bf16[192,1024]{1,0:T(8,128)(2,1)} %get-tuple-element.144), channel_id=1, source_target_pairs={{0,32},{32,0},{64,96},{96,64},{1,33},{33,1},{65,97},{97,65},{2,34}... | collective-permute-start | bytes 1179656 | tf_op jit(solution)/shard_map/ppermute | solution.py:484
  119.1 10.7 %collective-permute-start.4 = (bf16[192,1024]{1,0:T(8,128)(2,1)}, bf16[192,1024]{1,0:T(8,128)(2,1)S(1)}, u32[]{:S(2)}, u32[]{:S(2)}) collective-permute-start(bf16[192,1024]{1,0:T(8,128)(2,1)} %get-tuple-element.75), channel_id=1, source_target_pairs={{0,64},{32,96},{64,0},{96,32},{1,65},{33,97},{65,1},{97,33},{2,66}... | collective-permute-start | bytes 1179656 | tf_op jit(solution)/shard_map/ppermute | solution.py:521
  128.2 1.5 copy-start.2
  129.8 0.8 copy-start.17
  130.5 36.3 %collective-permute-start.5 = (bf16[384,1536]{1,0:T(8,128)(2,1)}, bf16[384,1536]{1,0:T(8,128)(2,1)}, u32[]{:S(2)}, u32[]{:S(2)}) collective-permute-start(bf16[384,1536]{1,0:T(8,128)(2,1)} %get-tuple-element.76), channel_id=1, source_target_pairs={{0,32},{32,0},{64,96},{96,64},{1,33},{33,1},{65,97},{97,65},{2,34}... | collective-permute-start | bytes 3538952 | tf_op jit(solution)/shard_map/ppermute | solution.py:478
  131.5 35.3 %collective-permute-start.6 = (bf16[384,1536]{1,0:T(8,128)(2,1)}, bf16[384,1536]{1,0:T(8,128)(2,1)}, u32[]{:S(2)}, u32[]{:S(2)}) collective-permute-start(bf16[384,1536]{1,0:T(8,128)(2,1)} %get-tuple-element.77), channel_id=1, source_target_pairs={{0,96},{96,0},{32,64},{64,32},{1,97},{97,1},{33,65},{65,33},{2,98}... | collective-permute-start | bytes 3538952 | tf_op jit(solution)/shard_map/ppermute | solution.py:478
  133.0 51.7 %all-to-all-start.1 = ((bf16[32,208,256]{2,1,0:T(8,128)(2,1)}), bf16[32,208,256]{2,1,0:T(8,128)(2,1)}, u32[]{:S(2)}, u32[]{:S(2)}) async-start(bf16[32,208,256]{2,1,0:T(8,128)(2,1)} %get-tuple-element.66), calls=%async_computation.1 | async-start | bytes 6815744 | tf_op jit(solution)/shard_map/all_to_all | solution.py:465
  139.8 26.2 %collective-permute-start.7 = (bf16[192,1024]{1,0:T(8,128)(2,1)}, bf16[192,1024]{1,0:T(8,128)(2,1)S(1)}, u32[]{:S(2)}, u32[]{:S(2)}) collective-permute-start(bf16[192,1024]{1,0:T(8,128)(2,1)} %get-tuple-element.79), channel_id=1, source_target_pairs={{0,32},{32,64},{64,96},{96,0},{1,33},{33,65},{65,97},{97,1},{2,34}... | collective-permute-start | bytes 1179656 | tf_op jit(solution)/shard_map/ppermute | solution.py:500
  141.3 24.7 %collective-permute-start.8 = (bf16[192,1024]{1,0:T(8,128)(2,1)}, bf16[192,1024]{1,0:T(8,128)(2,1)S(1)}, u32[]{:S(2)}, u32[]{:S(2)}) collective-permute-start(bf16[192,1024]{1,0:T(8,128)(2,1)} %get-tuple-element.81), channel_id=1, source_target_pairs={{0,96},{32,0},{64,32},{96,64},{1,97},{33,1},{65,33},{97,65},{2,98}... | collective-permute-start | bytes 1179656 | tf_op jit(solution)/shard_map/ppermute | solution.py:500
  149.4 17.4 %copy-start.3 = (bf16[2,384,1536]{2,1,0:T(8,128)(2,1)S(1)}, bf16[2,384,1536]{2,1,0:T(8,128)(2,1)}, u32[]{:S(2)}) copy-start(bf16[2,384,1536]{2,1,0:T(8,128)(2,1)} %copy-done.2) | copy-start | bytes 7077892
  156.7 0.7 copy-start.23
  157.4 11.1 %copy-start = (f32[2,512,768]{2,1,0:T(8,128)}, f32[2,512,768]{2,1,0:T(8,128)S(1)}, u32[]{:S(2)}) copy-start(f32[2,512,768]{2,1,0:T(8,128)S(1)} %get-tuple-element.105.refs_2_) | copy-start | bytes 9437188
  166.0 2.4 copy-start.19
  166.1 0.8 copy-start.21
  168.4 12.5 %collective-permute-start.9 = (bf16[192,1536]{1,0:T(8,128)(2,1)S(1)}, bf16[192,1536]{1,0:T(8,128)(2,1)S(1)}, u32[]{:S(2)}, u32[]{:S(2)}) collective-permute-start(bf16[192,1536]{1,0:T(8,128)(2,1)S(1)} %get-tuple-element.141), channel_id=1, source_target_pairs={{0,96},{96,0},{32,64},{64,32},{1,97},{97,1},{33,65},{65,33},{2,98}... | collective-permute-start | bytes 1769480 | tf_op jit(solution)/shard_map/ppermute | solution.py:484
  169.5 11.4 %collective-permute-start.10 = (bf16[192,1536]{1,0:T(8,128)(2,1)S(1)}, bf16[192,1536]{1,0:T(8,128)(2,1)S(1)}, u32[]{:S(2)}, u32[]{:S(2)}) collective-permute-start(bf16[192,1536]{1,0:T(8,128)(2,1)S(1)} %get-tuple-element.142), channel_id=1, source_target_pairs={{0,32},{32,0},{64,96},{96,64},{1,33},{33,1},{65,97},{97,65},{2,34}... | collective-permute-start | bytes 1769480 | tf_op jit(solution)/shard_map/ppermute | solution.py:484
  184.7 17.7 %copy-start.24 = (f32[2,32,768]{2,1,0:T(8,128)S(1)}, f32[2,32,768]{2,1,0:T(8,128)}, u32[]{:S(2)}) copy-start(f32[2,32,768]{2,1,0:T(8,128)} %copy-done.23) | copy-start | bytes 589828
  184.7 14.0 %collective-permute-start.11 = (bf16[192,1536]{1,0:T(8,128)(2,1)}, bf16[192,1536]{1,0:T(8,128)(2,1)S(1)}, u32[]{:S(2)}, u32[]{:S(2)}) collective-permute-start(bf16[192,1536]{1,0:T(8,128)(2,1)} %get-tuple-element.94), channel_id=1, source_target_pairs={{0,64},{32,96},{64,0},{96,32},{1,65},{33,97},{65,1},{97,33},{2,66}... | collective-permute-start | bytes 1769480 | tf_op jit(solution)/shard_map/ppermute | solution.py:521
  186.7 15.7 %copy-start.1 = (f32[2,512,768]{2,1,0:T(8,128)S(1)}, f32[2,512,768]{2,1,0:T(8,128)}, u32[]{:S(2)}) copy-start(f32[2,512,768]{2,1,0:T(8,128)} %copy-done) | copy-start | bytes 9437188
  198.7 0.8 copy-start.7
  199.5 41.2 %collective-permute-start.12 = (bf16[384,1536]{1,0:T(8,128)(2,1)}, bf16[384,1536]{1,0:T(8,128)(2,1)}, u32[]{:S(2)}, u32[]{:S(2)}) collective-permute-start(bf16[384,1536]{1,0:T(8,128)(2,1)} %get-tuple-element.95), channel_id=1, source_target_pairs={{0,32},{32,0},{64,96},{96,64},{1,33},{33,1},{65,97},{97,65},{2,34}... | collective-permute-start | bytes 3538952 | tf_op jit(solution)/shard_map/ppermute | solution.py:478
  200.9 39.7 %collective-permute-start.13 = (bf16[384,1536]{1,0:T(8,128)(2,1)}, bf16[384,1536]{1,0:T(8,128)(2,1)}, u32[]{:S(2)}, u32[]{:S(2)}) collective-permute-start(bf16[384,1536]{1,0:T(8,128)(2,1)} %get-tuple-element.96), channel_id=1, source_target_pairs={{0,96},{96,0},{32,64},{64,32},{1,97},{97,1},{33,65},{65,33},{2,98}... | collective-permute-start | bytes 3538952 | tf_op jit(solution)/shard_map/ppermute | solution.py:478
  212.1 34.7 %all-to-all-start.3 = ((bf16[32,104,256]{2,1,0:T(8,128)(2,1)}), bf16[32,104,256]{2,1,0:T(8,128)(2,1)}, u32[]{:S(2)}, u32[]{:S(2)}) async-start(bf16[32,104,256]{2,1,0:T(8,128)(2,1)} %project.5), calls=%async_computation.3 | async-start | bytes 3407872 | tf_op jit(solution)/shard_map/all_to_all | solution.py:465
  217.6 21.4 %collective-permute-start.14 = (bf16[192,1536]{1,0:T(8,128)(2,1)}, bf16[192,1536]{1,0:T(8,128)(2,1)S(1)}, u32[]{:S(2)}, u32[]{:S(2)}) collective-permute-start(bf16[192,1536]{1,0:T(8,128)(2,1)} %get-tuple-element.98), channel_id=1, source_target_pairs={{0,32},{32,64},{64,96},{96,0},{1,33},{33,65},{65,97},{97,1},{2,34}... | collective-permute-start | bytes 1769480 | tf_op jit(solution)/shard_map/ppermute | solution.py:500
  218.8 21.0 %collective-permute-start.15 = (bf16[192,1536]{1,0:T(8,128)(2,1)}, bf16[192,1536]{1,0:T(8,128)(2,1)S(1)}, u32[]{:S(2)}, u32[]{:S(2)}) collective-permute-start(bf16[192,1536]{1,0:T(8,128)(2,1)} %get-tuple-element.100), channel_id=1, source_target_pairs={{0,96},{32,0},{64,32},{96,64},{1,97},{33,1},{65,33},{97,65},{2,98}... | collective-permute-start | bytes 1769480 | tf_op jit(solution)/shard_map/ppermute | solution.py:500
  239.0 0.8 copy-start.9
  239.8 0.8 copy-start.11
  243.3 12.4 %collective-permute-start.17 = (bf16[192,1536]{1,0:T(8,128)(2,1)}, bf16[192,1536]{1,0:T(8,128)(2,1)}, u32[]{:S(2)}, u32[]{:S(2)}) collective-permute-start(bf16[192,1536]{1,0:T(8,128)(2,1)} %get-tuple-element.139), channel_id=1, source_target_pairs={{0,32},{32,0},{64,96},{96,64},{1,33},{33,1},{65,97},{97,65},{2,34}... | collective-permute-start | bytes 1769480 | tf_op jit(solution)/shard_map/ppermute | solution.py:484
  243.3 12.6 %collective-permute-start.16 = (bf16[192,1536]{1,0:T(8,128)(2,1)}, bf16[192,1536]{1,0:T(8,128)(2,1)}, u32[]{:S(2)}, u32[]{:S(2)}) collective-permute-start(bf16[192,1536]{1,0:T(8,128)(2,1)} %get-tuple-element.140), channel_id=1, source_target_pairs={{0,96},{96,0},{32,64},{64,32},{1,97},{97,1},{33,65},{65,33},{2,98}... | collective-permute-start | bytes 1769480 | tf_op jit(solution)/shard_map/ppermute | solution.py:484
  246.8 1.4 copy-start.5
  248.2 1.0 copy-start.15
  249.2 1.0 copy-start.16
  255.7 3.1 %copy-start.13 = (f32[1024,1]{1,0:T(8,128)}, f32[1024,1]{1,0:T(8,128)S(1)}, u32[]{:S(2)}) copy-start(f32[1024,1]{1,0:T(8,128)S(1)} %get-tuple-element.110) | copy-start | bytes 12292
  258.8 16.6 %collective-permute-start.20 = (bf16[192,1536]{1,0:T(8,128)(2,1)}, bf16[192,1536]{1,0:T(8,128)(2,1)}, u32[]{:S(2)}, u32[]{:S(2)}) collective-permute-start(bf16[192,1536]{1,0:T(8,128)(2,1)} %get-tuple-element.130), channel_id=1, source_target_pairs={{0,96},{32,0},{64,32},{96,64},{1,97},{33,1},{65,33},{97,65},{2,98}... | collective-permute-start | bytes 1769480 | tf_op jit(solution)/shard_map/ppermute | solution.py:500
  260.9 3.2 %copy-start.4 = (bf16[192,1024]{1,0:T(8,128)(2,1)S(1)}, bf16[192,1024]{1,0:T(8,128)(2,1)}, u32[]{:S(2)}) copy-start(bf16[192,1024]{1,0:T(8,128)(2,1)} %get-tuple-element.117.refs_0_) | copy-start | bytes 1179652
  260.9 3.2 %copy-start.18 = (bf16[192,1024]{1,0:T(8,128)(2,1)S(1)}, bf16[192,1024]{1,0:T(8,128)(2,1)}, u32[]{:S(2)}) copy-start(bf16[192,1024]{1,0:T(8,128)(2,1)} %copy-done.17) | copy-start | bytes 1179652
  260.9 3.2 %copy-start.20 = (bf16[192,1024]{1,0:T(8,128)(2,1)S(1)}, bf16[192,1024]{1,0:T(8,128)(2,1)}, u32[]{:S(2)}) copy-start(bf16[192,1024]{1,0:T(8,128)(2,1)} %copy-done.19) | copy-start | bytes 1179652
  260.9 3.2 %copy-start.22 = (bf16[192,1024]{1,0:T(8,128)(2,1)S(1)}, bf16[192,1024]{1,0:T(8,128)(2,1)}, u32[]{:S(2)}) copy-start(bf16[192,1024]{1,0:T(8,128)(2,1)} %copy-done.21) | copy-start | bytes 1179652
  262.1 18.1 %collective-permute-start.19 = (bf16[192,1536]{1,0:T(8,128)(2,1)}, bf16[192,1536]{1,0:T(8,128)(2,1)}, u32[]{:S(2)}, u32[]{:S(2)}) collective-permute-start(bf16[192,1536]{1,0:T(8,128)(2,1)} %get-tuple-element.145), channel_id=1, source_target_pairs={{0,64},{32,96},{64,0},{96,32},{1,65},{33,97},{65,1},{97,33},{2,66}... | collective-permute-start | bytes 1769480 | tf_op jit(solution)/shard_map/ppermute | solution.py:500
  262.7 24.4 %collective-permute-start.18 = (bf16[192,1536]{1,0:T(8,128)(2,1)}, bf16[192,1536]{1,0:T(8,128)(2,1)}, u32[]{:S(2)}, u32[]{:S(2)}) collective-permute-start(bf16[192,1536]{1,0:T(8,128)(2,1)} %get-tuple-element.146), channel_id=1, source_target_pairs={{0,32},{32,64},{64,96},{96,0},{1,33},{33,65},{65,97},{97,1},{2,34}... | collective-permute-start | bytes 1769480 | tf_op jit(solution)/shard_map/ppermute | solution.py:500
  264.1 1.8 copy-start.8
  264.2 1.8 copy-start.10
  264.2 1.8 copy-start.12
  265.9 2.0 copy-start.14

commit v5 on v4

--- a/solution.py
+++ b/solution.py
@@ -398,8 +398,8 @@
     )(code, prob, act, back)
 
 
-def place_kernel(column, sources_ref, *refs):
-    blocks, (out_ref, sems) = refs[:4], refs[-2:]
+def place_kernel(column, count, sources_ref, *refs):
+    blocks, (out_ref, sems) = refs[:count], refs[-2:]
     copies = []
     for d, block in enumerate(blocks):
         rows, size = block.shape
@@ -418,7 +418,7 @@
     args = [sources, *blocks] + ([] if first else [own])
     own_spec = pl.BlockSpec(memory_space=pltpu.HBM)
     return pl.pallas_call(
-        functools.partial(place_kernel, column),
+        functools.partial(place_kernel, column, len(blocks)),
         in_specs=[pl.BlockSpec(memory_space=pltpu.SMEM)] + [resident()] * len(blocks) + [own_spec] * (not first),
         out_specs=own_spec,
         out_shape=pltpu.HBM((hidden, width), BF16),
@@ -543,8 +543,11 @@
         sends[c] = wanted(completed(keep, came, last_came))
     blocks[last] = [hop(sends[last], d) for d in range(groups)]
     own = None
-    for c in range(last + 1):
+    for c in range(last):
         own = place(sources, blocks[c], own, hidden, width, starts[c] * V)
+    for early in ((0, 2, 3), (1,)):
+        where = jnp.stack([sources[d] for d in early])
+        own = place(where, [blocks[last][d] for d in early], own, hidden, width, starts[last] * V)
     return (
         grad_act.reshape(tok, top, hidden),
         grad_prob.reshape(tok, top),

time: 293 us -> 292 us (level)
    pallas_call x3 -> x4, Pallas kernels: 6.56 us -> 8.07 us  [place(): pl.pallas_call(functools.partial(place_kernel, column, len(blocks)), in_s...]
    unnamed x57 -> x53, local copies, waits for them, and re-layouts: 10.4 us -> 9.6 us
  transfers between devices with their start and end apart: 25 -> 25, of which waited for: 13 -> 12; matrix products, arithmetic and copies ran while one was open for 6% -> 6% of each run, Pallas kernels for 20% -> 21%
where the time goes in v5:
time: 292 us; the launch traced here: 290 us
  waiting for transfers between devices  129 us (44%)
  Pallas kernels  69.3 us (24%)
  starting transfers between devices  54.1 us (19%)
  other arithmetic  19.7 us (7%)
  local copies, waits for them, and re-layouts  13.7 us (5%)
  between operations  3.5 us (1%)
    all_to_all x4, waiting for transfers between devices, exchange(): return lax.all_to_all(v, 'sp', 0, 0, tiled=True)  44.9 us
    ppermute x7, waiting for transfers between devices, hop(): return lax.ppermute(sends[d], 'grp', hops[d]) if d else sends[0]  43.1 us
    all_to_all x4, starting transfers between devices, exchange(): return lax.all_to_all(v, 'sp', 0, 0, tiled=True)  24.4 us
    pallas_call x3, Pallas kernels, project(): pl.pallas_call(functools.partial(project_kernel, skip, parts, state is no...  23.1 us
    ppermute x6, waiting for transfers between devices, second_round(): return (lax.ppermute(low, 'grp', far), lax.ppermute(high, 'grp', near))  19.4 us
    ppermute x6, waiting for transfers between devices, first_round(): return (lax.ppermute(low, 'grp', near), lax.ppermute(high, 'grp', far))  18 us
    pallas_call x2, Pallas kernels, weight_rest(): pl.pallas_call(weight_kernel, grid=(parts // parts_a_step(parts),), in_sp...  14.5 us
    select_n x6, other arithmetic, wanted(): out.append(jnp.where(which == 0, mine[0], mine[1]))  11.7 us
  transfers between devices with their start and end apart: 25, of which 12 were waited for; matrix products, arithmetic and copies ran while one was open for 6% of the time, Pallas kernels for 21%

profile of v5, /device:TPU:0, one launch (start us, length us, event | category | flops | bytes accessed | tf_op | source)
XLA Modules:
  0.0 289.9 jit_solution(14637572081372897608)
XLA Ops:
  3.2 0.8 copy.28
  4.0 6.8 %send_first.1 = bf16[32,240,256]{2,1,0:T(8,128)(2,1)} custom-call(s32[8,128]{1,0:T(8,128)S(1)} %bitcast.65, s32[1,1024]{1,0:T(1,128)S(1)} %reshape.82.flat_ref, f32[1,1024]{1,0:T(1,128)S(1)} %reshape.83.prob_ref, bf16[1024,768]{1,0:T(8,128)(2,1)} %bitcast.63, bf16[128,4096]{1,0:T(8,128)(2,1)} %grad_ref.3), custom_call_target="tpu_custom_call" | custom-call | flops 1610612736 | bytes 5505024 | tf_op jit(solution)/shard_map/send_first/pallas_call | solution.py:124
  10.8 7.5 %all-to-all-start = ((bf16[32,240,256]{2,1,0:T(8,128)(2,1)}), bf16[32,240,256]{2,1,0:T(8,128)(2,1)}, u32[]{:S(2)}, u32[]{:S(2)}) async-start(bf16[32,240,256]{2,1,0:T(8,128)(2,1)} %send_first.1), calls=%async_computation | async-start | bytes 7864320 | tf_op jit(solution)/shard_map/all_to_all | solution.py:465
  18.3 5.7 %send_rest.1 = (bf16[32,208,256]{2,1,0:T(8,128)(2,1)}, bf16[32,208,256]{2,1,0:T(8,128)(2,1)}) custom-call(s32[8,128]{1,0:T(8,128)S(1)} %bitcast.66, bf16[128,4096]{1,0:T(8,128)(2,1)} %grad_ref.3), custom_call_target="tpu_custom_call" | custom-call | flops 1073741824 | bytes 9961472 | tf_op jit(solution)/shard_map/send_rest/pallas_call | solution.py:145
  24.0 44.9 %all-to-all-done.got_ref.refs_0_ = bf16[32,240,256]{2,1,0:T(8,128)(2,1)} async-done(((bf16[32,240,256]{2,1,0:T(8,128)(2,1)}), bf16[32,240,256]{2,1,0:T(8,128)(2,1)}, u32[]{:S(2)}, u32[]{:S(2)}) %all-to-all-start) | async-done | bytes 3932192 | tf_op jit(solution)/shard_map/all_to_all | solution.py:465
  68.9 4.1 %all-to-all-start.2 = ((bf16[32,208,256]{2,1,0:T(8,128)(2,1)}), bf16[32,208,256]{2,1,0:T(8,128)(2,1)S(1)}, u32[]{:S(2)}, u32[]{:S(2)}) async-start(bf16[32,208,256]{2,1,0:T(8,128)(2,1)} %get-tuple-element.67), calls=%async_computation.2 | async-start | bytes 6815744 | tf_op jit(solution)/shard_map/all_to_all | solution.py:465
  73.1 5.7 %weight_first.1 = (bf16[2,768,544]{2,1,0:T(8,128)(2,1)}, bf16[2,384,1024]{2,1,0:T(8,128)(2,1)S(1)}, bf16[384,1024]{1,0:T(8,128)(2,1)S(1)}, bf16[384,1024]{1,0:T(8,128)(2,1)S(1)}) custom-call(s32[2,4]{1,0:T(2,128)S(1)} %pad_add_fusion.order_ref, bf16[32,240,256]{2,1,0:T(8,128)(2,1)} %all-to-all-done.got_ref.refs_0_), custom_call_target="tpu_custom_call" | custom-call | flops 1711276032 | bytes 7274496 | tf_op jit(solution)/shard_map/weight_first/pallas_call | solution.py:243
  78.8 2.0 collective-permute-start
  80.8 2.5 collective-permute-start.2
  83.3 15.3 %collective-permute-done = bf16[384,1024]{1,0:T(8,128)(2,1)S(1)} collective-permute-done((bf16[384,1024]{1,0:T(8,128)(2,1)S(1)}, bf16[384,1024]{1,0:T(8,128)(2,1)S(1)}, u32[]{:S(2)}, u32[]{:S(2)}) %collective-permute-start) | collective-permute-done | bytes 786464 | tf_op jit(solution)/shard_map/ppermute | solution.py:478
  98.7 2.7 collective-permute-done.2
  101.3 1.2 fusion.15
  102.5 2.6 collective-permute-start.1
  108.3 5.9 %collective-permute-done.1 = bf16[192,1024]{1,0:T(8,128)(2,1)} collective-permute-done((bf16[192,1024]{1,0:T(8,128)(2,1)}, bf16[192,1024]{1,0:T(8,128)(2,1)}, u32[]{:S(2)}, u32[]{:S(2)}) %collective-permute-start.1) | collective-permute-done | bytes 393248 | tf_op jit(solution)/shard_map/ppermute | solution.py:484
  114.2 1.0 collective-permute-done.3
  115.2 2.8 broadcast_select_fusion.8
  118.0 1.1 broadcast_select_fusion.9
  119.1 2.5 collective-permute-start.4
  121.6 6.6 %weight_rest.2 = (bf16[2,384,1536]{2,1,0:T(8,128)(2,1)S(1)}, bf16[384,1536]{1,0:T(8,128)(2,1)}, bf16[384,1536]{1,0:T(8,128)(2,1)}) custom-call(bf16[2,768,544]{2,1,0:T(8,128)(2,1)} %get-tuple-element.65.acts_ref, bf16[32,208,256]{2,1,0:T(8,128)(2,1)S(1)} %all-to-all-done.2.got_ref.refs_0_), custom_call_target="tpu_custom_call" | custom-call | flops 2566914048 | bytes 9797632 | tf_op jit(solution)/shard_map/weight_rest/pallas_call | solution.py:259
  128.3 1.5 copy-done.2
  130.5 1.0 collective-permute-start.5
  131.5 1.5 collective-permute-start.6
  133.0 6.6 %all-to-all-start.1 = ((bf16[32,208,256]{2,1,0:T(8,128)(2,1)}), bf16[32,208,256]{2,1,0:T(8,128)(2,1)}, u32[]{:S(2)}, u32[]{:S(2)}) async-start(bf16[32,208,256]{2,1,0:T(8,128)(2,1)} %get-tuple-element.66), calls=%async_computation.1 | async-start | bytes 6815744 | tf_op jit(solution)/shard_map/all_to_all | solution.py:465
  139.8 1.5 collective-permute-start.7
  141.3 1.8 collective-permute-start.8
  143.1 6.3 %project.3 = (f32[2,512,768]{2,1,0:T(8,128)S(1)}, f32[2,32,768]{2,1,0:T(8,128)S(1)}) custom-call(bf16[32,240,256]{2,1,0:T(8,128)(2,1)} %all-to-all-done.got_ref.refs_0_, bf16[2,768,4096]{2,1,0:T(8,128)(2,1)} %refs_1_.5), custom_call_target="tpu_custom_call" | custom-call | flops 1711276032 | bytes 13762560 | tf_op jit(solution)/shard_map/project/pallas_call | solution.py:344
  149.4 7.2 %project.4 = (f32[2,512,768]{2,1,0:T(8,128)S(1)}, f32[2,32,768]{2,1,0:T(8,128)S(1)}) custom-call(bf16[32,208,256]{2,1,0:T(8,128)(2,1)S(1)} %all-to-all-done.2.got_ref.refs_0_, bf16[2,768,4096]{2,1,0:T(8,128)(2,1)} %refs_1_.5, f32[2,512,768]{2,1,0:T(8,128)S(1)} %get-tuple-element.84.refs_2_, f32[2,32,768]{2,1,0:T(8,128)S(1)} %get-tuple-element.85.refs_3_), custom_call_target="tpu_custom_call" | custom-call | flops 2566914048 | bytes 14811136 | tf_op jit(solution)/shard_map/project/pallas_call | solution.py:344
  157.3 8.7 %collective-permute-done.7.refs_1_ = bf16[192,1024]{1,0:T(8,128)(2,1)S(1)} collective-permute-done((bf16[192,1024]{1,0:T(8,128)(2,1)}, bf16[192,1024]{1,0:T(8,128)(2,1)S(1)}, u32[]{:S(2)}, u32[]{:S(2)}) %collective-permute-start.7) | collective-permute-done | bytes 393248 | tf_op jit(solution)/shard_map/ppermute | solution.py:500
  166.9 1.6 fusion.9
  168.4 1.1 collective-permute-start.9
  169.5 11.4 %collective-permute-done.9 = bf16[192,1536]{1,0:T(8,128)(2,1)S(1)} collective-permute-done((bf16[192,1536]{1,0:T(8,128)(2,1)S(1)}, bf16[192,1536]{1,0:T(8,128)(2,1)S(1)}, u32[]{:S(2)}, u32[]{:S(2)}) %collective-permute-start.9) | collective-permute-done | bytes 589856 | tf_op jit(solution)/shard_map/ppermute | solution.py:484
  180.9 2.6 broadcast_select_fusion.1
  183.5 1.1 broadcast_select_fusion.3
  184.7 2.0 collective-permute-start.11
  186.7 7.8 %weight_rest.3 = (bf16[2,384,1536]{2,1,0:T(8,128)(2,1)S(1)}, bf16[384,1536]{1,0:T(8,128)(2,1)}, bf16[384,1536]{1,0:T(8,128)(2,1)}) custom-call(bf16[2,768,544]{2,1,0:T(8,128)(2,1)} %get-tuple-element.65.acts_ref, bf16[32,208,256]{2,1,0:T(8,128)(2,1)} %all-to-all-done.1.got_ref.refs_0_), custom_call_target="tpu_custom_call" | custom-call | flops 2566914048 | bytes 9797632 | tf_op jit(solution)/shard_map/weight_rest/pallas_call | solution.py:259
  194.5 4.1 %collective-permute-done.11.refs_2_ = bf16[192,1536]{1,0:T(8,128)(2,1)S(1)} collective-permute-done((bf16[192,1536]{1,0:T(8,128)(2,1)}, bf16[192,1536]{1,0:T(8,128)(2,1)S(1)}, u32[]{:S(2)}, u32[]{:S(2)}) %collective-permute-start.11) | collective-permute-done | bytes 589856 | tf_op jit(solution)/shard_map/ppermute | solution.py:521
  198.7 1.8 collective-permute-start.12
  200.5 1.1 collective-permute-start.13
  201.6 9.7 %project.5 = bf16[32,104,256]{2,1,0:T(8,128)(2,1)} custom-call(bf16[32,208,256]{2,1,0:T(8,128)(2,1)} %all-to-all-done.1.got_ref.refs_0_, bf16[2,768,4096]{2,1,0:T(8,128)(2,1)} %refs_1_.5, f32[2,512,768]{2,1,0:T(8,128)S(1)} %copy-done.1, f32[2,32,768]{2,1,0:T(8,128)S(1)} %copy-done.22), custom_call_target="tpu_custom_call" | custom-call | flops 2566914048 | bytes 14811136 | tf_op jit(solution)/shard_map/project/pallas_call | solution.py:344
  211.3 6.2 %all-to-all-start.3 = ((bf16[32,104,256]{2,1,0:T(8,128)(2,1)}), bf16[32,104,256]{2,1,0:T(8,128)(2,1)}, u32[]{:S(2)}, u32[]{:S(2)}) async-start(bf16[32,104,256]{2,1,0:T(8,128)(2,1)} %project.5), calls=%async_computation.3 | async-start | bytes 3407872 | tf_op jit(solution)/shard_map/all_to_all | solution.py:465
  217.5 1.3 collective-permute-start.14
  218.9 2.0 collective-permute-start.15
  220.8 17.3 %collective-permute-done.14.refs_1_ = bf16[192,1536]{1,0:T(8,128)(2,1)S(1)} collective-permute-done((bf16[192,1536]{1,0:T(8,128)(2,1)}, bf16[192,1536]{1,0:T(8,128)(2,1)S(1)}, u32[]{:S(2)}, u32[]{:S(2)}) %collective-permute-start.14) | collective-permute-done | bytes 589856 | tf_op jit(solution)/shard_map/ppermute | solution.py:500
  238.2 0.8 copy-done.7
  239.0 0.8 copy-done.9
  239.8 2.6 fusion.4
  242.4 1.4 collective-permute-start.16
  243.8 1.0 copy.31.code_ref
  244.8 1.1 copy.32.prob_ref
  245.9 1.4 copy-done.5
  247.3 1.0 copy-done.13
  248.4 1.0 copy-done.14
  249.4 5.4 %finish.1 = (bf16[1024,768]{1,0:T(8,128)(2,1)}, f32[1024,1]{1,0:T(8,128)S(1)}) custom-call(s32[1024,1]{1,0:T(8,128)S(1)} %copy-done.13, f32[1024,1]{1,0:T(8,128)S(1)} %copy-done.14, bf16[1024,768]{1,0:T(8,128)(2,1)S(1)} %bitcast.64, bf16[32,104,256]{2,1,0:T(8,128)(2,1)} %all-to-all-done.3.back_ref), custom_call_target="tpu_custom_call" | custom-call | flops 1610612736 | bytes 4849664 | tf_op jit(solution)/shard_map/finish/pallas_call | solution.py:389
  254.8 1.0 collective-permute-done.16
  255.8 2.9 %broadcast_select_fusion = (bf16[192,1536]{1,0:T(8,128)(2,1)}, bf16[192,1536]{1,0:T(8,128)(2,1)S(1)}, bf16[192,1536]{1,0:T(8,128)(2,1)S(1)}) fusion(pred[]{:T(512)} %bitcast.15, bf16[192,1536]{1,0:T(8,128)(2,1)} %collective-permute-done.17, bf16[384,1536]{1,0:T(8,128)(2,1)} %collective-permute-done.13, bf16[2,384,1536]{2,1,0:T(8,128)(2,1)S(1)} %get-tuple-element.91, ...), kind=kLoop, calls=%fused_computation.30 | loop fusion | flops 3833856 | bytes 5308417 | tf_op jit(solution)/shard_map/jit(_where)/select_n | solution.py:496
  258.7 2.1 collective-permute-start.20
  260.9 1.2 broadcast_select_fusion.2
  262.5 0.9 collective-permute-start.18
  263.6 1.7 place.4.refs_4_
  265.4 2.0 place.5.refs_3_
  268.3 14.7 %collective-permute-done.20.refs_2_ = bf16[192,1536]{1,0:T(8,128)(2,1)} collective-permute-done((bf16[192,1536]{1,0:T(8,128)(2,1)}, bf16[192,1536]{1,0:T(8,128)(2,1)}, u32[]{:S(2)}, u32[]{:S(2)}) %collective-permute-start.20) | collective-permute-done | bytes 589856 | tf_op jit(solution)/shard_map/ppermute | solution.py:500
  283.0 2.5 place.6.refs_1_
  285.5 2.4 collective-permute-done.18.refs_0_
  287.9 1.9 place.7
  (81 shorter events, 7.5 us)
Async XLA Ops:
  10.8 58.1 %all-to-all-start = ((bf16[32,240,256]{2,1,0:T(8,128)(2,1)}), bf16[32,240,256]{2,1,0:T(8,128)(2,1)}, u32[]{:S(2)}, u32[]{:S(2)}) async-start(bf16[32,240,256]{2,1,0:T(8,128)(2,1)} %send_first.1), calls=%async_computation | async-start | bytes 7864320 | tf_op jit(solution)/shard_map/all_to_all | solution.py:465
  68.9 50.2 %all-to-all-start.2 = ((bf16[32,208,256]{2,1,0:T(8,128)(2,1)}), bf16[32,208,256]{2,1,0:T(8,128)(2,1)S(1)}, u32[]{:S(2)}, u32[]{:S(2)}) async-start(bf16[32,208,256]{2,1,0:T(8,128)(2,1)} %get-tuple-element.67), calls=%async_computation.2 | async-start | bytes 6815744 | tf_op jit(solution)/shard_map/all_to_all | solution.py:465
  78.8 23.7 %copy-start.6 = (bf16[2,384,1024]{2,1,0:T(8,128)(2,1)}, bf16[2,384,1024]{2,1,0:T(8,128)(2,1)S(1)}, u32[]{:S(2)}) copy-start(bf16[2,384,1024]{2,1,0:T(8,128)(2,1)S(1)} %get-tuple-element.68) | copy-start | bytes 4718596
  78.8 19.9 %collective-permute-start = (bf16[384,1024]{1,0:T(8,128)(2,1)S(1)}, bf16[384,1024]{1,0:T(8,128)(2,1)S(1)}, u32[]{:S(2)}, u32[]{:S(2)}) collective-permute-start(bf16[384,1024]{1,0:T(8,128)(2,1)S(1)} %get-tuple-element.69), channel_id=1, source_target_pairs={{0,32},{32,0},{64,96},{96,64},{1,33},{33,1},{65,97},{97,65},{2,34}... | collective-permute-start | bytes 2359304 | tf_op jit(solution)/shard_map/ppermute | solution.py:478
  80.8 20.5 %collective-permute-start.2 = (bf16[384,1024]{1,0:T(8,128)(2,1)S(1)}, bf16[384,1024]{1,0:T(8,128)(2,1)S(1)}, u32[]{:S(2)}, u32[]{:S(2)}) collective-permute-start(bf16[384,1024]{1,0:T(8,128)(2,1)S(1)} %get-tuple-element.70), channel_id=1, source_target_pairs={{0,96},{96,0},{32,64},{64,32},{1,97},{97,1},{33,65},{65,33},{2,98}... | collective-permute-start | bytes 2359304 | tf_op jit(solution)/shard_map/ppermute | solution.py:478
  98.7 3.9 %copy-start.23 = (bf16[384,1024]{1,0:T(8,128)(2,1)}, bf16[384,1024]{1,0:T(8,128)(2,1)S(1)}, u32[]{:S(2)}) copy-start(bf16[384,1024]{1,0:T(8,128)(2,1)S(1)} %collective-permute-done) | copy-start | bytes 2359300
  101.3 1.2 copy-start.24
  101.3 3.8 %copy-start.25 = (s32[4,32]{1,0:T(4,128)S(1)}, s32[4,32]{1,0:T(4,128)}, u32[]{:S(2)}) copy-start(s32[4,32]{1,0:T(4,128)} %param.10) | copy-start | bytes 1540
  102.5 11.6 %collective-permute-start.1 = (bf16[192,1024]{1,0:T(8,128)(2,1)}, bf16[192,1024]{1,0:T(8,128)(2,1)}, u32[]{:S(2)}, u32[]{:S(2)}) collective-permute-start(bf16[192,1024]{1,0:T(8,128)(2,1)} %get-tuple-element.143), channel_id=1, source_target_pairs={{0,96},{96,0},{32,64},{64,32},{1,97},{97,1},{33,65},{65,33},{2,98}... | collective-permute-start | bytes 1179656 | tf_op jit(solution)/shard_map/ppermute | solution.py:484
  105.1 10.1 %collective-permute-start.3 = (bf16[192,1024]{1,0:T(8,128)(2,1)}, bf16[192,1024]{1,0:T(8,128)(2,1)}, u32[]{:S(2)}, u32[]{:S(2)}) collective-permute-start(bf16[192,1024]{1,0:T(8,128)(2,1)} %get-tuple-element.144), channel_id=1, source_target_pairs={{0,32},{32,0},{64,96},{96,64},{1,33},{33,1},{65,97},{97,65},{2,34}... | collective-permute-start | bytes 1179656 | tf_op jit(solution)/shard_map/ppermute | solution.py:484
  119.1 10.7 %collective-permute-start.4 = (bf16[192,1024]{1,0:T(8,128)(2,1)}, bf16[192,1024]{1,0:T(8,128)(2,1)S(1)}, u32[]{:S(2)}, u32[]{:S(2)}) collective-permute-start(bf16[192,1024]{1,0:T(8,128)(2,1)} %get-tuple-element.75), channel_id=1, source_target_pairs={{0,64},{32,96},{64,0},{96,32},{1,65},{33,97},{65,1},{97,33},{2,66}... | collective-permute-start | bytes 1179656 | tf_op jit(solution)/shard_map/ppermute | solution.py:521
  128.3 1.5 copy-start.2
  129.8 0.7 copy-start.15
  130.5 36.3 %collective-permute-start.5 = (bf16[384,1536]{1,0:T(8,128)(2,1)}, bf16[384,1536]{1,0:T(8,128)(2,1)}, u32[]{:S(2)}, u32[]{:S(2)}) collective-permute-start(bf16[384,1536]{1,0:T(8,128)(2,1)} %get-tuple-element.76), channel_id=1, source_target_pairs={{0,32},{32,0},{64,96},{96,64},{1,33},{33,1},{65,97},{97,65},{2,34}... | collective-permute-start | bytes 3538952 | tf_op jit(solution)/shard_map/ppermute | solution.py:478
  131.5 35.3 %collective-permute-start.6 = (bf16[384,1536]{1,0:T(8,128)(2,1)}, bf16[384,1536]{1,0:T(8,128)(2,1)}, u32[]{:S(2)}, u32[]{:S(2)}) collective-permute-start(bf16[384,1536]{1,0:T(8,128)(2,1)} %get-tuple-element.77), channel_id=1, source_target_pairs={{0,96},{96,0},{32,64},{64,32},{1,97},{97,1},{33,65},{65,33},{2,98}... | collective-permute-start | bytes 3538952 | tf_op jit(solution)/shard_map/ppermute | solution.py:478
  133.0 51.7 %all-to-all-start.1 = ((bf16[32,208,256]{2,1,0:T(8,128)(2,1)}), bf16[32,208,256]{2,1,0:T(8,128)(2,1)}, u32[]{:S(2)}, u32[]{:S(2)}) async-start(bf16[32,208,256]{2,1,0:T(8,128)(2,1)} %get-tuple-element.66), calls=%async_computation.1 | async-start | bytes 6815744 | tf_op jit(solution)/shard_map/all_to_all | solution.py:465
  139.8 26.2 %collective-permute-start.7 = (bf16[192,1024]{1,0:T(8,128)(2,1)}, bf16[192,1024]{1,0:T(8,128)(2,1)S(1)}, u32[]{:S(2)}, u32[]{:S(2)}) collective-permute-start(bf16[192,1024]{1,0:T(8,128)(2,1)} %get-tuple-element.79), channel_id=1, source_target_pairs={{0,32},{32,64},{64,96},{96,0},{1,33},{33,65},{65,97},{97,1},{2,34}... | collective-permute-start | bytes 1179656 | tf_op jit(solution)/shard_map/ppermute | solution.py:500
  141.3 24.8 %collective-permute-start.8 = (bf16[192,1024]{1,0:T(8,128)(2,1)}, bf16[192,1024]{1,0:T(8,128)(2,1)S(1)}, u32[]{:S(2)}, u32[]{:S(2)}) collective-permute-start(bf16[192,1024]{1,0:T(8,128)(2,1)} %get-tuple-element.81), channel_id=1, source_target_pairs={{0,96},{32,0},{64,32},{96,64},{1,97},{33,1},{65,33},{97,65},{2,98}... | collective-permute-start | bytes 1179656 | tf_op jit(solution)/shard_map/ppermute | solution.py:500
  149.4 17.4 %copy-start.3 = (bf16[2,384,1536]{2,1,0:T(8,128)(2,1)S(1)}, bf16[2,384,1536]{2,1,0:T(8,128)(2,1)}, u32[]{:S(2)}) copy-start(bf16[2,384,1536]{2,1,0:T(8,128)(2,1)} %copy-done.2) | copy-start | bytes 7077892
  156.7 0.7 copy-start.21
  157.3 11.1 %copy-start = (f32[2,512,768]{2,1,0:T(8,128)}, f32[2,512,768]{2,1,0:T(8,128)S(1)}, u32[]{:S(2)}) copy-start(f32[2,512,768]{2,1,0:T(8,128)S(1)} %get-tuple-element.105.refs_2_) | copy-start | bytes 9437188
  166.1 2.4 copy-start.17
  166.1 0.8 copy-start.19
  168.4 12.5 %collective-permute-start.9 = (bf16[192,1536]{1,0:T(8,128)(2,1)S(1)}, bf16[192,1536]{1,0:T(8,128)(2,1)S(1)}, u32[]{:S(2)}, u32[]{:S(2)}) collective-permute-start(bf16[192,1536]{1,0:T(8,128)(2,1)S(1)} %get-tuple-element.141), channel_id=1, source_target_pairs={{0,96},{96,0},{32,64},{64,32},{1,97},{97,1},{33,65},{65,33},{2,98}... | collective-permute-start | bytes 1769480 | tf_op jit(solution)/shard_map/ppermute | solution.py:484
  169.5 11.4 %collective-permute-start.10 = (bf16[192,1536]{1,0:T(8,128)(2,1)S(1)}, bf16[192,1536]{1,0:T(8,128)(2,1)S(1)}, u32[]{:S(2)}, u32[]{:S(2)}) collective-permute-start(bf16[192,1536]{1,0:T(8,128)(2,1)S(1)} %get-tuple-element.142), channel_id=1, source_target_pairs={{0,32},{32,0},{64,96},{96,64},{1,33},{33,1},{65,97},{97,65},{2,34}... | collective-permute-start | bytes 1769480 | tf_op jit(solution)/shard_map/ppermute | solution.py:484
  184.7 17.0 %copy-start.22 = (f32[2,32,768]{2,1,0:T(8,128)S(1)}, f32[2,32,768]{2,1,0:T(8,128)}, u32[]{:S(2)}) copy-start(f32[2,32,768]{2,1,0:T(8,128)} %copy-done.21) | copy-start | bytes 589828
  184.7 14.0 %collective-permute-start.11 = (bf16[192,1536]{1,0:T(8,128)(2,1)}, bf16[192,1536]{1,0:T(8,128)(2,1)S(1)}, u32[]{:S(2)}, u32[]{:S(2)}) collective-permute-start(bf16[192,1536]{1,0:T(8,128)(2,1)} %get-tuple-element.94), channel_id=1, source_target_pairs={{0,64},{32,96},{64,0},{96,32},{1,65},{33,97},{65,1},{97,33},{2,66}... | collective-permute-start | bytes 1769480 | tf_op jit(solution)/shard_map/ppermute | solution.py:521
  186.7 15.0 %copy-start.1 = (f32[2,512,768]{2,1,0:T(8,128)S(1)}, f32[2,512,768]{2,1,0:T(8,128)}, u32[]{:S(2)}) copy-start(f32[2,512,768]{2,1,0:T(8,128)} %copy-done) | copy-start | bytes 9437188
  198.7 41.2 %collective-permute-start.12 = (bf16[384,1536]{1,0:T(8,128)(2,1)}, bf16[384,1536]{1,0:T(8,128)(2,1)}, u32[]{:S(2)}, u32[]{:S(2)}) collective-permute-start(bf16[384,1536]{1,0:T(8,128)(2,1)} %get-tuple-element.95), channel_id=1, source_target_pairs={{0,32},{32,0},{64,96},{96,64},{1,33},{33,1},{65,97},{97,65},{2,34}... | collective-permute-start | bytes 3538952 | tf_op jit(solution)/shard_map/ppermute | solution.py:478
  200.5 39.3 %collective-permute-start.13 = (bf16[384,1536]{1,0:T(8,128)(2,1)}, bf16[384,1536]{1,0:T(8,128)(2,1)}, u32[]{:S(2)}, u32[]{:S(2)}) collective-permute-start(bf16[384,1536]{1,0:T(8,128)(2,1)} %get-tuple-element.96), channel_id=1, source_target_pairs={{0,96},{96,0},{32,64},{64,32},{1,97},{97,1},{33,65},{65,33},{2,98}... | collective-permute-start | bytes 3538952 | tf_op jit(solution)/shard_map/ppermute | solution.py:478
  211.3 34.6 %all-to-all-start.3 = ((bf16[32,104,256]{2,1,0:T(8,128)(2,1)}), bf16[32,104,256]{2,1,0:T(8,128)(2,1)}, u32[]{:S(2)}, u32[]{:S(2)}) async-start(bf16[32,104,256]{2,1,0:T(8,128)(2,1)} %project.5), calls=%async_computation.3 | async-start | bytes 3407872 | tf_op jit(solution)/shard_map/all_to_all | solution.py:465
  217.5 20.6 %collective-permute-start.14 = (bf16[192,1536]{1,0:T(8,128)(2,1)}, bf16[192,1536]{1,0:T(8,128)(2,1)S(1)}, u32[]{:S(2)}, u32[]{:S(2)}) collective-permute-start(bf16[192,1536]{1,0:T(8,128)(2,1)} %get-tuple-element.98), channel_id=1, source_target_pairs={{0,32},{32,64},{64,96},{96,0},{1,33},{33,65},{65,97},{97,1},{2,34}... | collective-permute-start | bytes 1769480 | tf_op jit(solution)/shard_map/ppermute | solution.py:500
  218.9 20.1 %collective-permute-start.15 = (bf16[192,1536]{1,0:T(8,128)(2,1)}, bf16[192,1536]{1,0:T(8,128)(2,1)S(1)}, u32[]{:S(2)}, u32[]{:S(2)}) collective-permute-start(bf16[192,1536]{1,0:T(8,128)(2,1)} %get-tuple-element.100), channel_id=1, source_target_pairs={{0,96},{32,0},{64,32},{96,64},{1,97},{33,1},{65,33},{97,65},{2,98}... | collective-permute-start | bytes 1769480 | tf_op jit(solution)/shard_map/ppermute | solution.py:500
  238.2 0.8 copy-start.7
  239.0 0.8 copy-start.9
  242.4 12.4 %collective-permute-start.17 = (bf16[192,1536]{1,0:T(8,128)(2,1)}, bf16[192,1536]{1,0:T(8,128)(2,1)}, u32[]{:S(2)}, u32[]{:S(2)}) collective-permute-start(bf16[192,1536]{1,0:T(8,128)(2,1)} %get-tuple-element.139), channel_id=1, source_target_pairs={{0,32},{32,0},{64,96},{96,64},{1,33},{33,1},{65,97},{97,65},{2,34}... | collective-permute-start | bytes 1769480 | tf_op jit(solution)/shard_map/ppermute | solution.py:484
  242.4 13.3 %collective-permute-start.16 = (bf16[192,1536]{1,0:T(8,128)(2,1)}, bf16[192,1536]{1,0:T(8,128)(2,1)}, u32[]{:S(2)}, u32[]{:S(2)}) collective-permute-start(bf16[192,1536]{1,0:T(8,128)(2,1)} %get-tuple-element.140), channel_id=1, source_target_pairs={{0,96},{96,0},{32,64},{64,32},{1,97},{97,1},{33,65},{65,33},{2,98}... | collective-permute-start | bytes 1769480 | tf_op jit(solution)/shard_map/ppermute | solution.py:484
  245.9 1.4 copy-start.5
  247.3 1.0 copy-start.13
  248.4 1.0 copy-start.14
  254.8 3.9 %copy-start.11 = (f32[1024,1]{1,0:T(8,128)}, f32[1024,1]{1,0:T(8,128)S(1)}, u32[]{:S(2)}) copy-start(f32[1024,1]{1,0:T(8,128)S(1)} %get-tuple-element.110) | copy-start | bytes 12292
  258.7 24.3 %collective-permute-start.20 = (bf16[192,1536]{1,0:T(8,128)(2,1)}, bf16[192,1536]{1,0:T(8,128)(2,1)}, u32[]{:S(2)}, u32[]{:S(2)}) collective-permute-start(bf16[192,1536]{1,0:T(8,128)(2,1)} %get-tuple-element.130), channel_id=1, source_target_pairs={{0,96},{32,0},{64,32},{96,64},{1,97},{33,1},{65,33},{97,65},{2,98}... | collective-permute-start | bytes 1769480 | tf_op jit(solution)/shard_map/ppermute | solution.py:500
  260.8 2.7 copy-start.4
  260.9 2.7 copy-start.16
  260.9 2.7 copy-start.18
  260.9 2.7 copy-start.20
  262.0 21.0 %collective-permute-start.19 = (bf16[192,1536]{1,0:T(8,128)(2,1)}, bf16[192,1536]{1,0:T(8,128)(2,1)}, u32[]{:S(2)}, u32[]{:S(2)}) collective-permute-start(bf16[192,1536]{1,0:T(8,128)(2,1)} %get-tuple-element.145), channel_id=1, source_target_pairs={{0,64},{32,96},{64,0},{96,32},{1,65},{33,97},{65,1},{97,33},{2,66}... | collective-permute-start | bytes 1769480 | tf_op jit(solution)/shard_map/ppermute | solution.py:500
  262.5 25.4 %collective-permute-start.18 = (bf16[192,1536]{1,0:T(8,128)(2,1)}, bf16[192,1536]{1,0:T(8,128)(2,1)}, u32[]{:S(2)}, u32[]{:S(2)}) collective-permute-start(bf16[192,1536]{1,0:T(8,128)(2,1)} %get-tuple-element.147), channel_id=1, source_target_pairs={{0,32},{32,64},{64,96},{96,0},{1,33},{33,65},{65,97},{97,1},{2,34}... | collective-permute-start | bytes 1769480 | tf_op jit(solution)/shard_map/ppermute | solution.py:500
  263.6 1.7 copy-start.8
  263.6 1.7 copy-start.10
  265.4 2.0 copy-start.12
